TPU v7x, 128 devices: a whole 4x4x4 slice. The times are simulated.
128 devices in a mesh: gx: 8 (over x, core), gy: 16 (over z, y).
Axes of the slice: x: 4, y: 4, z: 4, core: 2. Of those that a mesh axis runs over, the one named last changes fastest.
Arguments:
- hidden_in: bfloat16 [1024, 16384], P('gx', 'gy'), may hold values from -6 to 6
- w_query: bfloat16 [16384, 16384], P('gy', 'gx'), may hold values from -0.046875 to 0.046875
- w_key: bfloat16 [16384, 1024], P('gy', 'gx'), may hold values from -0.046875 to 0.046875
- w_value: bfloat16 [16384, 1024], P('gy', 'gx'), may hold values from -0.046875 to 0.046875
- w_output: bfloat16 [16384, 16384], P('gx', 'gy'), may hold values from -0.046875 to 0.046875
- cache_keys: bfloat16 [1024, 448, 1024], P(('gx', 'gy')), may hold values from -210 to 210, as said below
- cache_values: bfloat16 [1024, 448, 1024], P(('gx', 'gy')), may hold values from -6 to 6
- cache_lengths: int32 [1024], P(('gx', 'gy')), may hold values from 2 to 448, as said below
- positions: int32 [1024], P(('gx', 'gy')), may hold values from 448 to 8191
Outputs:
- attended: bfloat16 [1024, 16384], P('gx', 'gy')
- new_keys: bfloat16 [1024, 1024], P(('gx', 'gy'))
- new_values: bfloat16 [1024, 1024], P(('gx', 'gy'))
Inputs may be any that keep to these rules, and one draw needn't show every extreme that they name: `cache_lengths`: each sequence has at least two filled slots; some sequence has all 448 slots filled. `cache_keys`: A few slots of a sequence may hold keys of magnitude up to about 205.
All inputs are finite; a program needn't handle non-finite values.
Results may differ from a plain program's by a relative error of at most 0.012.
The roundings to bfloat16 on the way count: a program that leaves them out, or rounds other values in their place, can miss the bound.
Values may be sent and summed in bfloat16 or wider, within the bound.
No kernel may reach another device: no remote copies, remote signals or barrier semaphores. Data moves between devices by JAX's collectives and lax.ppermute only.
A program may use at most 128 MiB of HBM per device.

v0:
```python
import functools
import math

import jax
import jax.numpy as jnp
from jax import lax
from jax.experimental import pallas as pl
from jax.experimental.pallas import tpu as pltpu
from jax.sharding import PartitionSpec as P

HQ = 128
KVH = 8
DH = 128
CACHE = 448
GROUP = HQ // KVH
AXES = ("gx", "gy")
SIDE = 4
ROWS = 8
LIFT = 32.0
PIECES = ((0,), (1, 3), (2,))
FOUND = {step: (p, i) for p, piece in enumerate(PIECES) for i, step in enumerate(piece)}


def rope_frequencies():
    index = jnp.arange(DH // 2, dtype=jnp.float32)
    base = jnp.power(jnp.float32(500000.0), -2.0 * index / DH)
    wavelength = 2.0 * math.pi / base
    smooth = (8192.0 / wavelength - 1.0) / 3.0
    middle = (1.0 - smooth) * base / 8.0 + smooth * base
    return jnp.where(wavelength > 8192.0, base / 8.0, jnp.where(wavelength < 2048.0, base, middle))


def permute(value, move):
    pairs = []
    for x in range(SIDE):
        for c in range(2):
            for z in range(SIDE):
                for y in range(SIDE):
                    tx, tc, tz, ty = move(x, c, z, y)
                    target = ((tx % SIDE) * 2 + tc) * SIDE + tz % SIDE
                    source = (x * 2 + c) * SIDE + z
                    pairs.append((source * SIDE + y, target * SIDE + ty % SIDE))
    return lax.ppermute(value, AXES, pairs)


def to_pair(value):
    return permute(value, lambda x, c, z, y: (x, 1 - c, z, y))


def along_x(value, step):
    return permute(value, lambda x, c, z, y: (x + step, c, z, y))


def along_first(value, step):
    return permute(value, lambda x, c, z, y: (x, c, z + step * c, y + step * (1 - c)))


def along_second(value, step):
    return permute(value, lambda x, c, z, y: (x, c, z + step * (1 - c), y + step * c))


def group_at(place, first, second, sign):
    z, y, core = place[0], place[1], place[2]
    dz = jnp.where(core == 0, second, first)
    dy = jnp.where(core == 0, first, second)
    return lax.rem(z + sign * dz + SIDE, SIDE) * SIDE + lax.rem(y + sign * dy + SIDE, SIDE)


def order_kernel(place, h_ref, out_ref):
    for first in range(SIDE):
        for second in range(SIDE):
            out_ref[first, second] = h_ref[group_at(place, first, second, 1)]


def order_rows(place, hidden):
    width = hidden.shape[1]
    return pl.pallas_call(
        order_kernel,
        out_shape=jax.ShapeDtypeStruct((SIDE, SIDE, ROWS, width), hidden.dtype),
        in_specs=[pl.BlockSpec(memory_space=pltpu.SMEM), pl.BlockSpec(memory_space=pltpu.VMEM)],
        out_specs=pl.BlockSpec(memory_space=pltpu.VMEM),
        cost_estimate=pl.CostEstimate(flops=0, bytes_accessed=2**19, transcendentals=0),
        name="order_rows",
    )(place, hidden.reshape(SIDE * SIDE, ROWS, width))


def total_of(first, others):
    return functools.reduce(
        jnp.add, [first.astype(jnp.float32)] + [item.astype(jnp.float32) for item in others]
    )


def sum_over_plane(groups, weights):
    width = weights.shape[1]
    rows = jnp.stack(groups, axis=2)
    rows = rows.reshape(SIDE, SIDE * len(groups) * ROWS, rows.shape[-1])

    def term(step):
        return jnp.dot(rows[step], weights, preferred_element_type=jnp.float32) * LIFT

    came = [along_first(term(step).astype(jnp.float16), step) for step in (1, 3, 2)]
    kept = total_of(term(0), came).reshape(SIDE, len(groups) * ROWS, width)
    came = [along_second(kept[step].astype(jnp.float16), step) for step in (2, 1, 3)]
    kept = total_of(kept[0], came) * (1.0 / LIFT)
    return kept.astype(jnp.bfloat16).reshape(len(groups), ROWS, width)


def attention_kernel(
    head, length, q_ref, cos_ref, sin_ref, k_ref, v_ref, o_ref, nk_ref, nv_ref, queries, results
):
    cosine = cos_ref[...]
    sine = sin_ref[...]

    def rotated(columns):
        u = q_ref[0, :, columns].astype(jnp.float32)
        return (u * cosine + pltpu.roll(u, DH // 2, 1) * sine).astype(jnp.bfloat16)

    for h in range(GROUP):
        queries[pl.ds(h, ROWS, stride=GROUP), :] = rotated(
            slice(h * DH, (h + 1) * DH)
        ).astype(jnp.float32)
    key_new = rotated(slice(GROUP * DH, (GROUP + 1) * DH))
    nk_ref[...] = key_new
    value_new = q_ref[0, :, (GROUP + 1) * DH :]
    nv_ref[...] = value_new
    key_new = key_new.astype(jnp.float32)
    value_new = value_new.astype(jnp.float32)
    scale = DH ** (-0.5)
    slot = lax.broadcasted_iota(jnp.int32, (GROUP, CACHE), 1)
    for s in range(ROWS):
        q = queries[s * GROUP : (s + 1) * GROUP, :]
        scores = lax.dot_general(
            q.astype(jnp.bfloat16),
            k_ref[s],
            (((1,), (1,)), ((), ())),
            preferred_element_type=jnp.float32,
        )
        scores = jnp.where(slot < length[s], scores * scale, -jnp.inf)
        score_new = jnp.sum(q * key_new[s : s + 1], axis=1, keepdims=True) * scale
        top = jnp.maximum(jnp.max(scores, axis=1, keepdims=True), score_new)
        expo = jnp.exp(scores - top)
        expo_new = jnp.exp(score_new - top)
        total = jnp.sum(expo, axis=1, keepdims=True) + expo_new
        weights = (expo / total).astype(jnp.bfloat16)
        weight_new = (expo_new / total).astype(jnp.bfloat16).astype(jnp.float32)
        mixed = jnp.dot(weights, v_ref[s], preferred_element_type=jnp.float32)
        results[s * GROUP : (s + 1) * GROUP, :] = mixed + weight_new * value_new[s : s + 1]
    for h in range(GROUP):
        o_ref[0, :, h * DH : (h + 1) * DH] = results[pl.ds(h, ROWS, stride=GROUP), :].astype(
            jnp.bfloat16
        )


def attention(heads, lengths, packed, cosine, sine, cache_keys, cache_values):
    width = packed.shape[2] // 2
    cache = pl.BlockSpec((ROWS, CACHE, DH), lambda r, head, length: (0, 0, head[r]))
    whole = pl.BlockSpec((ROWS, DH), lambda r, head, length: (0, 0))
    column = pl.BlockSpec((ROWS, DH), lambda r, head, length: (0, head[r]))
    new = jax.ShapeDtypeStruct((ROWS, KVH * DH), jnp.bfloat16)
    half = (KVH // 2, ROWS, 2 * GROUP * DH)
    return pl.pallas_call(
        attention_kernel,
        out_shape=(jax.ShapeDtypeStruct(half, jnp.bfloat16), new, new),
        grid_spec=pltpu.PrefetchScalarGridSpec(
            num_scalar_prefetch=2,
            grid=(KVH,),
            in_specs=[
                pl.BlockSpec((1, ROWS, width), lambda r, head, length: (r // 2, 0, r % 2)),
                whole,
                whole,
                cache,
                cache,
            ],
            out_specs=(
                pl.BlockSpec((1, ROWS, GROUP * DH), lambda r, head, length: (r // 2, 0, r % 2)),
                column,
                column,
            ),
            scratch_shapes=[
                pltpu.VMEM((ROWS * GROUP, DH), jnp.float32),
                pltpu.VMEM((ROWS * GROUP, DH), jnp.float32),
            ],
        ),
        compiler_params=pltpu.CompilerParams(vmem_limit_bytes=24 * 2**20),
        cost_estimate=pl.CostEstimate(
            flops=4 * ROWS * HQ * CACHE * DH,
            bytes_accessed=4 * ROWS * CACHE * KVH * DH,
            transcendentals=ROWS * HQ * CACHE,
        ),
        name="attention",
    )(heads, lengths, packed, cosine, sine, cache_keys, cache_values)


def final_kernel(place, *refs):
    terms, out_ref = refs[:-1], refs[-1]
    for second in range(SIDE):
        piece, inside = FOUND[second]
        for first in range(SIDE):
            total = terms[4 * piece][inside, first]
            for term in terms[4 * piece + 1 : 4 * piece + 4]:
                total = total + term[inside, first]
            out_ref[group_at(place, first, second, -1)] = total.astype(jnp.bfloat16)


def add_up(place, terms):
    width = terms[0].shape[-1]
    return pl.pallas_call(
        final_kernel,
        out_shape=jax.ShapeDtypeStruct((SIDE * SIDE, ROWS, width), jnp.bfloat16),
        in_specs=[pl.BlockSpec(memory_space=pltpu.SMEM)]
        + [pl.BlockSpec(memory_space=pltpu.VMEM)] * len(terms),
        out_specs=pl.BlockSpec(memory_space=pltpu.VMEM),
        cost_estimate=pl.CostEstimate(flops=2**19, bytes_accessed=2**21, transcendentals=0),
        name="add_up",
    )(place, *terms)


def project(parts, w_output):
    terms = []
    for part in parts:
        term = jnp.dot(part.reshape(-1, part.shape[-1]), w_output, preferred_element_type=jnp.float32)
        terms.append(term.reshape(SIDE, SIDE, ROWS, -1))
    sent = [jnp.stack([term[:, dx] for term in terms]) for dx in range(SIDE)]
    return [sent[0]] + [along_x(sent[dx], -dx) for dx in (2, 1, 3)]


def on_device(
    hidden_in, w_query, w_key, w_value, w_output, cache_keys, cache_values, cache_lengths, positions
):
    gx = lax.axis_index("gx")
    gy = lax.axis_index("gy")
    x, core = gx // 2, gx % 2
    place = jnp.stack([gy // SIDE, gy % SIDE, core]).astype(jnp.int32)

    own = order_rows(place, hidden_in)
    groups = {0: own}
    for step in (2, 1, 3):
        groups[step] = along_x(own, step)
    w_both = jnp.concatenate([w_key, w_value], axis=1)
    w_both = jnp.concatenate([w_query, w_both, to_pair(w_query), to_pair(w_both)], axis=1)
    w_back = jnp.concatenate([w_output, to_pair(w_output)], axis=0)
    summed = sum_over_plane([groups[dx] for dx in range(SIDE)], w_both)

    packed = [along_x(summed[dx], -dx) if dx else summed[dx] for dx in range(SIDE)]
    heads = [((x + dx) % SIDE) * 2 + (core + dc) % 2 for dx in range(SIDE) for dc in range(2)]
    angle = positions.astype(jnp.float32)[:, None] * rope_frequencies()[None, :]
    cosine, sine = jnp.cos(angle), jnp.sin(angle)
    mixed, new_keys, new_values = attention(
        jnp.stack(heads).astype(jnp.int32),
        cache_lengths,
        jnp.stack(packed),
        jnp.concatenate([cosine, cosine], axis=1),
        jnp.concatenate([-sine, sine], axis=1),
        cache_keys,
        cache_values,
    )

    rows = jnp.stack([along_x(mixed[dx], dx) if dx else mixed[dx] for dx in range(SIDE)])
    near = {0: rows}
    for step in (2, 1, 3):
        near[step] = along_first(rows, step)
    rows = jnp.stack([near[step] for step in range(SIDE)])
    far = {0: rows}
    for step in (1, 3, 2):
        far[step] = along_second(rows, step)
    terms = []
    for piece in PIECES:
        terms += project([far[step] for step in piece], w_back)
    attended = add_up(place, terms)
    return (attended.reshape(hidden_in.shape), new_keys, new_values)


def solution(mesh):
    placed = (
        P("gx", "gy"),
        P("gy", "gx"),
        P("gy", "gx"),
        P("gy", "gx"),
        P("gx", "gy"),
        P(("gx", "gy"), None, None),
        P(("gx", "gy"), None, None),
        P(("gx", "gy")),
        P(("gx", "gy")),
    )
    return jax.shard_map(
        on_device,
        mesh=mesh,
        in_specs=placed,
        out_specs=(P("gx", "gy"), P(("gx", "gy"), None), P(("gx", "gy"), None)),
        check_vma=False,
    )
```

profile of v0, /device:TPU:6, one launch (start us, length us, event | category | flops | bytes accessed | tf_op | source)
XLA Modules:
  0.0 204.1 jit_solution(3812549047320496742)
XLA Ops:
  1.4 1.8 order_rows.1
  3.6 2.5 %collective-permute-start.1 = (bf16[4,4,8,1024]{3,2,1,0:T(8,128)(2,1)}, bf16[4,4,8,1024]{3,2,1,0:T(8,128)(2,1)S(1)}, u32[]{:S(2)}, u32[]{:S(2)}) collective-permute-start(bf16[4,4,8,1024]{3,2,1,0:T(8,128)(2,1)} %order_rows.1), channel_id=1, source_target_pairs={{0,64},{1,65},{2,66},{3,67},{4,68},{5,69},{6,70},{7,71},{8,72},{9,... | collective-permute-start | bytes 786440 | tf_op jit(solution)/shard_map/ppermute | solution.py:43
  6.1 1.1 pad_maximum_fusion.2
  7.3 2.6 %constant_dynamic-update-slice_fusion.4 = bf16[1024,4608]{1,0:T(8,128)(2,1)S(1)} fusion(bf16[1024,2048]{1,0:T(8,128)(2,1)} %param.10), kind=kLoop, calls=%fused_computation.57 | loop fusion | bytes 8388608
  10.0 2.5 %collective-permute-done = bf16[4,4,8,1024]{3,2,1,0:T(8,128)(2,1)S(1)} collective-permute-done((bf16[4,4,8,1024]{3,2,1,0:T(8,128)(2,1)}, bf16[4,4,8,1024]{3,2,1,0:T(8,128)(2,1)S(1)}, u32[]{:S(2)}, u32[]{:S(2)}) %collective-permute-start) | collective-permute-done | bytes 262176 | tf_op jit(solution)/shard_map/ppermute | solution.py:43
  12.5 2.0 collective-permute-done.1
  14.5 4.8 %collective-permute-done.2 = bf16[4,4,8,1024]{3,2,1,0:T(8,128)(2,1)S(1)} collective-permute-done((bf16[4,4,8,1024]{3,2,1,0:T(8,128)(2,1)}, bf16[4,4,8,1024]{3,2,1,0:T(8,128)(2,1)S(1)}, u32[]{:S(2)}, u32[]{:S(2)}) %collective-permute-start.2) | collective-permute-done | bytes 262176 | tf_op jit(solution)/shard_map/ppermute | solution.py:43
  20.3 2.5 %constant_dynamic-update-slice_fusion.1 = bf16[1024,4608]{1,0:T(8,128)(2,1)S(1)} fusion(bf16[1024,4608]{1,0:T(8,128)(2,1)S(1)} %constant_dynamic-update-slice_fusion.2, bf16[1024,2048]{1,0:T(8,128)(2,1)} %collective-permute-done.3), kind=kLoop, calls=%fused_computation.54 | loop fusion | bytes 8388608
  22.9 3.0 %fusion.3 = f16[128,4608]{1,0:T(8,128)(2,1)} fusion(bf16[128,1024]{1,0:T(8,128)(2,1)S(1)} %bitcast.92, bf16[1024,4608]{1,0:T(8,128)(2,1)S(1)} %constant_dynamic-update-slice_fusion), kind=kOutput, calls=%fused_computation.8 | convolution fusion | flops 1209139200 | bytes 10878976 | tf_op jit(solution)/shard_map/dot_general | solution.py:99
  26.0 1.7 collective-permute-start.5
  27.6 2.4 %fusion.4 = f16[128,4608]{1,0:T(8,128)(2,1)} fusion(bf16[128,1024]{1,0:T(8,128)(2,1)S(1)} %bitcast.91, bf16[1024,4608]{1,0:T(8,128)(2,1)S(1)} %constant_dynamic-update-slice_fusion), kind=kOutput, calls=%fused_computation.9 | convolution fusion | flops 1209139200 | bytes 10878976 | tf_op jit(solution)/shard_map/dot_general | solution.py:99
  30.1 1.6 collective-permute-start.6
  31.6 2.5 %fusion.5 = f16[128,4608]{1,0:T(8,128)(2,1)} fusion(bf16[128,1024]{1,0:T(8,128)(2,1)S(1)} %bitcast.90, bf16[1024,4608]{1,0:T(8,128)(2,1)S(1)} %constant_dynamic-update-slice_fusion), kind=kOutput, calls=%fused_computation.10 | convolution fusion | flops 1209139200 | bytes 10878976 | tf_op jit(solution)/shard_map/dot_general | solution.py:99
  34.1 2.1 %collective-permute-start.7 = (f16[128,4608]{1,0:T(8,128)(2,1)}, f16[128,4608]{1,0:T(8,128)(2,1)S(1)}, u32[]{:S(2)}, u32[]{:S(2)}) collective-permute-start(f16[128,4608]{1,0:T(8,128)(2,1)} %fusion.5), channel_id=1, source_target_pairs={{0,2},{1,3},{2,0},{3,1},{4,6},{5,7},{6,4},{7,5},{8,10},{9,11},{10,... | collective-permute-start | bytes 3538952 | tf_op jit(solution)/shard_map/ppermute | solution.py:43
  37.2 6.3 %collective-permute-done.5 = f16[128,4608]{1,0:T(8,128)(2,1)S(1)} collective-permute-done((f16[128,4608]{1,0:T(8,128)(2,1)}, f16[128,4608]{1,0:T(8,128)(2,1)S(1)}, u32[]{:S(2)}, u32[]{:S(2)}) %collective-permute-start.5) | collective-permute-done | bytes 1179680 | tf_op jit(solution)/shard_map/ppermute | solution.py:43
  43.6 2.9 %collective-permute-done.6 = f16[128,4608]{1,0:T(8,128)(2,1)S(1)} collective-permute-done((f16[128,4608]{1,0:T(8,128)(2,1)}, f16[128,4608]{1,0:T(8,128)(2,1)S(1)}, u32[]{:S(2)}, u32[]{:S(2)}) %collective-permute-start.6) | collective-permute-done | bytes 1179680 | tf_op jit(solution)/shard_map/ppermute | solution.py:43
  46.5 11.1 %collective-permute-done.7 = f16[128,4608]{1,0:T(8,128)(2,1)S(1)} collective-permute-done((f16[128,4608]{1,0:T(8,128)(2,1)}, f16[128,4608]{1,0:T(8,128)(2,1)S(1)}, u32[]{:S(2)}, u32[]{:S(2)}) %collective-permute-start.7) | collective-permute-done | bytes 1179680 | tf_op jit(solution)/shard_map/ppermute | solution.py:43
  57.6 5.9 %fusion.23 = (f16[128,4608]{1,0:T(8,128)(2,1)S(1)}, f32[128,4608]{1,0:T(8,128)S(1)}) fusion(f16[128,4608]{1,0:T(8,128)(2,1)S(1)} %collective-permute-done.7, f16[128,4608]{1,0:T(8,128)(2,1)S(1)} %collective-permute-done.6, f16[128,4608]{1,0:T(8,128)(2,1)S(1)} %collective-permute-done.5, bf16[128,1024]{1,0:T(8,128)(2,1)S(1)} %bitcast.93, ...), kind=kOutput, calls=%fused_computation.70 | convolution fusion | flops 1212678144 | bytes 16777216 | tf_op jit(solution)/shard_map/dot_general | solution.py:99
  63.6 4.1 %collective-permute-start.10 = (f16[32,4608]{1,0:T(8,128)(2,1)S(1)}, f16[32,4608]{1,0:T(8,128)(2,1)S(1)}, u32[]{:S(2)}, u32[]{:S(2)}) collective-permute-start(f16[32,4608]{1,0:T(8,128)(2,1)S(1)} %get-tuple-element.10), channel_id=1, source_target_pairs={{0,12},{1,13},{2,14},{3,15},{4,0},{5,1},{6,2},{7,3},{8,4},{9,5},{1... | collective-permute-start | bytes 884744 | tf_op jit(solution)/shard_map/ppermute | solution.py:43
  67.7 1.3 collective-permute-start.9
  69.1 6.0 %collective-permute-done.10 = f16[32,4608]{1,0:T(8,128)(2,1)S(1)} collective-permute-done((f16[32,4608]{1,0:T(8,128)(2,1)S(1)}, f16[32,4608]{1,0:T(8,128)(2,1)S(1)}, u32[]{:S(2)}, u32[]{:S(2)}) %collective-permute-start.10) | collective-permute-done | bytes 294944 | tf_op jit(solution)/shard_map/ppermute | solution.py:43
  76.0 2.8 %collective-permute-done.9 = f16[32,4608]{1,0:T(8,128)(2,1)S(1)} collective-permute-done((f16[32,4608]{1,0:T(8,128)(2,1)S(1)}, f16[32,4608]{1,0:T(8,128)(2,1)S(1)}, u32[]{:S(2)}, u32[]{:S(2)}) %collective-permute-start.9) | collective-permute-done | bytes 294944 | tf_op jit(solution)/shard_map/ppermute | solution.py:43
  79.0 1.0 collective-permute-start.11
  80.0 1.5 collective-permute-start.12
  81.5 1.9 collective-permute-start.13
  83.5 1.1 collective-permute-done.11
  84.6 1.3 collective-permute-done.12
  86.4 30.2 %attention.1 = (bf16[4,8,4096]{2,1,0:T(8,128)(2,1)S(1)}, bf16[8,1024]{1,0:T(8,128)(2,1)}, bf16[8,1024]{1,0:T(8,128)(2,1)}) custom-call(s32[8]{0:T(128)S(1)} %stack.117.head, s32[8]{0:T(128)S(1)} %copy-done, bf16[4,8,4608]{2,1,0:T(8,128)(2,1)S(1)} %pad_maximum_fusion.3.q_ref, f32[8,128]{1,0:T(8,128)S(1)} %get-tuple-element.47.cos_ref, ...), custom_call_target="tpu_custom_call" | custom-call | flops 234881024 | bytes 14680064 | tf_op jit(solution)/shard_map/attention/pallas_call | solution.py:161
  116.6 2.8 %collective-permute-start.14 = (bf16[8,4096]{1,0:T(8,128)(2,1)S(1)}, bf16[8,4096]{1,0:T(8,128)(2,1)S(1)}, u32[]{:S(2)}, u32[]{:S(2)}) collective-permute-start(bf16[8,4096]{1,0:T(8,128)(2,1)S(1)} %get-tuple-element.41), channel_id=1, source_target_pairs={{0,32},{1,33},{2,34},{3,35},{4,36},{5,37},{6,38},{7,39},{8,40},{9,... | collective-permute-start | bytes 196616 | tf_op jit(solution)/shard_map/ppermute | solution.py:43
  120.3 1.6 collective-permute-done.14
  121.9 3.3 %collective-permute-done.15 = bf16[8,4096]{1,0:T(8,128)(2,1)S(1)} collective-permute-done((bf16[8,4096]{1,0:T(8,128)(2,1)S(1)}, bf16[8,4096]{1,0:T(8,128)(2,1)S(1)}, u32[]{:S(2)}, u32[]{:S(2)}) %collective-permute-start.15) | collective-permute-done | bytes 65568 | tf_op jit(solution)/shard_map/ppermute | solution.py:43
  125.9 3.9 %collective-permute-start.17 = (bf16[4,8,4096]{2,1,0:T(8,128)(2,1)S(1)}, bf16[4,8,4096]{2,1,0:T(8,128)(2,1)S(1)}, u32[]{:S(2)}, u32[]{:S(2)}) collective-permute-start(bf16[4,8,4096]{2,1,0:T(8,128)(2,1)S(1)} %get-tuple-element.37), channel_id=1, source_target_pairs={{0,1},{1,2},{2,3},{3,0},{4,5},{5,6},{6,7},{7,4},{8,9},{9,10},{10,1... | collective-permute-start | bytes 786440 | tf_op jit(solution)/shard_map/ppermute | solution.py:43
  129.8 2.1 %collective-permute-start.18 = (bf16[4,8,4096]{2,1,0:T(8,128)(2,1)S(1)}, bf16[4,8,4096]{2,1,0:T(8,128)(2,1)S(1)}, u32[]{:S(2)}, u32[]{:S(2)}) collective-permute-start(bf16[4,8,4096]{2,1,0:T(8,128)(2,1)S(1)} %get-tuple-element.37), channel_id=1, source_target_pairs={{0,2},{1,3},{2,0},{3,1},{4,6},{5,7},{6,4},{7,5},{8,10},{9,11},{10,... | collective-permute-start | bytes 786440 | tf_op jit(solution)/shard_map/ppermute | solution.py:43
  132.6 2.2 %collective-permute-done.17 = bf16[4,8,4096]{2,1,0:T(8,128)(2,1)S(1)} collective-permute-done((bf16[4,8,4096]{2,1,0:T(8,128)(2,1)S(1)}, bf16[4,8,4096]{2,1,0:T(8,128)(2,1)S(1)}, u32[]{:S(2)}, u32[]{:S(2)}) %collective-permute-start.17) | collective-permute-done | bytes 262176 | tf_op jit(solution)/shard_map/ppermute | solution.py:43
  134.8 5.1 %collective-permute-done.18 = bf16[4,8,4096]{2,1,0:T(8,128)(2,1)S(1)} collective-permute-done((bf16[4,8,4096]{2,1,0:T(8,128)(2,1)S(1)}, bf16[4,8,4096]{2,1,0:T(8,128)(2,1)S(1)}, u32[]{:S(2)}, u32[]{:S(2)}) %collective-permute-start.18) | collective-permute-done | bytes 262176 | tf_op jit(solution)/shard_map/ppermute | solution.py:43
  139.8 10.4 %collective-permute-done.19 = bf16[4,8,4096]{2,1,0:T(8,128)(2,1)S(1)} collective-permute-done((bf16[4,8,4096]{2,1,0:T(8,128)(2,1)S(1)}, bf16[4,8,4096]{2,1,0:T(8,128)(2,1)S(1)}, u32[]{:S(2)}, u32[]{:S(2)}) %collective-permute-start.19) | collective-permute-done | bytes 262176 | tf_op jit(solution)/shard_map/ppermute | solution.py:43
  150.6 3.2 %collective-permute-start.25 = (bf16[4,4,8,4096]{3,2,1,0:T(8,128)(2,1)S(1)}, bf16[4,4,8,4096]{3,2,1,0:T(8,128)(2,1)S(1)}, u32[]{:S(2)}, u32[]{:S(2)}) collective-permute-start(bf16[4,4,8,4096]{3,2,1,0:T(8,128)(2,1)S(1)} %pad_maximum_fusion.1), channel_id=1, source_target_pairs={{0,12},{1,13},{2,14},{3,15},{4,0},{5,1},{6,2},{7,3},{8,4},{9,5},{1... | collective-permute-start | bytes 3145736 | tf_op jit(solution)/shard_map/ppermute | solution.py:43
  153.8 4.2 %fusion.12 = f32[4,4,8,1024]{3,2,0,1:T(8,128)S(1)} fusion(bf16[2048,1024]{1,0:T(8,128)(2,1)} %collective-permute-done.20, bf16[2048,1024]{1,0:T(8,128)(2,1)} %param.13, bf16[1,4,8,4096]{3,2,1,0:T(8,128)(2,1)S(1)} %bitcast.102, bf16[1,4,8,4096]{3,2,1,0:T(8,128)(2,1)S(1)} %bitcast.100, bf16[1,4,8,4096]{3,2,1,0:T(8,128)(2,1)S(1)} %bitcast.98, ...), kind=kOutput, calls=%fused_computation.19 | convolution fusion | flops 1092091904 | bytes 9961472 | tf_op jit(solution)/shard_map/dot_general | solution.py:221
  159.7 7.2 %collective-permute-done.29 = bf16[4,4,8,4096]{3,2,1,0:T(8,128)(2,1)S(1)} collective-permute-done((bf16[4,4,8,4096]{3,2,1,0:T(8,128)(2,1)S(1)}, bf16[4,4,8,4096]{3,2,1,0:T(8,128)(2,1)S(1)}, u32[]{:S(2)}, u32[]{:S(2)}) %collective-permute-start.29) | collective-permute-done | bytes 1048608 | tf_op jit(solution)/shard_map/ppermute | solution.py:43
  167.0 4.2 %fusion.6 = f32[4,4,8,1024]{3,2,0,1:T(8,128)S(1)} fusion(bf16[4,4,8,4096]{3,2,1,0:T(8,128)(2,1)S(1)} %collective-permute-done.29, bf16[2048,1024]{1,0:T(8,128)(2,1)} %collective-permute-done.20, bf16[2048,1024]{1,0:T(8,128)(2,1)} %param.13), kind=kOutput, calls=%fused_computation.13 | convolution fusion | flops 1090519040 | bytes 9961472 | tf_op jit(solution)/shard_map/dot_general | solution.py:221
  171.9 5.9 %collective-permute-done.24 = bf16[4,4,8,4096]{3,2,1,0:T(8,128)(2,1)S(1)} collective-permute-done((bf16[4,4,8,4096]{3,2,1,0:T(8,128)(2,1)S(1)}, bf16[4,4,8,4096]{3,2,1,0:T(8,128)(2,1)S(1)}, u32[]{:S(2)}, u32[]{:S(2)}) %collective-permute-start.24) | collective-permute-done | bytes 1048608 | tf_op jit(solution)/shard_map/ppermute | solution.py:43
  178.8 4.2 %fusion.10 = f32[4,4,8,1024]{3,2,0,1:T(8,128)S(1)} fusion(bf16[4,4,8,4096]{3,2,1,0:T(8,128)(2,1)S(1)} %collective-permute-done.24, bf16[2048,1024]{1,0:T(8,128)(2,1)} %collective-permute-done.20, bf16[2048,1024]{1,0:T(8,128)(2,1)} %param.13), kind=kOutput, calls=%fused_computation.17 | convolution fusion | flops 1090519040 | bytes 9961472 | tf_op jit(solution)/shard_map/dot_general | solution.py:221
  183.1 4.2 %fusion.8 = f32[4,4,8,1024]{3,2,0,1:T(8,128)S(1)} fusion(bf16[4,4,8,4096]{3,2,1,0:T(8,128)(2,1)S(1)} %collective-permute-done.25, bf16[2048,1024]{1,0:T(8,128)(2,1)} %collective-permute-done.20, bf16[2048,1024]{1,0:T(8,128)(2,1)} %param.13), kind=kOutput, calls=%fused_computation.15 | convolution fusion | flops 1090519040 | bytes 9961472 | tf_op jit(solution)/shard_map/dot_general | solution.py:221
  187.7 1.9 collective-permute-start.27
  189.6 2.5 %collective-permute-start.26 = (f32[2,4,8,1024]{3,2,1,0:T(8,128)S(1)}, f32[2,4,8,1024]{3,2,1,0:T(8,128)S(1)}, u32[]{:S(2)}, u32[]{:S(2)}) collective-permute-start(f32[2,4,8,1024]{3,2,1,0:T(8,128)S(1)} %pad_maximum_fusion.6), channel_id=1, source_target_pairs={{0,64},{1,65},{2,66},{3,67},{4,68},{5,69},{6,70},{7,71},{8,72},{9,... | collective-permute-start | bytes 786440 | tf_op jit(solution)/shard_map/ppermute | solution.py:43
  192.2 3.2 %collective-permute-start.32 = (f32[1,4,8,1024]{3,2,1,0:T(8,128)S(1)}, f32[1,4,8,1024]{3,2,1,0:T(8,128)S(1)}, u32[]{:S(2)}, u32[]{:S(2)}) collective-permute-start(f32[1,4,8,1024]{3,2,1,0:T(8,128)S(1)} %get-tuple-element.16), channel_id=1, source_target_pairs={{0,32},{1,33},{2,34},{3,35},{4,36},{5,37},{6,38},{7,39},{8,40},{9,... | collective-permute-start | bytes 393224 | tf_op jit(solution)/shard_map/ppermute | solution.py:43
  196.1 4.6 %collective-permute-done.31.refs_10_ = f32[1,4,8,1024]{3,2,1,0:T(8,128)S(1)} collective-permute-done((f32[1,4,8,1024]{3,2,1,0:T(8,128)S(1)}, f32[1,4,8,1024]{3,2,1,0:T(8,128)S(1)}, u32[]{:S(2)}, u32[]{:S(2)}) %collective-permute-start.31) | collective-permute-done | bytes 131104 | tf_op jit(solution)/shard_map/ppermute | solution.py:43
  201.7 2.4 %add_up.1 = bf16[16,8,1024]{2,1,0:T(8,128)(2,1)} custom-call(s32[3]{0:T(128)} %pad_add_fusion.place, f32[1,4,8,1024]{3,2,1,0:T(8,128)} %get-tuple-element.31.refs_0_, f32[1,4,8,1024]{3,2,1,0:T(8,128)} %copy-done.8, f32[1,4,8,1024]{3,2,1,0:T(8,128)} %copy-done.9, f32[1,4,8,1024]{3,2,1,0:T(8,128)} %copy-done.10, f32[2,4,8,1024]{3,2,1,0:T(8,128)} %pad_maximum_fusion.5.refs_4_, ...), custom_call_target="tpu_custom_call" | custom-call | flops 524288 | bytes 2097152 | tf_op jit(solution)/shard_map/add_up/pallas_call | solution.py:207
  (102 shorter events, 13.6 us)
Async XLA Ops:
  0.6 9.2 %copy-start.2 = (bf16[1024,128]{1,0:T(8,128)(2,1)S(1)}, bf16[1024,128]{1,0:T(8,128)(2,1)}, u32[]{:S(2)}) copy-start(bf16[1024,128]{1,0:T(8,128)(2,1)} %param.11) | copy-start | bytes 786436
  0.6 9.3 %copy-start.3 = (bf16[1024,128]{1,0:T(8,128)(2,1)S(1)}, bf16[1024,128]{1,0:T(8,128)(2,1)}, u32[]{:S(2)}) copy-start(bf16[1024,128]{1,0:T(8,128)(2,1)} %param.12) | copy-start | bytes 786436
  0.7 19.7 %collective-permute-start.3 = (bf16[1024,2048]{1,0:T(8,128)(2,1)}, bf16[1024,2048]{1,0:T(8,128)(2,1)}, u32[]{:S(2)}, u32[]{:S(2)}) collective-permute-start(bf16[1024,2048]{1,0:T(8,128)(2,1)} %param.10), channel_id=1, source_target_pairs={{0,16},{1,17},{2,18},{3,19},{4,20},{5,21},{6,22},{7,23},{8,24},{9,... | collective-permute-start | bytes 12582920 | tf_op jit(solution)/shard_map/ppermute | solution.py:43
  3.2 16.1 %copy-start.4 = (bf16[4,4,8,1024]{3,2,1,0:T(8,128)(2,1)S(1)}, bf16[4,4,8,1024]{3,2,1,0:T(8,128)(2,1)}, u32[]{:S(2)}) copy-start(bf16[4,4,8,1024]{3,2,1,0:T(8,128)(2,1)} %order_rows.1) | copy-start | bytes 786436
  3.2 9.3 %collective-permute-start = (bf16[4,4,8,1024]{3,2,1,0:T(8,128)(2,1)}, bf16[4,4,8,1024]{3,2,1,0:T(8,128)(2,1)S(1)}, u32[]{:S(2)}, u32[]{:S(2)}) collective-permute-start(bf16[4,4,8,1024]{3,2,1,0:T(8,128)(2,1)} %order_rows.1), channel_id=1, source_target_pairs={{0,32},{1,33},{2,34},{3,35},{4,36},{5,37},{6,38},{7,39},{8,40},{9,... | collective-permute-start | bytes 786440 | tf_op jit(solution)/shard_map/ppermute | solution.py:43
  3.6 10.9 %collective-permute-start.1 = (bf16[4,4,8,1024]{3,2,1,0:T(8,128)(2,1)}, bf16[4,4,8,1024]{3,2,1,0:T(8,128)(2,1)S(1)}, u32[]{:S(2)}, u32[]{:S(2)}) collective-permute-start(bf16[4,4,8,1024]{3,2,1,0:T(8,128)(2,1)} %order_rows.1), channel_id=1, source_target_pairs={{0,64},{1,65},{2,66},{3,67},{4,68},{5,69},{6,70},{7,71},{8,72},{9,... | collective-permute-start | bytes 786440 | tf_op jit(solution)/shard_map/ppermute | solution.py:43
  6.1 13.2 %collective-permute-start.2 = (bf16[4,4,8,1024]{3,2,1,0:T(8,128)(2,1)}, bf16[4,4,8,1024]{3,2,1,0:T(8,128)(2,1)S(1)}, u32[]{:S(2)}, u32[]{:S(2)}) collective-permute-start(bf16[4,4,8,1024]{3,2,1,0:T(8,128)(2,1)} %order_rows.1), channel_id=1, source_target_pairs={{0,96},{1,97},{2,98},{3,99},{4,100},{5,101},{6,102},{7,103},{8,104... | collective-permute-start | bytes 786440 | tf_op jit(solution)/shard_map/ppermute | solution.py:43
  7.2 15.7 %collective-permute-start.4 = (bf16[1024,256]{1,0:T(8,128)(2,1)S(1)}, bf16[1024,256]{1,0:T(8,128)(2,1)S(1)}, u32[]{:S(2)}, u32[]{:S(2)}) collective-permute-start(bf16[1024,256]{1,0:T(8,128)(2,1)S(1)} %pad_maximum_fusion.2), channel_id=1, source_target_pairs={{0,16},{1,17},{2,18},{3,19},{4,20},{5,21},{6,22},{7,23},{8,24},{9,... | collective-permute-start | bytes 1572872 | tf_op jit(solution)/shard_map/ppermute | solution.py:43
  22.9 8.7 %copy-start.1 = (bf16[1024,4608]{1,0:T(8,128)(2,1)}, bf16[1024,4608]{1,0:T(8,128)(2,1)S(1)}, u32[]{:S(2)}) copy-start(bf16[1024,4608]{1,0:T(8,128)(2,1)S(1)} %constant_dynamic-update-slice_fusion) | copy-start | bytes 28311556
  26.0 17.6 %collective-permute-start.5 = (f16[128,4608]{1,0:T(8,128)(2,1)}, f16[128,4608]{1,0:T(8,128)(2,1)S(1)}, u32[]{:S(2)}, u32[]{:S(2)}) collective-permute-start(f16[128,4608]{1,0:T(8,128)(2,1)} %fusion.3), channel_id=1, source_target_pairs={{0,1},{1,2},{2,3},{3,0},{4,5},{5,6},{6,7},{7,4},{8,9},{9,10},{10,1... | collective-permute-start | bytes 3538952 | tf_op jit(solution)/shard_map/ppermute | solution.py:43
  30.1 16.4 %collective-permute-start.6 = (f16[128,4608]{1,0:T(8,128)(2,1)}, f16[128,4608]{1,0:T(8,128)(2,1)S(1)}, u32[]{:S(2)}, u32[]{:S(2)}) collective-permute-start(f16[128,4608]{1,0:T(8,128)(2,1)} %fusion.4), channel_id=1, source_target_pairs={{0,3},{1,0},{2,1},{3,2},{4,7},{5,4},{6,5},{7,6},{8,11},{9,8},{10,9... | collective-permute-start | bytes 3538952 | tf_op jit(solution)/shard_map/ppermute | solution.py:43
  31.6 4.5 %copy-start.14 = (s32[8]{0:T(128)S(1)}, s32[8]{0:T(128)}, u32[]{:S(2)}) copy-start(s32[8]{0:T(128)} %param.17) | copy-start | bytes 100
  34.1 23.5 %collective-permute-start.7 = (f16[128,4608]{1,0:T(8,128)(2,1)}, f16[128,4608]{1,0:T(8,128)(2,1)S(1)}, u32[]{:S(2)}, u32[]{:S(2)}) collective-permute-start(f16[128,4608]{1,0:T(8,128)(2,1)} %fusion.5), channel_id=1, source_target_pairs={{0,2},{1,3},{2,0},{3,1},{4,6},{5,7},{6,4},{7,5},{8,10},{9,11},{10,... | collective-permute-start | bytes 3538952 | tf_op jit(solution)/shard_map/ppermute | solution.py:43
  36.2 117.7 %collective-permute-start.20 = (bf16[2048,1024]{1,0:T(8,128)(2,1)}, bf16[2048,1024]{1,0:T(8,128)(2,1)}, u32[]{:S(2)}, u32[]{:S(2)}) collective-permute-start(bf16[2048,1024]{1,0:T(8,128)(2,1)} %param.13), channel_id=1, source_target_pairs={{0,16},{1,17},{2,18},{3,19},{4,20},{5,21},{6,22},{7,23},{8,24},{9,... | collective-permute-start | bytes 12582920 | tf_op jit(solution)/shard_map/ppermute | solution.py:43
  57.5 28.8 %slice-start = ((s8[7340032]{0:T(1024)(128)(4,1)}), s8[4194304]{0:T(1024)(128)(4,1)S(1)}, s32[]{:S(2)}) async-start(s8[7340032]{0:T(1024)(128)(4,1)} %bitcast.86), calls=%async_computation | async-start | bytes 8388608
  57.5 28.8 %slice-start.2 = ((s8[7340032]{0:T(1024)(128)(4,1)}), s8[4194304]{0:T(1024)(128)(4,1)S(1)}, s32[]{:S(2)}) async-start(s8[7340032]{0:T(1024)(128)(4,1)} %bitcast.88), calls=%async_computation.2 | async-start | bytes 8388608
  57.5 28.8 %slice-start.1 = ((s8[7340032]{0:T(1024)(128)(4,1)}), s8[3145728]{0:T(1024)(128)(4,1)S(1)}, s32[]{:S(2)}) async-start(s8[7340032]{0:T(1024)(128)(4,1)} %bitcast.86), calls=%async_computation.1 | async-start | bytes 6291456
  57.5 28.8 %slice-start.3 = ((s8[7340032]{0:T(1024)(128)(4,1)}), s8[3145728]{0:T(1024)(128)(4,1)S(1)}, s32[]{:S(2)}) async-start(s8[7340032]{0:T(1024)(128)(4,1)} %bitcast.88), calls=%async_computation.3 | async-start | bytes 6291456
  57.6 28.8 %copy-start = (s32[8]{0:T(128)S(1)}, s32[8]{0:T(128)}, u32[]{:S(2)}) copy-start(s32[8]{0:T(128)} %length.1) | copy-start | bytes 100
  63.6 11.5 %collective-permute-start.10 = (f16[32,4608]{1,0:T(8,128)(2,1)S(1)}, f16[32,4608]{1,0:T(8,128)(2,1)S(1)}, u32[]{:S(2)}, u32[]{:S(2)}) collective-permute-start(f16[32,4608]{1,0:T(8,128)(2,1)S(1)} %get-tuple-element.10), channel_id=1, source_target_pairs={{0,12},{1,13},{2,14},{3,15},{4,0},{5,1},{6,2},{7,3},{8,4},{9,5},{1... | collective-permute-start | bytes 884744 | tf_op jit(solution)/shard_map/ppermute | solution.py:43
  67.7 8.3 %collective-permute-start.8 = (f16[32,4608]{1,0:T(8,128)(2,1)S(1)}, f16[32,4608]{1,0:T(8,128)(2,1)S(1)}, u32[]{:S(2)}, u32[]{:S(2)}) collective-permute-start(f16[32,4608]{1,0:T(8,128)(2,1)S(1)} %get-tuple-element.9), channel_id=1, source_target_pairs={{0,8},{1,9},{2,10},{3,11},{4,12},{5,13},{6,14},{7,15},{8,0},{9,1},... | collective-permute-start | bytes 884744 | tf_op jit(solution)/shard_map/ppermute | solution.py:43
  67.7 11.1 %collective-permute-start.9 = (f16[32,4608]{1,0:T(8,128)(2,1)S(1)}, f16[32,4608]{1,0:T(8,128)(2,1)S(1)}, u32[]{:S(2)}, u32[]{:S(2)}) collective-permute-start(f16[32,4608]{1,0:T(8,128)(2,1)S(1)} %get-tuple-element.11), channel_id=1, source_target_pairs={{0,4},{1,5},{2,6},{3,7},{4,8},{5,9},{6,10},{7,11},{8,12},{9,13},{1... | collective-permute-start | bytes 884744 | tf_op jit(solution)/shard_map/ppermute | solution.py:43
  79.0 5.6 %collective-permute-start.11 = (bf16[8,4608]{1,0:T(8,128)(2,1)S(1)}, bf16[8,4608]{1,0:T(8,128)(2,1)S(1)}, u32[]{:S(2)}, u32[]{:S(2)}) collective-permute-start(bf16[8,4608]{1,0:T(8,128)(2,1)S(1)} %get-tuple-element.35), channel_id=1, source_target_pairs={{0,96},{1,97},{2,98},{3,99},{4,100},{5,101},{6,102},{7,103},{8,104... | collective-permute-start | bytes 221192 | tf_op jit(solution)/shard_map/ppermute | solution.py:43
  80.0 5.9 %collective-permute-start.12 = (bf16[8,4608]{1,0:T(8,128)(2,1)S(1)}, bf16[8,4608]{1,0:T(8,128)(2,1)S(1)}, u32[]{:S(2)}, u32[]{:S(2)}) collective-permute-start(bf16[8,4608]{1,0:T(8,128)(2,1)S(1)} %get-tuple-element.34), channel_id=1, source_target_pairs={{0,64},{1,65},{2,66},{3,67},{4,68},{5,69},{6,70},{7,71},{8,72},{9,... | collective-permute-start | bytes 221192 | tf_op jit(solution)/shard_map/ppermute | solution.py:43
  81.5 4.8 %collective-permute-start.13 = (bf16[8,4608]{1,0:T(8,128)(2,1)S(1)}, bf16[8,4608]{1,0:T(8,128)(2,1)S(1)}, u32[]{:S(2)}, u32[]{:S(2)}) collective-permute-start(bf16[8,4608]{1,0:T(8,128)(2,1)S(1)} %get-tuple-element.33), channel_id=1, source_target_pairs={{0,32},{1,33},{2,34},{3,35},{4,36},{5,37},{6,38},{7,39},{8,40},{9,... | collective-permute-start | bytes 221192 | tf_op jit(solution)/shard_map/ppermute | solution.py:43
  116.6 5.3 %collective-permute-start.14 = (bf16[8,4096]{1,0:T(8,128)(2,1)S(1)}, bf16[8,4096]{1,0:T(8,128)(2,1)S(1)}, u32[]{:S(2)}, u32[]{:S(2)}) collective-permute-start(bf16[8,4096]{1,0:T(8,128)(2,1)S(1)} %get-tuple-element.41), channel_id=1, source_target_pairs={{0,32},{1,33},{2,34},{3,35},{4,36},{5,37},{6,38},{7,39},{8,40},{9,... | collective-permute-start | bytes 196616 | tf_op jit(solution)/shard_map/ppermute | solution.py:43
  119.4 5.8 %collective-permute-start.15 = (bf16[8,4096]{1,0:T(8,128)(2,1)S(1)}, bf16[8,4096]{1,0:T(8,128)(2,1)S(1)}, u32[]{:S(2)}, u32[]{:S(2)}) collective-permute-start(bf16[8,4096]{1,0:T(8,128)(2,1)S(1)} %get-tuple-element.40), channel_id=1, source_target_pairs={{0,64},{1,65},{2,66},{3,67},{4,68},{5,69},{6,70},{7,71},{8,72},{9,... | collective-permute-start | bytes 196616 | tf_op jit(solution)/shard_map/ppermute | solution.py:43
  119.9 5.9 %collective-permute-start.16 = (bf16[8,4096]{1,0:T(8,128)(2,1)S(1)}, bf16[8,4096]{1,0:T(8,128)(2,1)S(1)}, u32[]{:S(2)}, u32[]{:S(2)}) collective-permute-start(bf16[8,4096]{1,0:T(8,128)(2,1)S(1)} %get-tuple-element.39), channel_id=1, source_target_pairs={{0,96},{1,97},{2,98},{3,99},{4,100},{5,101},{6,102},{7,103},{8,104... | collective-permute-start | bytes 196616 | tf_op jit(solution)/shard_map/ppermute | solution.py:43
  125.9 8.9 %collective-permute-start.17 = (bf16[4,8,4096]{2,1,0:T(8,128)(2,1)S(1)}, bf16[4,8,4096]{2,1,0:T(8,128)(2,1)S(1)}, u32[]{:S(2)}, u32[]{:S(2)}) collective-permute-start(bf16[4,8,4096]{2,1,0:T(8,128)(2,1)S(1)} %get-tuple-element.37), channel_id=1, source_target_pairs={{0,1},{1,2},{2,3},{3,0},{4,5},{5,6},{6,7},{7,4},{8,9},{9,10},{10,1... | collective-permute-start | bytes 786440 | tf_op jit(solution)/shard_map/ppermute | solution.py:43
  129.8 10.0 %collective-permute-start.18 = (bf16[4,8,4096]{2,1,0:T(8,128)(2,1)S(1)}, bf16[4,8,4096]{2,1,0:T(8,128)(2,1)S(1)}, u32[]{:S(2)}, u32[]{:S(2)}) collective-permute-start(bf16[4,8,4096]{2,1,0:T(8,128)(2,1)S(1)} %get-tuple-element.37), channel_id=1, source_target_pairs={{0,2},{1,3},{2,0},{3,1},{4,6},{5,7},{6,4},{7,5},{8,10},{9,11},{10,... | collective-permute-start | bytes 786440 | tf_op jit(solution)/shard_map/ppermute | solution.py:43
  131.9 18.4 %collective-permute-start.19 = (bf16[4,8,4096]{2,1,0:T(8,128)(2,1)S(1)}, bf16[4,8,4096]{2,1,0:T(8,128)(2,1)S(1)}, u32[]{:S(2)}, u32[]{:S(2)}) collective-permute-start(bf16[4,8,4096]{2,1,0:T(8,128)(2,1)S(1)} %get-tuple-element.37), channel_id=1, source_target_pairs={{0,3},{1,0},{2,1},{3,2},{4,7},{5,4},{6,5},{7,6},{8,11},{9,8},{10,9... | collective-permute-start | bytes 786440 | tf_op jit(solution)/shard_map/ppermute | solution.py:43
  150.4 16.5 %collective-permute-start.29 = (bf16[4,4,8,4096]{3,2,1,0:T(8,128)(2,1)S(1)}, bf16[4,4,8,4096]{3,2,1,0:T(8,128)(2,1)S(1)}, u32[]{:S(2)}, u32[]{:S(2)}) collective-permute-start(bf16[4,4,8,4096]{3,2,1,0:T(8,128)(2,1)S(1)} %pad_maximum_fusion.1), channel_id=1, source_target_pairs={{0,8},{1,9},{2,10},{3,11},{4,12},{5,13},{6,14},{7,15},{8,0},{9,1},... | collective-permute-start | bytes 3145736 | tf_op jit(solution)/shard_map/ppermute | solution.py:43
  150.5 27.3 %collective-permute-start.24 = (bf16[4,4,8,4096]{3,2,1,0:T(8,128)(2,1)S(1)}, bf16[4,4,8,4096]{3,2,1,0:T(8,128)(2,1)S(1)}, u32[]{:S(2)}, u32[]{:S(2)}) collective-permute-start(bf16[4,4,8,4096]{3,2,1,0:T(8,128)(2,1)S(1)} %pad_maximum_fusion.1), channel_id=1, source_target_pairs={{0,4},{1,5},{2,6},{3,7},{4,8},{5,9},{6,10},{7,11},{8,12},{9,13},{1... | collective-permute-start | bytes 3145736 | tf_op jit(solution)/shard_map/ppermute | solution.py:43
  150.6 32.5 %collective-permute-start.25 = (bf16[4,4,8,4096]{3,2,1,0:T(8,128)(2,1)S(1)}, bf16[4,4,8,4096]{3,2,1,0:T(8,128)(2,1)S(1)}, u32[]{:S(2)}, u32[]{:S(2)}) collective-permute-start(bf16[4,4,8,4096]{3,2,1,0:T(8,128)(2,1)S(1)} %pad_maximum_fusion.1), channel_id=1, source_target_pairs={{0,12},{1,13},{2,14},{3,15},{4,0},{5,1},{6,2},{7,3},{8,4},{9,5},{1... | collective-permute-start | bytes 3145736 | tf_op jit(solution)/shard_map/ppermute | solution.py:43
  158.7 29.0 %collective-permute-start.21 = (f32[1,4,8,1024]{3,2,1,0:T(8,128)S(1)}, f32[1,4,8,1024]{3,2,1,0:T(8,128)S(1)}, u32[]{:S(2)}, u32[]{:S(2)}) collective-permute-start(f32[1,4,8,1024]{3,2,1,0:T(8,128)S(1)} %get-tuple-element.30), channel_id=1, source_target_pairs={{0,64},{1,65},{2,66},{3,67},{4,68},{5,69},{6,70},{7,71},{8,72},{9,... | collective-permute-start | bytes 393224 | tf_op jit(solution)/shard_map/ppermute | solution.py:43
  159.7 29.9 %collective-permute-start.22 = (f32[1,4,8,1024]{3,2,1,0:T(8,128)S(1)}, f32[1,4,8,1024]{3,2,1,0:T(8,128)S(1)}, u32[]{:S(2)}, u32[]{:S(2)}) collective-permute-start(f32[1,4,8,1024]{3,2,1,0:T(8,128)S(1)} %get-tuple-element.29), channel_id=1, source_target_pairs={{0,96},{1,97},{2,98},{3,99},{4,100},{5,101},{6,102},{7,103},{8,104... | collective-permute-start | bytes 393224 | tf_op jit(solution)/shard_map/ppermute | solution.py:43
  166.9 25.3 %collective-permute-start.23 = (f32[1,4,8,1024]{3,2,1,0:T(8,128)S(1)}, f32[1,4,8,1024]{3,2,1,0:T(8,128)S(1)}, u32[]{:S(2)}, u32[]{:S(2)}) collective-permute-start(f32[1,4,8,1024]{3,2,1,0:T(8,128)S(1)} %get-tuple-element.28), channel_id=1, source_target_pairs={{0,32},{1,33},{2,34},{3,35},{4,36},{5,37},{6,38},{7,39},{8,40},{9,... | collective-permute-start | bytes 393224 | tf_op jit(solution)/shard_map/ppermute | solution.py:43
  177.8 14.4 %collective-permute-start.30 = (f32[1,4,8,1024]{3,2,1,0:T(8,128)S(1)}, f32[1,4,8,1024]{3,2,1,0:T(8,128)S(1)}, u32[]{:S(2)}, u32[]{:S(2)}) collective-permute-start(f32[1,4,8,1024]{3,2,1,0:T(8,128)S(1)} %get-tuple-element.18), channel_id=1, source_target_pairs={{0,64},{1,65},{2,66},{3,67},{4,68},{5,69},{6,70},{7,71},{8,72},{9,... | collective-permute-start | bytes 393224 | tf_op jit(solution)/shard_map/ppermute | solution.py:43
  187.4 13.4 %collective-permute-start.28 = (f32[2,4,8,1024]{3,2,1,0:T(8,128)S(1)}, f32[2,4,8,1024]{3,2,1,0:T(8,128)S(1)}, u32[]{:S(2)}, u32[]{:S(2)}) collective-permute-start(f32[2,4,8,1024]{3,2,1,0:T(8,128)S(1)} %pad_maximum_fusion.8), channel_id=1, source_target_pairs={{0,32},{1,33},{2,34},{3,35},{4,36},{5,37},{6,38},{7,39},{8,40},{9,... | collective-permute-start | bytes 786440 | tf_op jit(solution)/shard_map/ppermute | solution.py:43
  187.7 13.1 %copy-start.8 = (f32[1,4,8,1024]{3,2,1,0:T(8,128)}, f32[1,4,8,1024]{3,2,1,0:T(8,128)S(1)}, u32[]{:S(2)}) copy-start(f32[1,4,8,1024]{3,2,1,0:T(8,128)S(1)} %collective-permute-done.21.refs_1_) | copy-start | bytes 393220
  187.7 13.0 %collective-permute-start.27 = (f32[2,4,8,1024]{3,2,1,0:T(8,128)S(1)}, f32[2,4,8,1024]{3,2,1,0:T(8,128)S(1)}, u32[]{:S(2)}, u32[]{:S(2)}) collective-permute-start(f32[2,4,8,1024]{3,2,1,0:T(8,128)S(1)} %pad_maximum_fusion.7), channel_id=1, source_target_pairs={{0,96},{1,97},{2,98},{3,99},{4,100},{5,101},{6,102},{7,103},{8,104... | collective-permute-start | bytes 786440 | tf_op jit(solution)/shard_map/ppermute | solution.py:43
  189.6 11.2 %copy-start.9 = (f32[1,4,8,1024]{3,2,1,0:T(8,128)}, f32[1,4,8,1024]{3,2,1,0:T(8,128)S(1)}, u32[]{:S(2)}) copy-start(f32[1,4,8,1024]{3,2,1,0:T(8,128)S(1)} %collective-permute-done.22.refs_2_) | copy-start | bytes 393220
  189.6 11.2 %collective-permute-start.26 = (f32[2,4,8,1024]{3,2,1,0:T(8,128)S(1)}, f32[2,4,8,1024]{3,2,1,0:T(8,128)S(1)}, u32[]{:S(2)}, u32[]{:S(2)}) collective-permute-start(f32[2,4,8,1024]{3,2,1,0:T(8,128)S(1)} %pad_maximum_fusion.6), channel_id=1, source_target_pairs={{0,64},{1,65},{2,66},{3,67},{4,68},{5,69},{6,70},{7,71},{8,72},{9,... | collective-permute-start | bytes 786440 | tf_op jit(solution)/shard_map/ppermute | solution.py:43
  192.2 8.6 %copy-start.10 = (f32[1,4,8,1024]{3,2,1,0:T(8,128)}, f32[1,4,8,1024]{3,2,1,0:T(8,128)S(1)}, u32[]{:S(2)}) copy-start(f32[1,4,8,1024]{3,2,1,0:T(8,128)S(1)} %collective-permute-done.23.refs_3_) | copy-start | bytes 393220
  192.2 8.5 %collective-permute-start.31 = (f32[1,4,8,1024]{3,2,1,0:T(8,128)S(1)}, f32[1,4,8,1024]{3,2,1,0:T(8,128)S(1)}, u32[]{:S(2)}, u32[]{:S(2)}) collective-permute-start(f32[1,4,8,1024]{3,2,1,0:T(8,128)S(1)} %get-tuple-element.17), channel_id=1, source_target_pairs={{0,96},{1,97},{2,98},{3,99},{4,100},{5,101},{6,102},{7,103},{8,104... | collective-permute-start | bytes 393224 | tf_op jit(solution)/shard_map/ppermute | solution.py:43
  192.2 8.6 %copy-start.11 = (f32[1,4,8,1024]{3,2,1,0:T(8,128)}, f32[1,4,8,1024]{3,2,1,0:T(8,128)S(1)}, u32[]{:S(2)}) copy-start(f32[1,4,8,1024]{3,2,1,0:T(8,128)S(1)} %collective-permute-done.30.refs_9_) | copy-start | bytes 393220
  192.2 8.5 %collective-permute-start.32 = (f32[1,4,8,1024]{3,2,1,0:T(8,128)S(1)}, f32[1,4,8,1024]{3,2,1,0:T(8,128)S(1)}, u32[]{:S(2)}, u32[]{:S(2)}) collective-permute-start(f32[1,4,8,1024]{3,2,1,0:T(8,128)S(1)} %get-tuple-element.16), channel_id=1, source_target_pairs={{0,32},{1,33},{2,34},{3,35},{4,36},{5,37},{6,38},{7,39},{8,40},{9,... | collective-permute-start | bytes 393224 | tf_op jit(solution)/shard_map/ppermute | solution.py:43
  200.8 0.9 copy-start.7
  (4 other events, 3.1 us)
where the time goes:
time: 207 us; the launch traced here: 204 us
  waiting for transfers between devices  83 us (40%)
  starting transfers between devices  42 us (20%)
  Pallas kernels  34.3 us (17%)
  matrix products  30.6 us (15%)
  local copies, waits for them, and re-layouts  9.77 us (5%)
  other arithmetic  3.22 us (2%)
    ppermute x33, waiting for transfers between devices, permute(): return lax.ppermute(value, AXES, pairs)  83 us
    ppermute x33, starting transfers between devices, permute(): return lax.ppermute(value, AXES, pairs)  42 us
    pallas_call x1, Pallas kernels, attention(): pl.pallas_call(attention_kernel, out_shape=(jax.ShapeDtypeStruct(half, jn...  30.2 us
    dot_general x4, matrix products, project(): jnp.dot(part.reshape(-1, part.shape[-1]), w_output, preferred_element_typ...  16.8 us
    dot_general x4, matrix products, term(): jnp.dot(rows[step], weights, preferred_element_type=jnp.float32) * LIFT  13.8 us
    unnamed x42, local copies, waits for them, and re-layouts  6.19 us
  transfers between devices with their start and end apart: 33, of which 21 were waited for; matrix products, arithmetic and copies ran while one was open for 19% of the time, Pallas kernels for 16%

commit v1 on v0

v1 whole, which is shorter than its diff:
```python
import functools
import math

import jax
import jax.numpy as jnp
from jax import lax
from jax.experimental import pallas as pl
from jax.experimental.pallas import tpu as pltpu
from jax.sharding import PartitionSpec as P

HQ = 128
KVH = 8
DH = 128
CACHE = 448
GROUP = HQ // KVH
AXES = ("gx", "gy")
SIDE = 4
ROWS = 8
LIFT = 32.0
PIECES = ((((0, 1, 2, 3),), (1, 3)), (((0, 1, 3), (2,)), (0, 2)))


def rope_frequencies():
    index = jnp.arange(DH // 2, dtype=jnp.float32)
    base = jnp.power(jnp.float32(500000.0), -2.0 * index / DH)
    wavelength = 2.0 * math.pi / base
    smooth = (8192.0 / wavelength - 1.0) / 3.0
    middle = (1.0 - smooth) * base / 8.0 + smooth * base
    return jnp.where(wavelength > 8192.0, base / 8.0, jnp.where(wavelength < 2048.0, base, middle))


def permute(value, move):
    pairs = []
    for x in range(SIDE):
        for c in range(2):
            for z in range(SIDE):
                for y in range(SIDE):
                    tx, tc, tz, ty = move(x, c, z, y)
                    target = ((tx % SIDE) * 2 + tc) * SIDE + tz % SIDE
                    source = (x * 2 + c) * SIDE + z
                    pairs.append((source * SIDE + y, target * SIDE + ty % SIDE))
    return lax.ppermute(value, AXES, pairs)


def to_pair(value):
    return permute(value, lambda x, c, z, y: (x, 1 - c, z, y))


def along_x(value, step):
    return permute(value, lambda x, c, z, y: (x + step, c, z, y))


def along_first(value, step):
    return permute(value, lambda x, c, z, y: (x, c, z + step * c, y + step * (1 - c)))


def along_second(value, step):
    return permute(value, lambda x, c, z, y: (x, c, z + step * (1 - c), y + step * c))


def group_at(place, first, second, sign):
    z, y, core = place[0], place[1], place[2]
    dz = jnp.where(core == 0, second, first)
    dy = jnp.where(core == 0, first, second)
    return lax.rem(z + sign * dz + SIDE, SIDE) * SIDE + lax.rem(y + sign * dy + SIDE, SIDE)


def order_kernel(place, h_ref, out_ref):
    for first in range(SIDE):
        for second in range(SIDE):
            out_ref[first, second] = h_ref[group_at(place, first, second, 1)]


def order_rows(place, hidden):
    width = hidden.shape[1]
    return pl.pallas_call(
        order_kernel,
        out_shape=jax.ShapeDtypeStruct((SIDE, SIDE, ROWS, width), hidden.dtype),
        in_specs=[pl.BlockSpec(memory_space=pltpu.SMEM), pl.BlockSpec(memory_space=pltpu.VMEM)],
        out_specs=pl.BlockSpec(memory_space=pltpu.VMEM),
        cost_estimate=pl.CostEstimate(flops=0, bytes_accessed=2**19, transcendentals=0),
        name="order_rows",
    )(place, hidden.reshape(SIDE * SIDE, ROWS, width))


def total_of(first, others):
    return functools.reduce(
        jnp.add, [first.astype(jnp.float32)] + [item.astype(jnp.float32) for item in others]
    )


def after(value, *others):
    return lax.optimization_barrier((value, *others))[0]


def sum_over_plane(groups, weights, earlier):
    width = weights.shape[1]
    rows = jnp.stack(groups, axis=2)
    terms = jnp.dot(
        rows.reshape(-1, rows.shape[-1]), weights, preferred_element_type=jnp.float32
    )
    terms = (terms * LIFT).astype(jnp.float16).reshape(SIDE, SIDE * len(groups) * ROWS, width)
    came = {}
    for step in (1, 3, 2):
        message = after(terms[step], earlier[step]) if earlier else terms[step]
        came[step] = along_first(message, step)
    kept = total_of(terms[0], came.values()).reshape(SIDE, len(groups) * ROWS, width)
    last = [along_second(kept[step].astype(jnp.float16), step) for step in (2, 1, 3)]
    kept = total_of(kept[0], last) * (1.0 / LIFT)
    return kept.astype(jnp.bfloat16).reshape(len(groups), ROWS, width), came


def attention_kernel(
    place,
    q_ref,
    cos_ref,
    sin_ref,
    mask_ref,
    k_ref,
    v_ref,
    _,
    __,
    o_ref,
    nk_ref,
    nv_ref,
    queries,
    results,
):
    cosine = cos_ref[...]
    sine = sin_ref[...]
    scale = DH ** (-0.5)
    for pair in range(2):
        base = pair * (GROUP + 2) * DH

        def column(h):
            return q_ref[0, :, base + h * DH : base + (h + 1) * DH]

        def rotated(h):
            u = column(h).astype(jnp.float32)
            return (u * cosine + pltpu.roll(u, DH // 2, 1) * sine).astype(jnp.bfloat16)

        head = pl.ds(pl.multiple_of((place[0] + pair) % 2 * DH, DH), DH)
        for h in range(GROUP):
            queries[pair, pl.ds(h, ROWS, stride=GROUP), :] = rotated(h).astype(jnp.float32)
        key_new = rotated(GROUP)
        value_new = column(GROUP + 1)
        nk_ref[:, head] = key_new
        nv_ref[:, head] = value_new
        key_new = key_new.astype(jnp.float32)
        value_new = value_new.astype(jnp.float32)
        q = queries[pair].reshape(ROWS, GROUP, DH)
        scores = lax.dot_general(
            q.astype(jnp.bfloat16),
            k_ref[:, :, head],
            (((2,), (2,)), ((0,), (0,))),
            preferred_element_type=jnp.float32,
        )
        scores = scores * scale + mask_ref[...]
        score_new = jnp.sum(q * key_new[:, None, :], axis=2, keepdims=True) * scale
        top = jnp.maximum(jnp.max(scores, axis=2, keepdims=True), score_new)
        expo = jnp.exp(scores - top)
        expo_new = jnp.exp(score_new - top)
        share = 1.0 / (jnp.sum(expo, axis=2, keepdims=True) + expo_new)
        weights = (expo * share).astype(jnp.bfloat16)
        weight_new = (expo_new * share).astype(jnp.bfloat16).astype(jnp.float32)
        result = lax.dot_general(
            weights,
            v_ref[:, :, head],
            (((2,), (1,)), ((0,), (0,))),
            preferred_element_type=jnp.float32,
        )
        result = result + weight_new * value_new[:, None, :]
        results[pair] = result.reshape(ROWS * GROUP, DH)
        for h in range(GROUP):
            where = (pair * GROUP + h) * DH
            o_ref[0, :, where : where + DH] = results[
                pair, pl.ds(h, ROWS, stride=GROUP), :
            ].astype(jnp.bfloat16)


def attention(place, packed, cosine, sine, mask, cache_keys, cache_values, keys, values):
    steps, _, width = packed.shape
    chip = KVH // SIDE * DH
    cache = pl.BlockSpec((ROWS, CACHE, chip), lambda r, place: (0, 0, place[1 + r]))
    whole = pl.BlockSpec((ROWS, DH), lambda r, place: (0, 0))
    column = pl.BlockSpec((ROWS, chip), lambda r, place: (0, place[1 + r]))
    new = jax.ShapeDtypeStruct((ROWS, KVH * DH), jnp.bfloat16)
    return pl.pallas_call(
        attention_kernel,
        out_shape=(jax.ShapeDtypeStruct((steps, ROWS, chip * GROUP), jnp.bfloat16), new, new),
        grid_spec=pltpu.PrefetchScalarGridSpec(
            num_scalar_prefetch=1,
            grid=(steps,),
            in_specs=[
                pl.BlockSpec((1, ROWS, width), lambda r, place: (r, 0, 0)),
                whole,
                whole,
                pl.BlockSpec((ROWS, GROUP, CACHE), lambda r, place: (0, 0, 0)),
                cache,
                cache,
                pl.BlockSpec(memory_space=pl.ANY),
                pl.BlockSpec(memory_space=pl.ANY),
            ],
            out_specs=(
                pl.BlockSpec((1, ROWS, chip * GROUP), lambda r, place: (r, 0, 0)),
                column,
                column,
            ),
            scratch_shapes=[pltpu.VMEM((2, ROWS * GROUP, DH), jnp.float32)] * 2,
        ),
        input_output_aliases={7: 1, 8: 2},
        compiler_params=pltpu.CompilerParams(vmem_limit_bytes=32 * 2**20),
        cost_estimate=pl.CostEstimate(
            flops=4 * ROWS * HQ * CACHE * DH * steps // SIDE,
            bytes_accessed=4 * ROWS * CACHE * KVH * DH * steps // SIDE,
            transcendentals=ROWS * HQ * CACHE * steps // SIDE,
        ),
        name="attention",
    )(place, packed, cosine, sine, mask, cache_keys, cache_values, keys, values)


def final_kernel(place, *refs):
    terms, out_ref = refs[:-1], refs[-1]
    for second in range(SIDE):
        for first in range(SIDE):
            total = 0.0
            at = 0
            for pieces, group in PIECES:
                for piece in pieces:
                    if second in piece:
                        for term in terms[at : at + len(group)]:
                            total = total + term[piece.index(second), first]
                    at += len(group)
            out_ref[group_at(place, first, second, -1)] = total.astype(jnp.bfloat16)


def add_up(place, terms):
    width = terms[0].shape[-1]
    return pl.pallas_call(
        final_kernel,
        out_shape=jax.ShapeDtypeStruct((SIDE * SIDE, ROWS, width), jnp.bfloat16),
        in_specs=[pl.BlockSpec(memory_space=pltpu.SMEM)]
        + [pl.BlockSpec(memory_space=pltpu.VMEM)] * len(terms),
        out_specs=pl.BlockSpec(memory_space=pltpu.VMEM),
        cost_estimate=pl.CostEstimate(flops=2**19, bytes_accessed=2**21, transcendentals=0),
        name="add_up",
    )(place, *terms)


def project(parts, group, w_output):
    rows = jnp.concatenate([part.reshape(-1, part.shape[-1]) for part in parts], axis=0)
    terms = jnp.dot(rows, w_output, preferred_element_type=jnp.float32)
    terms = terms.reshape(len(parts), SIDE, len(group), ROWS, -1)
    return [along_x(terms[:, :, i], -dx) if dx else terms[:, :, i] for i, dx in enumerate(group)]


def on_device(
    hidden_in, w_query, w_key, w_value, w_output, cache_keys, cache_values, cache_lengths, positions
):
    gx = lax.axis_index("gx")
    gy = lax.axis_index("gy")
    x, core = gx // 2, gx % 2
    place = jnp.stack([gy // SIDE, gy % SIDE, core]).astype(jnp.int32)

    own = order_rows(place, hidden_in)
    hidden = {0: own}
    for step in (1, 3, 2):
        hidden[step] = along_x(own, step)
    w_both = jnp.concatenate([w_key, w_value], axis=1)
    pair_query = to_pair(w_query)
    w_both = jnp.concatenate([w_query, w_both, pair_query, to_pair(w_both)], axis=1)
    w_back = jnp.concatenate([w_output, to_pair(after(w_output, pair_query))], axis=0)

    angle = positions.astype(jnp.float32)[:, None] * rope_frequencies()[None, :]
    cosine, sine = jnp.cos(angle), jnp.sin(angle)
    cosine = jnp.concatenate([cosine, cosine], axis=1)
    sine = jnp.concatenate([-sine, sine], axis=1)
    kept = jnp.arange(CACHE)[None, None, :] < cache_lengths[:, None, None]
    mask = jnp.where(kept, 0.0, -jnp.inf).astype(jnp.float32)
    mask = jnp.broadcast_to(mask, (mask.shape[0], GROUP, CACHE))
    new_keys = jnp.zeros((ROWS, KVH * DH), jnp.bfloat16)
    new_values = jnp.zeros((ROWS, KVH * DH), jnp.bfloat16)

    terms = []
    came = {}
    for pieces, group in PIECES:
        summed, came = sum_over_plane([hidden[dx] for dx in group], w_both, came)
        packed = [along_x(summed[i], -dx) if dx else summed[i] for i, dx in enumerate(group)]
        chips = jnp.stack([core] + [(x + dx) % SIDE for dx in group]).astype(jnp.int32)
        mixed, new_keys, new_values = attention(
            chips,
            jnp.stack(packed),
            cosine,
            sine,
            mask,
            cache_keys,
            cache_values,
            new_keys,
            new_values,
        )
        rows = [along_x(mixed[i], dx) if dx else mixed[i] for i, dx in enumerate(group)]
        rows = jnp.stack(rows)
        near = {0: rows}
        for step in (2, 1, 3):
            near[step] = along_first(rows, step)
        rows = jnp.stack([near[step] for step in range(SIDE)])
        far = {0: rows}
        for step in (1, 3, 2):
            far[step] = along_second(rows, step)
        for piece in pieces:
            terms += project([far[step] for step in piece], group, w_back)
    attended = add_up(place, terms)
    return (attended.reshape(hidden_in.shape), new_keys, new_values)


def solution(mesh):
    placed = (
        P("gx", "gy"),
        P("gy", "gx"),
        P("gy", "gx"),
        P("gy", "gx"),
        P("gx", "gy"),
        P(("gx", "gy"), None, None),
        P(("gx", "gy"), None, None),
        P(("gx", "gy")),
        P(("gx", "gy")),
    )
    return jax.shard_map(
        on_device,
        mesh=mesh,
        in_specs=placed,
        out_specs=(P("gx", "gy"), P(("gx", "gy"), None), P(("gx", "gy"), None)),
        check_vma=False,
    )
```

time: 207 us -> 165 us (0.80)
  waiting for transfers between devices: 83 us -> 51.9 us
  Pallas kernels: 34.3 us -> 14.6 us
  local copies, waits for them, and re-layouts: 9.77 us -> 21.4 us
  matrix products: 30.6 us -> 19.1 us
  starting transfers between devices: 42 us -> 50.3 us
    ppermute x33 -> x40, waiting for transfers between devices: 83 us -> 51.9 us  [permute(): return lax.ppermute(value, AXES, pairs)]
    pallas_call x1 -> x2, Pallas kernels: 30.2 us -> 10.5 us  [attention(): pl.pallas_call(attention_kernel, out_shape=(jax.ShapeDtypeStruct((steps,...]
    dot_general x8 -> x5, matrix products: 30.6 us -> 19.1 us  [the longest x2 13.2 us: sum_over_plane(): jnp.dot(rows.reshape(-1, rows.shape[-1]), weights, preferred_element_type...]
    ppermute x33 -> x40, starting transfers between devices: 42 us -> 50.3 us  [permute(): return lax.ppermute(value, AXES, pairs)]
    unnamed x42 -> x39, local copies, waits for them, and re-layouts: 6.19 us -> 14.3 us
    concatenate x1 -> x2, local copies, waits for them, and re-layouts: 0.04 us -> 3.5 us  [the longest x1 2.64 us: on_device(): jnp.concatenate([w_output, to_pair(after(w_output, pair_query))], axis=0)]
  transfers between devices with their start and end apart: 33 -> 40, of which waited for: 21 -> 18; matrix products, arithmetic and copies ran while one was open for 19% -> 20% of each run, Pallas kernels for 16% -> 8%
where the time goes in v1:
time: 165 us; the launch traced here: 162 us
  waiting for transfers between devices  51.9 us (31%)
  starting transfers between devices  50.3 us (30%)
  local copies, waits for them, and re-layouts  21.4 us (13%)
  matrix products  19.1 us (12%)
  Pallas kernels  14.6 us (9%)
  other arithmetic  4 us (2%)
    ppermute x40, waiting for transfers between devices, permute(): return lax.ppermute(value, AXES, pairs)  51.9 us
    ppermute x40, starting transfers between devices, permute(): return lax.ppermute(value, AXES, pairs)  50.3 us
    unnamed x39, local copies, waits for them, and re-layouts  14.3 us
    dot_general x2, matrix products, sum_over_plane(): jnp.dot(rows.reshape(-1, rows.shape[-1]), weights, preferred_element_type...  13.2 us
    pallas_call x2, Pallas kernels, attention(): pl.pallas_call(attention_kernel, out_shape=(jax.ShapeDtypeStruct((steps,...  10.5 us
    dot_general x3, matrix products, project(): terms = jnp.dot(rows, w_output, preferred_element_type=jnp.float32)  5.83 us
  transfers between devices with their start and end apart: 40, of which 18 were waited for; matrix products, arithmetic and copies ran while one was open for 20% of the time, Pallas kernels for 8%

profile of v1, /device:TPU:6, one launch (start us, length us, event | category | flops | bytes accessed | tf_op | source)
XLA Modules:
  0.0 162.4 jit_solution(3331947861132398185)
XLA Ops:
  1.4 1.8 %order_rows.1 = bf16[4,4,8,1024]{3,2,1,0:T(8,128)(2,1)} custom-call(s32[3]{0:T(128)} %pad_add_fusion.place, bf16[16,8,1024]{2,1,0:T(8,128)(2,1)} %bitcast.95), custom_call_target="tpu_custom_call" | custom-call | bytes 524288 | tf_op jit(solution)/shard_map/order_rows/pallas_call | solution.py:76
  3.5 1.6 %collective-permute-start.1 = (bf16[4,4,8,1024]{3,2,1,0:T(8,128)(2,1)}, bf16[4,4,8,1024]{3,2,1,0:T(8,128)(2,1)S(1)}, u32[]{:S(2)}, u32[]{:S(2)}) collective-permute-start(bf16[4,4,8,1024]{3,2,1,0:T(8,128)(2,1)} %order_rows.1), channel_id=1, source_target_pairs={{0,96},{1,97},{2,98},{3,99},{4,100},{5,101},{6,102},{7,103},{8,104... | collective-permute-start | bytes 786440 | tf_op jit(solution)/shard_map/ppermute | solution.py:42
  5.1 1.4 collective-permute-start.23
  8.7 2.7 %constant_dynamic-update-slice_fusion.4 = bf16[1024,4608]{1,0:T(8,128)(2,1)S(1)} fusion(bf16[1024,2048]{1,0:T(8,128)(2,1)} %param.10), kind=kLoop, calls=%fused_computation.57 | loop fusion | bytes 8388608
  12.2 2.5 %constant_dynamic-update-slice_fusion.6 = bf16[4096,1024]{1,0:T(8,128)(2,1)} fusion(bf16[2048,1024]{1,0:T(8,128)(2,1)S(1)} %copy-done), kind=kLoop, calls=%fused_computation.59 | loop fusion | bytes 8388608
  14.8 1.7 %copy-done.2 = bf16[1024,4608]{1,0:T(8,128)(2,1)} copy-done((bf16[1024,4608]{1,0:T(8,128)(2,1)}, bf16[1024,4608]{1,0:T(8,128)(2,1)S(1)}, u32[]{:S(2)}) %copy-start.2) | copy-done | bytes 9437208
  17.4 1.6 collective-permute-done.1
  19.2 4.8 %constant_dynamic-update-slice_fusion.1 = bf16[1024,4608]{1,0:T(8,128)(2,1)} fusion(bf16[1024,4608]{1,0:T(8,128)(2,1)} %constant_dynamic-update-slice_fusion.2, bf16[1024,2048]{1,0:T(8,128)(2,1)} %collective-permute-done.2), kind=kLoop, calls=%fused_computation.54 | loop fusion | bytes 8388608
  24.9 6.5 %fusion.2 = f16[256,4608]{1,0:T(8,128)(2,1)S(1)} fusion(bf16[256,1024]{1,0:T(8,128)(2,1)S(1)} %bitcast.93, bf16[1024,4608]{1,0:T(8,128)(2,1)} %constant_dynamic-update-slice_fusion), kind=kOutput, calls=%fused_computation.4 | convolution fusion | flops 2418278400 | bytes 12320768 | tf_op jit(solution)/shard_map/dot_general | solution.py:99
  31.7 1.7 %collective-permute-start.4 = (f16[64,4608]{1,0:T(8,128)(2,1)S(1)}, f16[64,4608]{1,0:T(8,128)(2,1)S(1)}, u32[]{:S(2)}, u32[]{:S(2)}) collective-permute-start(f16[64,4608]{1,0:T(8,128)(2,1)S(1)} %get-tuple-element.30), channel_id=1, source_target_pairs={{0,1},{1,2},{2,3},{3,0},{4,5},{5,6},{6,7},{7,4},{8,9},{9,10},{10,1... | collective-permute-start | bytes 1769480 | tf_op jit(solution)/shard_map/ppermute | solution.py:42
  33.4 1.6 collective-permute-start.5
  35.0 2.1 %collective-permute-start.6 = (f16[64,4608]{1,0:T(8,128)(2,1)S(1)}, f16[64,4608]{1,0:T(8,128)(2,1)S(1)}, u32[]{:S(2)}, u32[]{:S(2)}) collective-permute-start(f16[64,4608]{1,0:T(8,128)(2,1)S(1)} %get-tuple-element.31), channel_id=1, source_target_pairs={{0,2},{1,3},{2,0},{3,1},{4,6},{5,7},{6,4},{7,5},{8,10},{9,11},{10,... | collective-permute-start | bytes 1769480 | tf_op jit(solution)/shard_map/ppermute | solution.py:42
  37.1 6.7 %fusion.3 = f16[256,4608]{1,0:T(8,128)(2,1)S(1)} fusion(bf16[256,1024]{1,0:T(8,128)(2,1)S(1)} %bitcast.92, bf16[1024,4608]{1,0:T(8,128)(2,1)} %constant_dynamic-update-slice_fusion), kind=kOutput, calls=%fused_computation.5 | convolution fusion | flops 2418278400 | bytes 12320768 | tf_op jit(solution)/shard_map/dot_general | solution.py:99
  43.8 6.7 %collective-permute-done.6 = f16[64,4608]{1,0:T(8,128)(2,1)S(1)} collective-permute-done((f16[64,4608]{1,0:T(8,128)(2,1)S(1)}, f16[64,4608]{1,0:T(8,128)(2,1)S(1)}, u32[]{:S(2)}, u32[]{:S(2)}) %collective-permute-start.6) | collective-permute-done | bytes 589856 | tf_op jit(solution)/shard_map/ppermute | solution.py:42
  51.0 4.0 %collective-permute-start.7 = (f16[16,4608]{1,0:T(8,128)(2,1)S(1)}, f16[16,4608]{1,0:T(8,128)(2,1)S(1)}, u32[]{:S(2)}, u32[]{:S(2)}) collective-permute-start(f16[16,4608]{1,0:T(8,128)(2,1)S(1)} %get-tuple-element.40), channel_id=1, source_target_pairs={{0,8},{1,9},{2,10},{3,11},{4,12},{5,13},{6,14},{7,15},{8,0},{9,1},... | collective-permute-start | bytes 442376 | tf_op jit(solution)/shard_map/ppermute | solution.py:42
  56.0 2.2 %collective-permute-start.9 = (f16[16,4608]{1,0:T(8,128)(2,1)S(1)}, f16[16,4608]{1,0:T(8,128)(2,1)S(1)}, u32[]{:S(2)}, u32[]{:S(2)}) collective-permute-start(f16[16,4608]{1,0:T(8,128)(2,1)S(1)} %get-tuple-element.41), channel_id=1, source_target_pairs={{0,12},{1,13},{2,14},{3,15},{4,0},{5,1},{6,2},{7,3},{8,4},{9,5},{1... | collective-permute-start | bytes 442376 | tf_op jit(solution)/shard_map/ppermute | solution.py:42
  58.6 1.5 collective-permute-start.24
  60.1 1.8 %collective-permute-start.25 = (f16[64,4608]{1,0:T(8,128)(2,1)S(1)}, f16[64,4608]{1,0:T(8,128)(2,1)S(1)}, u32[]{:S(2)}, u32[]{:S(2)}) collective-permute-start(f16[64,4608]{1,0:T(8,128)(2,1)S(1)} %get-tuple-element.16), channel_id=1, source_target_pairs={{0,3},{1,0},{2,1},{3,2},{4,7},{5,4},{6,5},{7,6},{8,11},{9,8},{10,9... | collective-permute-start | bytes 1769480 | tf_op jit(solution)/shard_map/ppermute | solution.py:42
  62.3 7.4 %collective-permute-done.24 = f16[64,4608]{1,0:T(8,128)(2,1)S(1)} collective-permute-done((f16[64,4608]{1,0:T(8,128)(2,1)S(1)}, f16[64,4608]{1,0:T(8,128)(2,1)S(1)}, u32[]{:S(2)}, u32[]{:S(2)}) %collective-permute-start.24) | collective-permute-done | bytes 589856 | tf_op jit(solution)/shard_map/ppermute | solution.py:42
  69.8 5.9 %collective-permute-done.25 = f16[64,4608]{1,0:T(8,128)(2,1)S(1)} collective-permute-done((f16[64,4608]{1,0:T(8,128)(2,1)S(1)}, f16[64,4608]{1,0:T(8,128)(2,1)S(1)}, u32[]{:S(2)}, u32[]{:S(2)}) %collective-permute-start.25) | collective-permute-done | bytes 589856 | tf_op jit(solution)/shard_map/ppermute | solution.py:42
  76.7 1.3 collective-permute-start.27
  78.9 2.3 %collective-permute-start.29 = (f16[16,4608]{1,0:T(8,128)(2,1)S(1)}, f16[16,4608]{1,0:T(8,128)(2,1)S(1)}, u32[]{:S(2)}, u32[]{:S(2)}) collective-permute-start(f16[16,4608]{1,0:T(8,128)(2,1)S(1)} %get-tuple-element.38), channel_id=1, source_target_pairs={{0,12},{1,13},{2,14},{3,15},{4,0},{5,1},{6,2},{7,3},{8,4},{9,5},{1... | collective-permute-start | bytes 442376 | tf_op jit(solution)/shard_map/ppermute | solution.py:42
  81.2 1.2 collective-permute-start.11
  83.5 1.5 collective-permute-done.28
  85.1 1.8 %collective-permute-start.30 = (bf16[8,4608]{1,0:T(8,128)(2,1)S(1)}, bf16[8,4608]{1,0:T(8,128)(2,1)S(1)}, u32[]{:S(2)}, u32[]{:S(2)}) collective-permute-start(bf16[8,4608]{1,0:T(8,128)(2,1)S(1)} %get-tuple-element.46), channel_id=1, source_target_pairs={{0,64},{1,65},{2,66},{3,67},{4,68},{5,69},{6,70},{7,71},{8,72},{9,... | collective-permute-start | bytes 221192 | tf_op jit(solution)/shard_map/ppermute | solution.py:42
  86.9 2.7 %collective-permute-done.10 = bf16[8,4608]{1,0:T(8,128)(2,1)S(1)} collective-permute-done((bf16[8,4608]{1,0:T(8,128)(2,1)S(1)}, bf16[8,4608]{1,0:T(8,128)(2,1)S(1)}, u32[]{:S(2)}, u32[]{:S(2)}) %collective-permute-start.10) | collective-permute-done | bytes 73760 | tf_op jit(solution)/shard_map/ppermute | solution.py:42
  91.0 5.3 %attention.2 = (bf16[2,8,4096]{2,1,0:T(8,128)(2,1)S(1)}, bf16[8,1024]{1,0:T(8,128)(2,1)}, bf16[8,1024]{1,0:T(8,128)(2,1)}) custom-call(s32[3]{0:T(128)S(1)} %pad_add_fusion.1.place, bf16[2,8,4608]{2,1,0:T(8,128)(2,1)S(1)} %pad_maximum_fusion.5.q_ref, f32[8,128]{1,0:T(8,128)S(1)} %get-tuple-element.60.cos_ref, ...), custom_call_target="tpu_custom_call", output_to_operand_aliasing={{1}: (7, {}), {2}: (8, {})} | custom-call | flops 117440512 | bytes 7340032 | tf_op jit(solution)/shard_map/attention/pallas_call | solution.py:188
  96.2 5.3 %attention.3 = (bf16[2,8,4096]{2,1,0:T(8,128)(2,1)S(1)}, bf16[8,1024]{1,0:T(8,128)(2,1)}, bf16[8,1024]{1,0:T(8,128)(2,1)}) custom-call(s32[3]{0:T(128)S(1)} %pad_add_fusion.2.place, bf16[2,8,4608]{2,1,0:T(8,128)(2,1)S(1)} %pad_maximum_fusion.6.q_ref, f32[8,128]{1,0:T(8,128)S(1)} %get-tuple-element.60.cos_ref, ...), custom_call_target="tpu_custom_call", output_to_operand_aliasing={{1}: (7, {}), {2}: (8, {})} | custom-call | flops 117440512 | bytes 7340032 | tf_op jit(solution)/shard_map/attention/pallas_call | solution.py:188
  102.6 1.1 collective-permute-start.13
  103.7 3.6 %collective-permute-done.31 = bf16[8,4096]{1,0:T(8,128)(2,1)S(1)} collective-permute-done((bf16[8,4096]{1,0:T(8,128)(2,1)S(1)}, bf16[8,4096]{1,0:T(8,128)(2,1)S(1)}, u32[]{:S(2)}, u32[]{:S(2)}) %collective-permute-start.31) | collective-permute-done | bytes 65568 | tf_op jit(solution)/shard_map/ppermute | solution.py:42
  107.4 1.4 collective-permute-start.32
  108.8 2.5 %collective-permute-start.33 = (bf16[2,8,4096]{2,1,0:T(8,128)(2,1)S(1)}, bf16[2,8,4096]{2,1,0:T(8,128)(2,1)S(1)}, u32[]{:S(2)}, u32[]{:S(2)}) collective-permute-start(bf16[2,8,4096]{2,1,0:T(8,128)(2,1)S(1)} %get-tuple-element.50), channel_id=1, source_target_pairs={{0,2},{1,3},{2,0},{3,1},{4,6},{5,7},{6,4},{7,5},{8,10},{9,11},{10,... | collective-permute-start | bytes 393224 | tf_op jit(solution)/shard_map/ppermute | solution.py:42
  111.8 1.7 %collective-permute-start.14 = (bf16[2,8,4096]{2,1,0:T(8,128)(2,1)S(1)}, bf16[2,8,4096]{2,1,0:T(8,128)(2,1)S(1)}, u32[]{:S(2)}, u32[]{:S(2)}) collective-permute-start(bf16[2,8,4096]{2,1,0:T(8,128)(2,1)S(1)} %get-tuple-element.54), channel_id=1, source_target_pairs={{0,1},{1,2},{2,3},{3,0},{4,5},{5,6},{6,7},{7,4},{8,9},{9,10},{10,1... | collective-permute-start | bytes 393224 | tf_op jit(solution)/shard_map/ppermute | solution.py:42
  114.5 1.4 collective-permute-done.33
  115.9 1.3 collective-permute-start.16
  117.9 2.3 %collective-permute-done.14 = bf16[2,8,4096]{2,1,0:T(8,128)(2,1)S(1)} collective-permute-done((bf16[2,8,4096]{2,1,0:T(8,128)(2,1)S(1)}, bf16[2,8,4096]{2,1,0:T(8,128)(2,1)S(1)}, u32[]{:S(2)}, u32[]{:S(2)}) %collective-permute-start.14) | collective-permute-done | bytes 131104 | tf_op jit(solution)/shard_map/ppermute | solution.py:42
  120.2 1.6 collective-permute-start.36
  121.8 1.6 collective-permute-done.16
  123.5 3.9 %collective-permute-start.18 = (bf16[4,2,8,4096]{3,2,1,0:T(8,128)(2,1)S(1)}, bf16[4,2,8,4096]{3,2,1,0:T(8,128)(2,1)S(1)}, u32[]{:S(2)}, u32[]{:S(2)}) collective-permute-start(bf16[4,2,8,4096]{3,2,1,0:T(8,128)(2,1)S(1)} %pad_maximum_fusion.2), channel_id=1, source_target_pairs={{0,8},{1,9},{2,10},{3,11},{4,12},{5,13},{6,14},{7,15},{8,0},{9,1},... | collective-permute-start | bytes 1572872 | tf_op jit(solution)/shard_map/ppermute | solution.py:42
  128.0 2.6 %constant_dynamic-update-slice_fusion.5 = bf16[4096,1024]{1,0:T(8,128)(2,1)S(1)} fusion(bf16[4096,1024]{1,0:T(8,128)(2,1)S(1)} %bitcast.86, bf16[2048,1024]{1,0:T(8,128)(2,1)} %collective-permute-done.20), kind=kLoop, calls=%fused_computation.58 | loop fusion | bytes 8388608 | tf_op jit(solution)/shard_map/concatenate | solution.py:272
  130.7 1.9 %collective-permute-start.38 = (bf16[4,2,8,4096]{3,2,1,0:T(8,128)(2,1)S(1)}, bf16[4,2,8,4096]{3,2,1,0:T(8,128)(2,1)S(1)}, u32[]{:S(2)}, u32[]{:S(2)}) collective-permute-start(bf16[4,2,8,4096]{3,2,1,0:T(8,128)(2,1)S(1)} %pad_maximum_fusion.4), channel_id=1, source_target_pairs={{0,8},{1,9},{2,10},{3,11},{4,12},{5,13},{6,14},{7,15},{8,0},{9,1},... | collective-permute-start | bytes 1572872 | tf_op jit(solution)/shard_map/ppermute | solution.py:42
  132.6 1.8 %fusion.12 = f32[192,1024]{1,0:T(8,128)S(1)} fusion(bf16[4096,1024]{1,0:T(8,128)(2,1)S(1)} %constant_dynamic-update-slice_fusion.5, bf16[64,4096]{1,0:T(8,128)(2,1)S(1)} %bitcast.113, bf16[64,4096]{1,0:T(8,128)(2,1)S(1)} %bitcast.111, bf16[64,4096]{1,0:T(8,128)(2,1)S(1)} %bitcast.90), kind=kOutput, calls=%fused_computation.14 | convolution fusion | flops 1615331328 | bytes 10747904 | tf_op jit(solution)/shard_map/dot_general | solution.py:252
  136.2 3.9 %collective-permute-done.18 = bf16[4,2,8,4096]{3,2,1,0:T(8,128)(2,1)S(1)} collective-permute-done((bf16[4,2,8,4096]{3,2,1,0:T(8,128)(2,1)S(1)}, bf16[4,2,8,4096]{3,2,1,0:T(8,128)(2,1)S(1)}, u32[]{:S(2)}, u32[]{:S(2)}) %collective-permute-start.18) | collective-permute-done | bytes 524320 | tf_op jit(solution)/shard_map/ppermute | solution.py:42
  140.6 2.4 %fusion.4 = f32[256,1024]{1,0:T(8,128)S(1)} fusion(bf16[4096,1024]{1,0:T(8,128)(2,1)S(1)} %constant_dynamic-update-slice_fusion.5, bf16[64,4096]{1,0:T(8,128)(2,1)S(1)} %bitcast.115, bf16[64,4096]{1,0:T(8,128)(2,1)S(1)} %bitcast.114, bf16[64,4096]{1,0:T(8,128)(2,1)S(1)} %bitcast.112, bf16[64,4096]{1,0:T(8,128)(2,1)S(1)} %bitcast.91), kind=kOutput, calls=%fused_computation.6 | convolution fusion | flops 2155872256 | bytes 11534336 | tf_op jit(solution)/shard_map/dot_general | solution.py:252
  143.2 3.2 %collective-permute-start.22 = (f32[4,4,8,1024]{3,2,1,0:T(8,128)S(1)}, f32[4,4,8,1024]{3,2,1,0:T(8,128)S(1)}, u32[]{:S(2)}, u32[]{:S(2)}) collective-permute-start(f32[4,4,8,1024]{3,2,1,0:T(8,128)S(1)} %get-tuple-element.33), channel_id=1, source_target_pairs={{0,32},{1,33},{2,34},{3,35},{4,36},{5,37},{6,38},{7,39},{8,40},{9,... | collective-permute-start | bytes 1572872 | tf_op jit(solution)/shard_map/ppermute | solution.py:42
  146.4 1.6 fusion.18
  148.7 10.0 %collective-permute-done.39.refs_5_ = f32[1,4,8,1024]{3,2,1,0:T(8,128)S(1)} collective-permute-done((f32[1,4,8,1024]{3,2,1,0:T(8,128)S(1)}, f32[1,4,8,1024]{3,2,1,0:T(8,128)S(1)}, u32[]{:S(2)}, u32[]{:S(2)}) %collective-permute-start.39) | collective-permute-done | bytes 131104 | tf_op jit(solution)/shard_map/ppermute | solution.py:42
  160.1 2.3 %add_up.1 = bf16[16,8,1024]{2,1,0:T(8,128)(2,1)} custom-call(s32[3]{0:T(128)} %pad_add_fusion.place, f32[4,4,8,1024]{3,2,1,0:T(8,128)} %copy-done.6, f32[4,4,8,1024]{3,2,1,0:T(8,128)} %copy-done.7, f32[3,4,8,1024]{3,2,1,0:T(8,128)} %get-tuple-element.36.refs_2_, f32[3,4,8,1024]{3,2,1,0:T(8,128)} %copy-done.8, f32[1,4,8,1024]{3,2,1,0:T(8,128)} %get-tuple-element.44.refs_4_, ...), custom_call_target="tpu_custom_call" | custom-call | flops 524288 | bytes 2097152 | tf_op jit(solution)/shard_map/add_up/pallas_call | solution.py:239
  (122 shorter events, 21.4 us)
Async XLA Ops:
  0.6 18.5 %collective-permute-start.2 = (bf16[1024,2048]{1,0:T(8,128)(2,1)}, bf16[1024,2048]{1,0:T(8,128)(2,1)}, u32[]{:S(2)}, u32[]{:S(2)}) collective-permute-start(bf16[1024,2048]{1,0:T(8,128)(2,1)} %param.10), channel_id=1, source_target_pairs={{0,16},{1,17},{2,18},{3,19},{4,20},{5,21},{6,22},{7,23},{8,24},{9,... | collective-permute-start | bytes 12582920 | tf_op jit(solution)/shard_map/ppermute | solution.py:42
  3.1 14.2 %collective-permute-start = (bf16[4,4,8,1024]{3,2,1,0:T(8,128)(2,1)}, bf16[4,4,8,1024]{3,2,1,0:T(8,128)(2,1)S(1)}, u32[]{:S(2)}, u32[]{:S(2)}) collective-permute-start(bf16[4,4,8,1024]{3,2,1,0:T(8,128)(2,1)} %order_rows.1), channel_id=1, source_target_pairs={{0,32},{1,33},{2,34},{3,35},{4,36},{5,37},{6,38},{7,39},{8,40},{9,... | collective-permute-start | bytes 786440 | tf_op jit(solution)/shard_map/ppermute | solution.py:42
  3.5 15.4 %collective-permute-start.1 = (bf16[4,4,8,1024]{3,2,1,0:T(8,128)(2,1)}, bf16[4,4,8,1024]{3,2,1,0:T(8,128)(2,1)S(1)}, u32[]{:S(2)}, u32[]{:S(2)}) collective-permute-start(bf16[4,4,8,1024]{3,2,1,0:T(8,128)(2,1)} %order_rows.1), channel_id=1, source_target_pairs={{0,96},{1,97},{2,98},{3,99},{4,100},{5,101},{6,102},{7,103},{8,104... | collective-permute-start | bytes 786440 | tf_op jit(solution)/shard_map/ppermute | solution.py:42
  5.1 13.9 %collective-permute-start.23 = (bf16[4,4,8,1024]{3,2,1,0:T(8,128)(2,1)}, bf16[4,4,8,1024]{3,2,1,0:T(8,128)(2,1)S(1)}, u32[]{:S(2)}, u32[]{:S(2)}) collective-permute-start(bf16[4,4,8,1024]{3,2,1,0:T(8,128)(2,1)} %order_rows.1), channel_id=1, source_target_pairs={{0,64},{1,65},{2,66},{3,67},{4,68},{5,69},{6,70},{7,71},{8,72},{9,... | collective-permute-start | bytes 786440 | tf_op jit(solution)/shard_map/ppermute | solution.py:42
  7.6 16.4 %collective-permute-start.3 = (bf16[1024,256]{1,0:T(8,128)(2,1)S(1)}, bf16[1024,256]{1,0:T(8,128)(2,1)S(1)}, u32[]{:S(2)}, u32[]{:S(2)}) collective-permute-start(bf16[1024,256]{1,0:T(8,128)(2,1)S(1)} %pad_maximum_fusion.1), channel_id=1, source_target_pairs={{0,16},{1,17},{2,18},{3,19},{4,20},{5,21},{6,22},{7,23},{8,24},{9,... | collective-permute-start | bytes 1572872 | tf_op jit(solution)/shard_map/ppermute | solution.py:42
  12.2 6.8 %copy-start.3 = (bf16[4,4,8,1024]{3,2,1,0:T(8,128)(2,1)S(1)}, bf16[4,4,8,1024]{3,2,1,0:T(8,128)(2,1)}, u32[]{:S(2)}) copy-start(bf16[4,4,8,1024]{3,2,1,0:T(8,128)(2,1)} %order_rows.1) | copy-start | bytes 786436
  31.7 12.1 %collective-permute-start.4 = (f16[64,4608]{1,0:T(8,128)(2,1)S(1)}, f16[64,4608]{1,0:T(8,128)(2,1)S(1)}, u32[]{:S(2)}, u32[]{:S(2)}) collective-permute-start(f16[64,4608]{1,0:T(8,128)(2,1)S(1)} %get-tuple-element.30), channel_id=1, source_target_pairs={{0,1},{1,2},{2,3},{3,0},{4,5},{5,6},{6,7},{7,4},{8,9},{9,10},{10,1... | collective-permute-start | bytes 1769480 | tf_op jit(solution)/shard_map/ppermute | solution.py:42
  33.4 10.4 %collective-permute-start.5 = (f16[64,4608]{1,0:T(8,128)(2,1)S(1)}, f16[64,4608]{1,0:T(8,128)(2,1)S(1)}, u32[]{:S(2)}, u32[]{:S(2)}) collective-permute-start(f16[64,4608]{1,0:T(8,128)(2,1)S(1)} %get-tuple-element.32), channel_id=1, source_target_pairs={{0,3},{1,0},{2,1},{3,2},{4,7},{5,4},{6,5},{7,6},{8,11},{9,8},{10,9... | collective-permute-start | bytes 1769480 | tf_op jit(solution)/shard_map/ppermute | solution.py:42
  35.0 15.5 %collective-permute-start.6 = (f16[64,4608]{1,0:T(8,128)(2,1)S(1)}, f16[64,4608]{1,0:T(8,128)(2,1)S(1)}, u32[]{:S(2)}, u32[]{:S(2)}) collective-permute-start(f16[64,4608]{1,0:T(8,128)(2,1)S(1)} %get-tuple-element.31), channel_id=1, source_target_pairs={{0,2},{1,3},{2,0},{3,1},{4,6},{5,7},{6,4},{7,5},{8,10},{9,11},{10,... | collective-permute-start | bytes 1769480 | tf_op jit(solution)/shard_map/ppermute | solution.py:42
  37.1 53.8 %slice-start.2 = ((s8[7340032]{0:T(1024)(128)(4,1)}), s8[4194304]{0:T(1024)(128)(4,1)S(1)}, s32[]{:S(2)}) async-start(s8[7340032]{0:T(1024)(128)(4,1)} %bitcast.83), calls=%async_computation.2 | async-start | bytes 8388608
  37.1 53.8 %slice-start.3 = ((s8[7340032]{0:T(1024)(128)(4,1)}), s8[3145728]{0:T(1024)(128)(4,1)S(1)}, s32[]{:S(2)}) async-start(s8[7340032]{0:T(1024)(128)(4,1)} %bitcast.83), calls=%async_computation.3 | async-start | bytes 6291456
  43.8 14.7 %copy-start.1 = (bf16[2048,1024]{1,0:T(8,128)(2,1)S(1)}, bf16[2048,1024]{1,0:T(8,128)(2,1)}, u32[]{:S(2)}) copy-start(bf16[2048,1024]{1,0:T(8,128)(2,1)} %param.13) | copy-start | bytes 12582916
  50.5 40.4 %slice-start = ((s8[7340032]{0:T(1024)(128)(4,1)}), s8[4194304]{0:T(1024)(128)(4,1)S(1)}, s32[]{:S(2)}) async-start(s8[7340032]{0:T(1024)(128)(4,1)} %bitcast.81), calls=%async_computation | async-start | bytes 8388608
  51.0 9.1 %collective-permute-start.7 = (f16[16,4608]{1,0:T(8,128)(2,1)S(1)}, f16[16,4608]{1,0:T(8,128)(2,1)S(1)}, u32[]{:S(2)}, u32[]{:S(2)}) collective-permute-start(f16[16,4608]{1,0:T(8,128)(2,1)S(1)} %get-tuple-element.40), channel_id=1, source_target_pairs={{0,8},{1,9},{2,10},{3,11},{4,12},{5,13},{6,14},{7,15},{8,0},{9,1},... | collective-permute-start | bytes 442376 | tf_op jit(solution)/shard_map/ppermute | solution.py:42
  55.0 6.9 %collective-permute-start.8 = (f16[16,4608]{1,0:T(8,128)(2,1)S(1)}, f16[16,4608]{1,0:T(8,128)(2,1)S(1)}, u32[]{:S(2)}, u32[]{:S(2)}) collective-permute-start(f16[16,4608]{1,0:T(8,128)(2,1)S(1)} %get-tuple-element.42), channel_id=1, source_target_pairs={{0,4},{1,5},{2,6},{3,7},{4,8},{5,9},{6,10},{7,11},{8,12},{9,13},{1... | collective-permute-start | bytes 442376 | tf_op jit(solution)/shard_map/ppermute | solution.py:42
  56.0 34.9 %slice-start.1 = ((s8[7340032]{0:T(1024)(128)(4,1)}), s8[3145728]{0:T(1024)(128)(4,1)S(1)}, s32[]{:S(2)}) async-start(s8[7340032]{0:T(1024)(128)(4,1)} %bitcast.81), calls=%async_computation.1 | async-start | bytes 6291456
  56.0 6.3 %collective-permute-start.9 = (f16[16,4608]{1,0:T(8,128)(2,1)S(1)}, f16[16,4608]{1,0:T(8,128)(2,1)S(1)}, u32[]{:S(2)}, u32[]{:S(2)}) collective-permute-start(f16[16,4608]{1,0:T(8,128)(2,1)S(1)} %get-tuple-element.41), channel_id=1, source_target_pairs={{0,12},{1,13},{2,14},{3,15},{4,0},{5,1},{6,2},{7,3},{8,4},{9,5},{1... | collective-permute-start | bytes 442376 | tf_op jit(solution)/shard_map/ppermute | solution.py:42
  58.5 68.8 %collective-permute-start.20 = (bf16[2048,1024]{1,0:T(8,128)(2,1)S(1)}, bf16[2048,1024]{1,0:T(8,128)(2,1)}, u32[]{:S(2)}, u32[]{:S(2)}) collective-permute-start(bf16[2048,1024]{1,0:T(8,128)(2,1)S(1)} %copy-done.1), channel_id=1, source_target_pairs={{0,16},{1,17},{2,18},{3,19},{4,20},{5,21},{6,22},{7,23},{8,24},{9,... | collective-permute-start | bytes 12582920 | tf_op jit(solution)/shard_map/ppermute | solution.py:42
  58.6 11.2 %collective-permute-start.24 = (f16[64,4608]{1,0:T(8,128)(2,1)S(1)}, f16[64,4608]{1,0:T(8,128)(2,1)S(1)}, u32[]{:S(2)}, u32[]{:S(2)}) collective-permute-start(f16[64,4608]{1,0:T(8,128)(2,1)S(1)} %get-tuple-element.15), channel_id=1, source_target_pairs={{0,1},{1,2},{2,3},{3,0},{4,5},{5,6},{6,7},{7,4},{8,9},{9,10},{10,1... | collective-permute-start | bytes 1769480 | tf_op jit(solution)/shard_map/ppermute | solution.py:42
  60.1 15.6 %collective-permute-start.25 = (f16[64,4608]{1,0:T(8,128)(2,1)S(1)}, f16[64,4608]{1,0:T(8,128)(2,1)S(1)}, u32[]{:S(2)}, u32[]{:S(2)}) collective-permute-start(f16[64,4608]{1,0:T(8,128)(2,1)S(1)} %get-tuple-element.16), channel_id=1, source_target_pairs={{0,3},{1,0},{2,1},{3,2},{4,7},{5,4},{6,5},{7,6},{8,11},{9,8},{10,9... | collective-permute-start | bytes 1769480 | tf_op jit(solution)/shard_map/ppermute | solution.py:42
  61.9 14.4 %collective-permute-start.26 = (f16[64,4608]{1,0:T(8,128)(2,1)S(1)}, f16[64,4608]{1,0:T(8,128)(2,1)S(1)}, u32[]{:S(2)}, u32[]{:S(2)}) collective-permute-start(f16[64,4608]{1,0:T(8,128)(2,1)S(1)} %get-tuple-element.17), channel_id=1, source_target_pairs={{0,2},{1,3},{2,0},{3,1},{4,6},{5,7},{6,4},{7,5},{8,10},{9,11},{10,... | collective-permute-start | bytes 1769480 | tf_op jit(solution)/shard_map/ppermute | solution.py:42
  76.7 6.8 %collective-permute-start.27 = (f16[16,4608]{1,0:T(8,128)(2,1)S(1)}, f16[16,4608]{1,0:T(8,128)(2,1)S(1)}, u32[]{:S(2)}, u32[]{:S(2)}) collective-permute-start(f16[16,4608]{1,0:T(8,128)(2,1)S(1)} %get-tuple-element.37), channel_id=1, source_target_pairs={{0,8},{1,9},{2,10},{3,11},{4,12},{5,13},{6,14},{7,15},{8,0},{9,1},... | collective-permute-start | bytes 442376 | tf_op jit(solution)/shard_map/ppermute | solution.py:42
  78.0 7.1 %collective-permute-start.28 = (f16[16,4608]{1,0:T(8,128)(2,1)S(1)}, f16[16,4608]{1,0:T(8,128)(2,1)S(1)}, u32[]{:S(2)}, u32[]{:S(2)}) collective-permute-start(f16[16,4608]{1,0:T(8,128)(2,1)S(1)} %get-tuple-element.39), channel_id=1, source_target_pairs={{0,4},{1,5},{2,6},{3,7},{4,8},{5,9},{6,10},{7,11},{8,12},{9,13},{1... | collective-permute-start | bytes 442376 | tf_op jit(solution)/shard_map/ppermute | solution.py:42
  78.9 6.1 %collective-permute-start.29 = (f16[16,4608]{1,0:T(8,128)(2,1)S(1)}, f16[16,4608]{1,0:T(8,128)(2,1)S(1)}, u32[]{:S(2)}, u32[]{:S(2)}) collective-permute-start(f16[16,4608]{1,0:T(8,128)(2,1)S(1)} %get-tuple-element.38), channel_id=1, source_target_pairs={{0,12},{1,13},{2,14},{3,15},{4,0},{5,1},{6,2},{7,3},{8,4},{9,5},{1... | collective-permute-start | bytes 442376 | tf_op jit(solution)/shard_map/ppermute | solution.py:42
  81.2 5.7 %collective-permute-start.11 = (bf16[8,4608]{1,0:T(8,128)(2,1)S(1)}, bf16[8,4608]{1,0:T(8,128)(2,1)S(1)}, u32[]{:S(2)}, u32[]{:S(2)}) collective-permute-start(bf16[8,4608]{1,0:T(8,128)(2,1)S(1)} %get-tuple-element.48), channel_id=1, source_target_pairs={{0,32},{1,33},{2,34},{3,35},{4,36},{5,37},{6,38},{7,39},{8,40},{9,... | collective-permute-start | bytes 221192 | tf_op jit(solution)/shard_map/ppermute | solution.py:42
  83.5 6.1 %collective-permute-start.10 = (bf16[8,4608]{1,0:T(8,128)(2,1)S(1)}, bf16[8,4608]{1,0:T(8,128)(2,1)S(1)}, u32[]{:S(2)}, u32[]{:S(2)}) collective-permute-start(bf16[8,4608]{1,0:T(8,128)(2,1)S(1)} %get-tuple-element.47), channel_id=1, source_target_pairs={{0,96},{1,97},{2,98},{3,99},{4,100},{5,101},{6,102},{7,103},{8,104... | collective-permute-start | bytes 221192 | tf_op jit(solution)/shard_map/ppermute | solution.py:42
  85.1 11.1 %collective-permute-start.30 = (bf16[8,4608]{1,0:T(8,128)(2,1)S(1)}, bf16[8,4608]{1,0:T(8,128)(2,1)S(1)}, u32[]{:S(2)}, u32[]{:S(2)}) collective-permute-start(bf16[8,4608]{1,0:T(8,128)(2,1)S(1)} %get-tuple-element.46), channel_id=1, source_target_pairs={{0,64},{1,65},{2,66},{3,67},{4,68},{5,69},{6,70},{7,71},{8,72},{9,... | collective-permute-start | bytes 221192 | tf_op jit(solution)/shard_map/ppermute | solution.py:42
  90.9 37.1 %slice-start.4 = ((s8[8388608]{0:T(1024)(128)(4,1)}), s8[4194304]{0:T(1024)(128)(4,1)S(1)}, s32[]{:S(2)}) async-start(s8[8388608]{0:T(1024)(128)(4,1)} %bitcast.85), calls=%async_computation.4 | async-start | bytes 8388608
  96.2 31.8 %slice-start.5 = ((s8[8388608]{0:T(1024)(128)(4,1)}), s8[4194304]{0:T(1024)(128)(4,1)S(1)}, s32[]{:S(2)}) async-start(s8[8388608]{0:T(1024)(128)(4,1)} %bitcast.85), calls=%async_computation.5 | async-start | bytes 8388608
  101.5 5.8 %collective-permute-start.31 = (bf16[8,4096]{1,0:T(8,128)(2,1)S(1)}, bf16[8,4096]{1,0:T(8,128)(2,1)S(1)}, u32[]{:S(2)}, u32[]{:S(2)}) collective-permute-start(bf16[8,4096]{1,0:T(8,128)(2,1)S(1)} %get-tuple-element.52), channel_id=1, source_target_pairs={{0,64},{1,65},{2,66},{3,67},{4,68},{5,69},{6,70},{7,71},{8,72},{9,... | collective-permute-start | bytes 196616 | tf_op jit(solution)/shard_map/ppermute | solution.py:42
  101.6 9.7 %collective-permute-start.12 = (bf16[8,4096]{1,0:T(8,128)(2,1)S(1)}, bf16[8,4096]{1,0:T(8,128)(2,1)S(1)}, u32[]{:S(2)}, u32[]{:S(2)}) collective-permute-start(bf16[8,4096]{1,0:T(8,128)(2,1)S(1)} %get-tuple-element.55), channel_id=1, source_target_pairs={{0,32},{1,33},{2,34},{3,35},{4,36},{5,37},{6,38},{7,39},{8,40},{9,... | collective-permute-start | bytes 196616 | tf_op jit(solution)/shard_map/ppermute | solution.py:42
  102.6 9.1 %collective-permute-start.13 = (bf16[8,4096]{1,0:T(8,128)(2,1)S(1)}, bf16[8,4096]{1,0:T(8,128)(2,1)S(1)}, u32[]{:S(2)}, u32[]{:S(2)}) collective-permute-start(bf16[8,4096]{1,0:T(8,128)(2,1)S(1)} %get-tuple-element.56), channel_id=1, source_target_pairs={{0,96},{1,97},{2,98},{3,99},{4,100},{5,101},{6,102},{7,103},{8,104... | collective-permute-start | bytes 196616 | tf_op jit(solution)/shard_map/ppermute | solution.py:42
  107.4 6.2 %collective-permute-start.32 = (bf16[2,8,4096]{2,1,0:T(8,128)(2,1)S(1)}, bf16[2,8,4096]{2,1,0:T(8,128)(2,1)S(1)}, u32[]{:S(2)}, u32[]{:S(2)}) collective-permute-start(bf16[2,8,4096]{2,1,0:T(8,128)(2,1)S(1)} %get-tuple-element.50), channel_id=1, source_target_pairs={{0,1},{1,2},{2,3},{3,0},{4,5},{5,6},{6,7},{7,4},{8,9},{9,10},{10,1... | collective-permute-start | bytes 393224 | tf_op jit(solution)/shard_map/ppermute | solution.py:42
  108.8 7.1 %collective-permute-start.33 = (bf16[2,8,4096]{2,1,0:T(8,128)(2,1)S(1)}, bf16[2,8,4096]{2,1,0:T(8,128)(2,1)S(1)}, u32[]{:S(2)}, u32[]{:S(2)}) collective-permute-start(bf16[2,8,4096]{2,1,0:T(8,128)(2,1)S(1)} %get-tuple-element.50), channel_id=1, source_target_pairs={{0,2},{1,3},{2,0},{3,1},{4,6},{5,7},{6,4},{7,5},{8,10},{9,11},{10,... | collective-permute-start | bytes 393224 | tf_op jit(solution)/shard_map/ppermute | solution.py:42
  111.3 6.4 %collective-permute-start.34 = (bf16[2,8,4096]{2,1,0:T(8,128)(2,1)S(1)}, bf16[2,8,4096]{2,1,0:T(8,128)(2,1)S(1)}, u32[]{:S(2)}, u32[]{:S(2)}) collective-permute-start(bf16[2,8,4096]{2,1,0:T(8,128)(2,1)S(1)} %get-tuple-element.50), channel_id=1, source_target_pairs={{0,3},{1,0},{2,1},{3,2},{4,7},{5,4},{6,5},{7,6},{8,11},{9,8},{10,9... | collective-permute-start | bytes 393224 | tf_op jit(solution)/shard_map/ppermute | solution.py:42
  111.8 8.4 %collective-permute-start.14 = (bf16[2,8,4096]{2,1,0:T(8,128)(2,1)S(1)}, bf16[2,8,4096]{2,1,0:T(8,128)(2,1)S(1)}, u32[]{:S(2)}, u32[]{:S(2)}) collective-permute-start(bf16[2,8,4096]{2,1,0:T(8,128)(2,1)S(1)} %get-tuple-element.54), channel_id=1, source_target_pairs={{0,1},{1,2},{2,3},{3,0},{4,5},{5,6},{6,7},{7,4},{8,9},{9,10},{10,1... | collective-permute-start | bytes 393224 | tf_op jit(solution)/shard_map/ppermute | solution.py:42
  113.6 8.1 %collective-permute-start.15 = (bf16[2,8,4096]{2,1,0:T(8,128)(2,1)S(1)}, bf16[2,8,4096]{2,1,0:T(8,128)(2,1)S(1)}, u32[]{:S(2)}, u32[]{:S(2)}) collective-permute-start(bf16[2,8,4096]{2,1,0:T(8,128)(2,1)S(1)} %get-tuple-element.54), channel_id=1, source_target_pairs={{0,2},{1,3},{2,0},{3,1},{4,6},{5,7},{6,4},{7,5},{8,10},{9,11},{10,... | collective-permute-start | bytes 393224 | tf_op jit(solution)/shard_map/ppermute | solution.py:42
  115.9 7.4 %collective-permute-start.16 = (bf16[2,8,4096]{2,1,0:T(8,128)(2,1)S(1)}, bf16[2,8,4096]{2,1,0:T(8,128)(2,1)S(1)}, u32[]{:S(2)}, u32[]{:S(2)}) collective-permute-start(bf16[2,8,4096]{2,1,0:T(8,128)(2,1)S(1)} %get-tuple-element.54), channel_id=1, source_target_pairs={{0,3},{1,0},{2,1},{3,2},{4,7},{5,4},{6,5},{7,6},{8,11},{9,8},{10,9... | collective-permute-start | bytes 393224 | tf_op jit(solution)/shard_map/ppermute | solution.py:42
  117.8 12.9 %collective-permute-start.35 = (bf16[4,2,8,4096]{3,2,1,0:T(8,128)(2,1)S(1)}, bf16[4,2,8,4096]{3,2,1,0:T(8,128)(2,1)S(1)}, u32[]{:S(2)}, u32[]{:S(2)}) collective-permute-start(bf16[4,2,8,4096]{3,2,1,0:T(8,128)(2,1)S(1)} %pad_maximum_fusion.4), channel_id=1, source_target_pairs={{0,4},{1,5},{2,6},{3,7},{4,8},{5,9},{6,10},{7,11},{8,12},{9,13},{1... | collective-permute-start | bytes 1572872 | tf_op jit(solution)/shard_map/ppermute | solution.py:42
  120.2 12.4 %collective-permute-start.36 = (bf16[4,2,8,4096]{3,2,1,0:T(8,128)(2,1)S(1)}, bf16[4,2,8,4096]{3,2,1,0:T(8,128)(2,1)S(1)}, u32[]{:S(2)}, u32[]{:S(2)}) collective-permute-start(bf16[4,2,8,4096]{3,2,1,0:T(8,128)(2,1)S(1)} %pad_maximum_fusion.4), channel_id=1, source_target_pairs={{0,12},{1,13},{2,14},{3,15},{4,0},{5,1},{6,2},{7,3},{8,4},{9,5},{1... | collective-permute-start | bytes 1572872 | tf_op jit(solution)/shard_map/ppermute | solution.py:42
  123.4 12.8 %collective-permute-start.17 = (bf16[4,2,8,4096]{3,2,1,0:T(8,128)(2,1)S(1)}, bf16[4,2,8,4096]{3,2,1,0:T(8,128)(2,1)S(1)}, u32[]{:S(2)}, u32[]{:S(2)}) collective-permute-start(bf16[4,2,8,4096]{3,2,1,0:T(8,128)(2,1)S(1)} %pad_maximum_fusion.2), channel_id=1, source_target_pairs={{0,4},{1,5},{2,6},{3,7},{4,8},{5,9},{6,10},{7,11},{8,12},{9,13},{1... | collective-permute-start | bytes 1572872 | tf_op jit(solution)/shard_map/ppermute | solution.py:42
  123.5 16.7 %collective-permute-start.18 = (bf16[4,2,8,4096]{3,2,1,0:T(8,128)(2,1)S(1)}, bf16[4,2,8,4096]{3,2,1,0:T(8,128)(2,1)S(1)}, u32[]{:S(2)}, u32[]{:S(2)}) collective-permute-start(bf16[4,2,8,4096]{3,2,1,0:T(8,128)(2,1)S(1)} %pad_maximum_fusion.2), channel_id=1, source_target_pairs={{0,8},{1,9},{2,10},{3,11},{4,12},{5,13},{6,14},{7,15},{8,0},{9,1},... | collective-permute-start | bytes 1572872 | tf_op jit(solution)/shard_map/ppermute | solution.py:42
  127.4 13.3 %collective-permute-start.19 = (bf16[4,2,8,4096]{3,2,1,0:T(8,128)(2,1)S(1)}, bf16[4,2,8,4096]{3,2,1,0:T(8,128)(2,1)S(1)}, u32[]{:S(2)}, u32[]{:S(2)}) collective-permute-start(bf16[4,2,8,4096]{3,2,1,0:T(8,128)(2,1)S(1)} %pad_maximum_fusion.2), channel_id=1, source_target_pairs={{0,12},{1,13},{2,14},{3,15},{4,0},{5,1},{6,2},{7,3},{8,4},{9,5},{1... | collective-permute-start | bytes 1572872 | tf_op jit(solution)/shard_map/ppermute | solution.py:42
  130.7 15.7 %collective-permute-start.38 = (bf16[4,2,8,4096]{3,2,1,0:T(8,128)(2,1)S(1)}, bf16[4,2,8,4096]{3,2,1,0:T(8,128)(2,1)S(1)}, u32[]{:S(2)}, u32[]{:S(2)}) collective-permute-start(bf16[4,2,8,4096]{3,2,1,0:T(8,128)(2,1)S(1)} %pad_maximum_fusion.4), channel_id=1, source_target_pairs={{0,8},{1,9},{2,10},{3,11},{4,12},{5,13},{6,14},{7,15},{8,0},{9,1},... | collective-permute-start | bytes 1572872 | tf_op jit(solution)/shard_map/ppermute | solution.py:42
  135.2 23.4 %collective-permute-start.37 = (f32[3,4,8,1024]{3,2,1,0:T(8,128)S(1)}, f32[3,4,8,1024]{3,2,1,0:T(8,128)S(1)}, u32[]{:S(2)}, u32[]{:S(2)}) collective-permute-start(f32[3,4,8,1024]{3,2,1,0:T(8,128)S(1)} %get-tuple-element.35), channel_id=1, source_target_pairs={{0,64},{1,65},{2,66},{3,67},{4,68},{5,69},{6,70},{7,71},{8,72},{9,... | collective-permute-start | bytes 1179656 | tf_op jit(solution)/shard_map/ppermute | solution.py:42
  143.1 16.0 %collective-permute-start.21 = (f32[4,4,8,1024]{3,2,1,0:T(8,128)S(1)}, f32[4,4,8,1024]{3,2,1,0:T(8,128)S(1)}, u32[]{:S(2)}, u32[]{:S(2)}) collective-permute-start(f32[4,4,8,1024]{3,2,1,0:T(8,128)S(1)} %get-tuple-element.34), channel_id=1, source_target_pairs={{0,96},{1,97},{2,98},{3,99},{4,100},{5,101},{6,102},{7,103},{8,104... | collective-permute-start | bytes 1572872 | tf_op jit(solution)/shard_map/ppermute | solution.py:42
  143.2 15.9 %collective-permute-start.22 = (f32[4,4,8,1024]{3,2,1,0:T(8,128)S(1)}, f32[4,4,8,1024]{3,2,1,0:T(8,128)S(1)}, u32[]{:S(2)}, u32[]{:S(2)}) collective-permute-start(f32[4,4,8,1024]{3,2,1,0:T(8,128)S(1)} %get-tuple-element.33), channel_id=1, source_target_pairs={{0,32},{1,33},{2,34},{3,35},{4,36},{5,37},{6,38},{7,39},{8,40},{9,... | collective-permute-start | bytes 1572872 | tf_op jit(solution)/shard_map/ppermute | solution.py:42
  148.7 10.0 %collective-permute-start.39 = (f32[1,4,8,1024]{3,2,1,0:T(8,128)S(1)}, f32[1,4,8,1024]{3,2,1,0:T(8,128)S(1)}, u32[]{:S(2)}, u32[]{:S(2)}) collective-permute-start(f32[1,4,8,1024]{3,2,1,0:T(8,128)S(1)} %get-tuple-element.43), channel_id=1, source_target_pairs={{0,64},{1,65},{2,66},{3,67},{4,68},{5,69},{6,70},{7,71},{8,72},{9,... | collective-permute-start | bytes 393224 | tf_op jit(solution)/shard_map/ppermute | solution.py:42
  (9 other events, 21.6 us)

commit v2 on v1

--- a/solution.py
+++ b/solution.py
@@ -93,21 +93,25 @@
     return lax.optimization_barrier((value, *others))[0]
 
 
-def sum_over_plane(groups, weights, earlier):
+def sum_over_plane(groups, weights, earlier, hold):
     width = weights.shape[1]
     rows = jnp.stack(groups, axis=2)
-    terms = jnp.dot(
-        rows.reshape(-1, rows.shape[-1]), weights, preferred_element_type=jnp.float32
-    )
-    terms = (terms * LIFT).astype(jnp.float16).reshape(SIDE, SIDE * len(groups) * ROWS, width)
+    rows = rows.reshape(SIDE, SIDE * len(groups) * ROWS, rows.shape[-1])
+
+    terms = {}
+    for pair in ((1, 3), (2, 0)):
+        value = jnp.concatenate([rows[step] for step in pair], axis=0)
+        value = jnp.dot(value, weights, preferred_element_type=jnp.float32)
+        value = (value * LIFT).astype(jnp.float16).reshape(2, -1, width)
+        terms |= {step: value[i] for i, step in enumerate(pair)}
     came = {}
     for step in (1, 3, 2):
         message = after(terms[step], earlier[step]) if earlier else terms[step]
         came[step] = along_first(message, step)
-    kept = total_of(terms[0], came.values()).reshape(SIDE, len(groups) * ROWS, width)
+    kept = total_of(after(terms[0], hold), came.values()).reshape(SIDE, len(groups) * ROWS, width)
     last = [along_second(kept[step].astype(jnp.float16), step) for step in (2, 1, 3)]
     kept = total_of(kept[0], last) * (1.0 / LIFT)
-    return kept.astype(jnp.bfloat16).reshape(len(groups), ROWS, width), came
+    return kept.astype(jnp.bfloat16).reshape(len(groups), ROWS, width), came, message
 
 
 def attention_kernel(
@@ -118,14 +122,9 @@
     mask_ref,
     k_ref,
     v_ref,
-    _,
-    __,
-    o_ref,
-    nk_ref,
-    nv_ref,
-    queries,
-    results,
+    *refs,
 ):
+    o_ref, nk_ref, nv_ref, queries, results = refs[-5:]
     cosine = cos_ref[...]
     sine = sin_ref[...]
     scale = DH ** (-0.5)
@@ -178,7 +177,7 @@
             ].astype(jnp.bfloat16)
 
 
-def attention(place, packed, cosine, sine, mask, cache_keys, cache_values, keys, values):
+def attention(place, packed, cosine, sine, mask, cache_keys, cache_values, written):
     steps, _, width = packed.shape
     chip = KVH // SIDE * DH
     cache = pl.BlockSpec((ROWS, CACHE, chip), lambda r, place: (0, 0, place[1 + r]))
@@ -198,9 +197,8 @@
                 pl.BlockSpec((ROWS, GROUP, CACHE), lambda r, place: (0, 0, 0)),
                 cache,
                 cache,
-                pl.BlockSpec(memory_space=pl.ANY),
-                pl.BlockSpec(memory_space=pl.ANY),
-            ],
+            ]
+            + [pl.BlockSpec(memory_space=pl.ANY)] * len(written),
             out_specs=(
                 pl.BlockSpec((1, ROWS, chip * GROUP), lambda r, place: (r, 0, 0)),
                 column,
@@ -208,7 +206,7 @@
             ),
             scratch_shapes=[pltpu.VMEM((2, ROWS * GROUP, DH), jnp.float32)] * 2,
         ),
-        input_output_aliases={7: 1, 8: 2},
+        input_output_aliases={7: 1, 8: 2} if written else {},
         compiler_params=pltpu.CompilerParams(vmem_limit_bytes=32 * 2**20),
         cost_estimate=pl.CostEstimate(
             flops=4 * ROWS * HQ * CACHE * DH * steps // SIDE,
@@ -216,7 +214,7 @@
             transcendentals=ROWS * HQ * CACHE * steps // SIDE,
         ),
         name="attention",
-    )(place, packed, cosine, sine, mask, cache_keys, cache_values, keys, values)
+    )(place, packed, cosine, sine, mask, cache_keys, cache_values, *written)
 
 
 def final_kernel(place, *refs):
@@ -251,7 +249,8 @@
     rows = jnp.concatenate([part.reshape(-1, part.shape[-1]) for part in parts], axis=0)
     terms = jnp.dot(rows, w_output, preferred_element_type=jnp.float32)
     terms = terms.reshape(len(parts), SIDE, len(group), ROWS, -1)
-    return [along_x(terms[:, :, i], -dx) if dx else terms[:, :, i] for i, dx in enumerate(group)]
+    sent = [along_x(terms[:, :, i], -dx) if dx else terms[:, :, i] for i, dx in enumerate(group)]
+    return sent, terms
 
 
 def on_device(
@@ -264,11 +263,12 @@
 
     own = order_rows(place, hidden_in)
     hidden = {0: own}
-    for step in (1, 3, 2):
+    for step in (1, 3):
         hidden[step] = along_x(own, step)
+    hidden[2] = along_x(after(own, hidden[1], hidden[3]), 2)
     w_both = jnp.concatenate([w_key, w_value], axis=1)
     pair_query = to_pair(w_query)
-    w_both = jnp.concatenate([w_query, w_both, pair_query, to_pair(w_both)], axis=1)
+    w_in = jnp.concatenate([w_query, w_both, pair_query, to_pair(w_both)], axis=1)
     w_back = jnp.concatenate([w_output, to_pair(after(w_output, pair_query))], axis=0)
 
     angle = positions.astype(jnp.float32)[:, None] * rope_frequencies()[None, :]
@@ -278,39 +278,36 @@
     kept = jnp.arange(CACHE)[None, None, :] < cache_lengths[:, None, None]
     mask = jnp.where(kept, 0.0, -jnp.inf).astype(jnp.float32)
     mask = jnp.broadcast_to(mask, (mask.shape[0], GROUP, CACHE))
-    new_keys = jnp.zeros((ROWS, KVH * DH), jnp.bfloat16)
-    new_values = jnp.zeros((ROWS, KVH * DH), jnp.bfloat16)
+    new = ()
 
     terms = []
-    came = {}
+    came, far, ready, local = {}, {}, w_in, None
     for pieces, group in PIECES:
-        summed, came = sum_over_plane([hidden[dx] for dx in group], w_both, came)
+        rows = [after(hidden[dx], ready) for dx in group]
+        summed, came, ready = sum_over_plane(rows, w_in, came, w_back)
         packed = [along_x(summed[i], -dx) if dx else summed[i] for i, dx in enumerate(group)]
         chips = jnp.stack([core] + [(x + dx) % SIDE for dx in group]).astype(jnp.int32)
-        mixed, new_keys, new_values = attention(
-            chips,
-            jnp.stack(packed),
-            cosine,
-            sine,
-            mask,
-            cache_keys,
-            cache_values,
-            new_keys,
-            new_values,
-        )
+        packed = jnp.stack(packed)
+        mixed, *new = attention(chips, packed, cosine, sine, mask, cache_keys, cache_values, new)
         rows = [along_x(mixed[i], dx) if dx else mixed[i] for i, dx in enumerate(group)]
-        rows = jnp.stack(rows)
+        rows = after(jnp.stack(rows), to_pair(mixed[0, :, :DH]))
         near = {0: rows}
         for step in (2, 1, 3):
             near[step] = along_first(rows, step)
         rows = jnp.stack([near[step] for step in range(SIDE)])
-        far = {0: rows}
+        before, far = far, {0: rows}
         for step in (1, 3, 2):
-            far[step] = along_second(rows, step)
+            message = after(rows, before[step]) if before else rows
+            if local is not None and step == 2:
+                message = after(message, local)
+            far[step] = along_second(message, step)
+        earlier = list(terms)
         for piece in pieces:
-            terms += project([far[step] for step in piece], group, w_back)
+            parts = [after(far[step], *earlier) for step in piece]
+            sent, local = project(parts, group, w_back)
+            terms += sent
     attended = add_up(place, terms)
-    return (attended.reshape(hidden_in.shape), new_keys, new_values)
+    return (attended.reshape(hidden_in.shape), *new)
 
 
 def solution(mesh):

time: 165 us -> 154 us (0.933)
  the two profiles are of different devices: /device:TPU:6 before, /device:TPU:66 now
where the time goes in v2:
time: 154 us
  starting transfers between devices  59.6 us (39%)
  waiting for transfers between devices  51.3 us (33%)
  Pallas kernels  14.5 us (9%)
  matrix products  11.6 us (8%)
  local copies, waits for them, and re-layouts  10.7 us (7%)
  other arithmetic  5.28 us (3%)
    ppermute x40, starting transfers between devices, permute(): return lax.ppermute(value, AXES, pairs)  59.6 us
    ppermute x40, waiting for transfers between devices, permute(): return lax.ppermute(value, AXES, pairs)  51.3 us
    pallas_call x2, Pallas kernels, attention(): pl.pallas_call(attention_kernel, out_shape=(jax.ShapeDtypeStruct((steps,...  10.4 us
    unnamed x31, local copies, waits for them, and re-layouts  7.55 us
    dot_general x3, matrix products, project(): terms = jnp.dot(rows, w_output, preferred_element_type=jnp.float32)  5.88 us
    dot_general x4, matrix products, sum_over_plane(): value = jnp.dot(value, weights, preferred_element_type=jnp.float32)  5.71 us
  transfers between devices with their start and end apart: 40, of which 18 were waited for; matrix products, arithmetic and copies ran while one was open for 15% of the time, Pallas kernels for 8%

profile of v2, /device:TPU:66, one launch (start us, length us, event | category | flops | bytes accessed | tf_op | source)
XLA Modules:
  0.0 154.1 jit_solution(10566789056800387557)
XLA Ops:
  1.4 1.8 %order_rows.1 = bf16[4,4,8,1024]{3,2,1,0:T(8,128)(2,1)} custom-call(s32[3]{0:T(128)} %pad_add_fusion.place, bf16[16,8,1024]{2,1,0:T(8,128)(2,1)} %bitcast.105), custom_call_target="tpu_custom_call" | custom-call | bytes 524288 | tf_op jit(solution)/shard_map/order_rows/pallas_call | solution.py:76
  3.1 1.5 collective-permute-start
  7.4 2.7 %constant_dynamic-update-slice_fusion.4 = bf16[1024,4608]{1,0:T(8,128)(2,1)S(1)} fusion(bf16[1024,2048]{1,0:T(8,128)(2,1)} %param.10), kind=kLoop, calls=%fused_computation.91 | loop fusion | bytes 8388608
  12.0 1.2 collective-permute-done.3
  13.2 2.3 %collective-permute-start.23 = (bf16[4,4,8,1024]{3,2,1,0:T(8,128)(2,1)S(1)}, bf16[4,4,8,1024]{3,2,1,0:T(8,128)(2,1)S(1)}, u32[]{:S(2)}, u32[]{:S(2)}) collective-permute-start(bf16[4,4,8,1024]{3,2,1,0:T(8,128)(2,1)S(1)} %copy-done.1), channel_id=1, source_target_pairs={{0,64},{1,65},{2,66},{3,67},{4,68},{5,69},{6,70},{7,71},{8,72},{9,... | collective-permute-start | bytes 786440 | tf_op jit(solution)/shard_map/ppermute | solution.py:42
  15.6 2.5 %constant_dynamic-update-slice_fusion.1 = bf16[1024,4608]{1,0:T(8,128)(2,1)S(1)} fusion(bf16[1024,4608]{1,0:T(8,128)(2,1)S(1)} %constant_dynamic-update-slice_fusion.2, bf16[1024,2048]{1,0:T(8,128)(2,1)} %collective-permute-done.1), kind=kLoop, calls=%fused_computation.88 | loop fusion | bytes 8388608
  18.3 1.4 fusion.2
  19.9 3.3 %collective-permute-start.7 = (f16[64,4608]{1,0:T(8,128)(2,1)S(1)}, f16[64,4608]{1,0:T(8,128)(2,1)S(1)}, u32[]{:S(2)}, u32[]{:S(2)}) collective-permute-start(f16[64,4608]{1,0:T(8,128)(2,1)S(1)} %get-tuple-element.62), channel_id=1, source_target_pairs={{0,2},{1,3},{2,0},{3,1},{4,6},{5,7},{6,4},{7,5},{8,10},{9,11},{10,... | collective-permute-start | bytes 1769480 | tf_op jit(solution)/shard_map/ppermute | solution.py:42
  23.2 1.4 fusion.3
  24.8 1.1 collective-permute-start.6
  27.1 1.4 fusion.4
  28.5 1.4 fusion.5
  31.4 3.2 %collective-permute-start.26 = (f16[64,4608]{1,0:T(8,128)(2,1)S(1)}, f16[64,4608]{1,0:T(8,128)(2,1)S(1)}, u32[]{:S(2)}, u32[]{:S(2)}) collective-permute-start(f16[64,4608]{1,0:T(8,128)(2,1)S(1)} %get-tuple-element.39), channel_id=1, source_target_pairs={{0,2},{1,3},{2,0},{3,1},{4,6},{5,7},{6,4},{7,5},{8,10},{9,11},{10,... | collective-permute-start | bytes 1769480 | tf_op jit(solution)/shard_map/ppermute | solution.py:42
  34.7 3.4 %collective-permute-done.6 = f16[64,4608]{1,0:T(8,128)(2,1)S(1)} collective-permute-done((f16[64,4608]{1,0:T(8,128)(2,1)S(1)}, f16[64,4608]{1,0:T(8,128)(2,1)S(1)}, u32[]{:S(2)}, u32[]{:S(2)}) %collective-permute-start.6) | collective-permute-done | bytes 589856 | tf_op jit(solution)/shard_map/ppermute | solution.py:42
  38.1 2.6 %collective-permute-start.25 = (f16[64,4608]{1,0:T(8,128)(2,1)S(1)}, f16[64,4608]{1,0:T(8,128)(2,1)}, u32[]{:S(2)}, u32[]{:S(2)}) collective-permute-start(f16[64,4608]{1,0:T(8,128)(2,1)S(1)} %get-tuple-element.38), channel_id=1, source_target_pairs={{0,3},{1,0},{2,1},{3,2},{4,7},{5,4},{6,5},{7,6},{8,11},{9,8},{10,9... | collective-permute-start | bytes 1769480 | tf_op jit(solution)/shard_map/ppermute | solution.py:42
  41.8 1.9 %collective-permute-start.9 = (f16[16,4608]{1,0:T(8,128)(2,1)S(1)}, f16[16,4608]{1,0:T(8,128)(2,1)S(1)}, u32[]{:S(2)}, u32[]{:S(2)}) collective-permute-start(f16[16,4608]{1,0:T(8,128)(2,1)S(1)} %get-tuple-element.74), channel_id=1, source_target_pairs={{0,4},{1,5},{2,6},{3,7},{4,8},{5,9},{6,10},{7,11},{8,12},{9,13},{1... | collective-permute-start | bytes 442376 | tf_op jit(solution)/shard_map/ppermute | solution.py:42
  44.0 1.4 collective-permute-start.8
  45.4 8.6 %collective-permute-done.25 = f16[64,4608]{1,0:T(8,128)(2,1)} collective-permute-done((f16[64,4608]{1,0:T(8,128)(2,1)S(1)}, f16[64,4608]{1,0:T(8,128)(2,1)}, u32[]{:S(2)}, u32[]{:S(2)}) %collective-permute-start.25) | collective-permute-done | bytes 589856 | tf_op jit(solution)/shard_map/ppermute | solution.py:42
  55.1 1.7 %fusion.58 = (f16[64,4608]{1,0:T(8,128)(2,1)S(1)}, f32[64,4608]{1,0:T(8,128)S(1)}) fusion(f16[64,4608]{1,0:T(8,128)(2,1)S(1)} %collective-permute-done.26, f16[64,4608]{1,0:T(8,128)(2,1)} %collective-permute-done.25, f16[64,4608]{1,0:T(8,128)(2,1)} %collective-permute-done.24, f16[64,4608]{1,0:T(8,128)(2,1)S(1)} %get-tuple-element.36), kind=kLoop, calls=%fused_computation.112 | loop fusion | flops 2359296 | bytes 4128768 | tf_op jit(solution)/shard_map/convert.2
  57.0 1.9 %collective-permute-start.28 = (f16[16,4608]{1,0:T(8,128)(2,1)S(1)}, f16[16,4608]{1,0:T(8,128)(2,1)S(1)}, u32[]{:S(2)}, u32[]{:S(2)}) collective-permute-start(f16[16,4608]{1,0:T(8,128)(2,1)S(1)} %get-tuple-element.71), channel_id=1, source_target_pairs={{0,4},{1,5},{2,6},{3,7},{4,8},{5,9},{6,10},{7,11},{8,12},{9,13},{1... | collective-permute-start | bytes 442376 | tf_op jit(solution)/shard_map/ppermute | solution.py:42
  58.9 1.7 %collective-permute-start.27 = (f16[16,4608]{1,0:T(8,128)(2,1)S(1)}, f16[16,4608]{1,0:T(8,128)(2,1)S(1)}, u32[]{:S(2)}, u32[]{:S(2)}) collective-permute-start(f16[16,4608]{1,0:T(8,128)(2,1)S(1)} %get-tuple-element.69), channel_id=1, source_target_pairs={{0,8},{1,9},{2,10},{3,11},{4,12},{5,13},{6,14},{7,15},{8,0},{9,1},... | collective-permute-start | bytes 442376 | tf_op jit(solution)/shard_map/ppermute | solution.py:42
  60.8 2.0 %collective-permute-start.11 = (bf16[8,4608]{1,0:T(8,128)(2,1)S(1)}, bf16[8,4608]{1,0:T(8,128)(2,1)S(1)}, u32[]{:S(2)}, u32[]{:S(2)}) collective-permute-start(bf16[8,4608]{1,0:T(8,128)(2,1)S(1)} %get-tuple-element.87), channel_id=1, source_target_pairs={{0,96},{1,97},{2,98},{3,99},{4,100},{5,101},{6,102},{7,103},{8,104... | collective-permute-start | bytes 221192 | tf_op jit(solution)/shard_map/ppermute | solution.py:42
  62.8 2.8 %collective-permute-done.27 = f16[16,4608]{1,0:T(8,128)(2,1)S(1)} collective-permute-done((f16[16,4608]{1,0:T(8,128)(2,1)S(1)}, f16[16,4608]{1,0:T(8,128)(2,1)S(1)}, u32[]{:S(2)}, u32[]{:S(2)}) %collective-permute-start.27) | collective-permute-done | bytes 147488 | tf_op jit(solution)/shard_map/ppermute | solution.py:42
  65.7 1.3 collective-permute-start.30
  67.1 5.2 %attention.2 = (bf16[2,8,4096]{2,1,0:T(8,128)(2,1)S(1)}, bf16[8,1024]{1,0:T(8,128)(2,1)}, bf16[8,1024]{1,0:T(8,128)(2,1)}) custom-call(s32[3]{0:T(128)S(1)} %pad_add_fusion.1.place, bf16[2,8,4608]{2,1,0:T(8,128)(2,1)S(1)} %pad_maximum_fusion.3.q_ref, f32[8,128]{1,0:T(8,128)S(1)} %get-tuple-element.96.cos_ref, f32[8,128]{1,0:T(8,128)S(1)} %get-tuple-element.97.sin_ref, ...), custom_call_target="tpu_custom_call" | custom-call | flops 117440512 | bytes 7340032 | tf_op jit(solution)/shard_map/attention/pallas_call | solution.py:187
  73.0 1.4 collective-permute-start.13
  74.4 5.2 %attention.3 = (bf16[2,8,4096]{2,1,0:T(8,128)(2,1)S(1)}, bf16[8,1024]{1,0:T(8,128)(2,1)}, bf16[8,1024]{1,0:T(8,128)(2,1)}) custom-call(s32[3]{0:T(128)S(1)} %pad_add_fusion.2.place, bf16[2,8,4608]{2,1,0:T(8,128)(2,1)S(1)} %pad_maximum_fusion.4.q_ref, f32[8,128]{1,0:T(8,128)S(1)} %get-tuple-element.96.cos_ref, ...), custom_call_target="tpu_custom_call", output_to_operand_aliasing={{1}: (7, {}), {2}: (8, {})} | custom-call | flops 117440512 | bytes 7340032 | tf_op jit(solution)/shard_map/attention/pallas_call | solution.py:187
  79.6 4.5 %collective-permute-start.31 = (bf16[8,4096]{1,0:T(8,128)(2,1)S(1)}, bf16[8,4096]{1,0:T(8,128)(2,1)S(1)}, u32[]{:S(2)}, u32[]{:S(2)}) collective-permute-start(bf16[8,4096]{1,0:T(8,128)(2,1)S(1)} %get-tuple-element.90), channel_id=1, source_target_pairs={{0,64},{1,65},{2,66},{3,67},{4,68},{5,69},{6,70},{7,71},{8,72},{9,... | collective-permute-start | bytes 196616 | tf_op jit(solution)/shard_map/ppermute | solution.py:42
  84.1 1.7 %collective-permute-start.17 = (bf16[2,8,4096]{2,1,0:T(8,128)(2,1)S(1)}, bf16[2,8,4096]{2,1,0:T(8,128)(2,1)S(1)}, u32[]{:S(2)}, u32[]{:S(2)}) collective-permute-start(bf16[2,8,4096]{2,1,0:T(8,128)(2,1)S(1)} %pad_maximum_fusion.7), channel_id=1, source_target_pairs={{0,3},{1,0},{2,1},{3,2},{4,7},{5,4},{6,5},{7,6},{8,11},{9,8},{10,9... | collective-permute-start | bytes 393224 | tf_op jit(solution)/shard_map/ppermute | solution.py:42
  87.4 2.5 %collective-permute-start.34 = (bf16[2,8,4096]{2,1,0:T(8,128)(2,1)S(1)}, bf16[2,8,4096]{2,1,0:T(8,128)(2,1)S(1)}, u32[]{:S(2)}, u32[]{:S(2)}) collective-permute-start(bf16[2,8,4096]{2,1,0:T(8,128)(2,1)S(1)} %pad_maximum_fusion.8), channel_id=1, source_target_pairs={{0,3},{1,0},{2,1},{3,2},{4,7},{5,4},{6,5},{7,6},{8,11},{9,8},{10,9... | collective-permute-start | bytes 393224 | tf_op jit(solution)/shard_map/ppermute | solution.py:42
  89.9 1.5 collective-permute-start.33
  92.3 1.3 collective-permute-done.15
  93.7 7.6 %collective-permute-start.20 = (bf16[4,2,8,4096]{3,2,1,0:T(8,128)(2,1)S(1)}, bf16[4,2,8,4096]{3,2,1,0:T(8,128)(2,1)S(1)}, u32[]{:S(2)}, u32[]{:S(2)}) collective-permute-start(bf16[4,2,8,4096]{3,2,1,0:T(8,128)(2,1)S(1)} %pad_maximum_fusion.1), channel_id=1, source_target_pairs={{0,12},{1,13},{2,14},{3,15},{4,0},{5,1},{6,2},{7,3},{8,4},{9,5},{1... | collective-permute-start | bytes 1572872 | tf_op jit(solution)/shard_map/ppermute | solution.py:42
  101.3 2.2 %collective-permute-start.18 = (bf16[4,2,8,4096]{3,2,1,0:T(8,128)(2,1)S(1)}, bf16[4,2,8,4096]{3,2,1,0:T(8,128)(2,1)S(1)}, u32[]{:S(2)}, u32[]{:S(2)}) collective-permute-start(bf16[4,2,8,4096]{3,2,1,0:T(8,128)(2,1)S(1)} %pad_maximum_fusion.1), channel_id=1, source_target_pairs={{0,4},{1,5},{2,6},{3,7},{4,8},{5,9},{6,10},{7,11},{8,12},{9,13},{1... | collective-permute-start | bytes 1572872 | tf_op jit(solution)/shard_map/ppermute | solution.py:42
  104.3 9.3 %collective-permute-done.20 = bf16[4,2,8,4096]{3,2,1,0:T(8,128)(2,1)S(1)} collective-permute-done((bf16[4,2,8,4096]{3,2,1,0:T(8,128)(2,1)S(1)}, bf16[4,2,8,4096]{3,2,1,0:T(8,128)(2,1)S(1)}, u32[]{:S(2)}, u32[]{:S(2)}) %collective-permute-start.20) | collective-permute-done | bytes 524320 | tf_op jit(solution)/shard_map/ppermute | solution.py:42
  113.6 2.5 %collective-permute-done.18 = bf16[4,2,8,4096]{3,2,1,0:T(8,128)(2,1)S(1)} collective-permute-done((bf16[4,2,8,4096]{3,2,1,0:T(8,128)(2,1)S(1)}, bf16[4,2,8,4096]{3,2,1,0:T(8,128)(2,1)S(1)}, u32[]{:S(2)}, u32[]{:S(2)}) %collective-permute-start.18) | collective-permute-done | bytes 524320 | tf_op jit(solution)/shard_map/ppermute | solution.py:42
  116.1 2.4 %fusion.6 = f32[256,1024]{1,0:T(8,128)S(1)} fusion(bf16[4096,1024]{1,0:T(8,128)(2,1)S(1)} %constant_dynamic-update-slice_fusion.5, bf16[64,4096]{1,0:T(8,128)(2,1)S(1)} %bitcast.121, bf16[64,4096]{1,0:T(8,128)(2,1)S(1)} %bitcast.122, bf16[64,4096]{1,0:T(8,128)(2,1)S(1)} %bitcast.123, bf16[64,4096]{1,0:T(8,128)(2,1)S(1)} %bitcast.101), kind=kOutput, calls=%fused_computation.10 | convolution fusion | flops 2155872256 | bytes 11534336 | tf_op jit(solution)/shard_map/dot_general | solution.py:250
  118.7 2.0 %collective-permute-start.22 = (f32[4,4,8,1024]{3,2,1,0:T(8,128)S(1)}, f32[4,4,8,1024]{3,2,1,0:T(8,128)S(1)}, u32[]{:S(2)}, u32[]{:S(2)}) collective-permute-start(f32[4,4,8,1024]{3,2,1,0:T(8,128)S(1)} %get-tuple-element.65), channel_id=1, source_target_pairs={{0,32},{1,33},{2,34},{3,35},{4,36},{5,37},{6,38},{7,39},{8,40},{9,... | collective-permute-start | bytes 1572872 | tf_op jit(solution)/shard_map/ppermute | solution.py:42
  120.7 2.1 %collective-permute-start.36 = (bf16[4,2,8,4096]{3,2,1,0:T(8,128)(2,1)S(1)}, bf16[4,2,8,4096]{3,2,1,0:T(8,128)(2,1)S(1)}, u32[]{:S(2)}, u32[]{:S(2)}) collective-permute-start(bf16[4,2,8,4096]{3,2,1,0:T(8,128)(2,1)S(1)} %pad_maximum_fusion.2), channel_id=1, source_target_pairs={{0,12},{1,13},{2,14},{3,15},{4,0},{5,1},{6,2},{7,3},{8,4},{9,5},{1... | collective-permute-start | bytes 1572872 | tf_op jit(solution)/shard_map/ppermute | solution.py:42
  122.8 1.5 collective-permute-start.38
  124.3 3.6 %collective-permute-done.21.refs_0_ = f32[4,4,8,1024]{3,2,1,0:T(8,128)S(1)} collective-permute-done((f32[4,4,8,1024]{3,2,1,0:T(8,128)S(1)}, f32[4,4,8,1024]{3,2,1,0:T(8,128)S(1)}, u32[]{:S(2)}, u32[]{:S(2)}) %collective-permute-start.21) | collective-permute-done | bytes 524320 | tf_op jit(solution)/shard_map/ppermute | solution.py:42
  127.9 7.2 %collective-permute-done.36 = bf16[4,2,8,4096]{3,2,1,0:T(8,128)(2,1)S(1)} collective-permute-done((bf16[4,2,8,4096]{3,2,1,0:T(8,128)(2,1)S(1)}, bf16[4,2,8,4096]{3,2,1,0:T(8,128)(2,1)S(1)}, u32[]{:S(2)}, u32[]{:S(2)}) %collective-permute-start.36) | collective-permute-done | bytes 524320 | tf_op jit(solution)/shard_map/ppermute | solution.py:42
  135.1 2.4 %collective-permute-done.35 = bf16[4,2,8,4096]{3,2,1,0:T(8,128)(2,1)S(1)} collective-permute-done((bf16[4,2,8,4096]{3,2,1,0:T(8,128)(2,1)S(1)}, bf16[4,2,8,4096]{3,2,1,0:T(8,128)(2,1)S(1)}, u32[]{:S(2)}, u32[]{:S(2)}) %collective-permute-start.35) | collective-permute-done | bytes 524320 | tf_op jit(solution)/shard_map/ppermute | solution.py:42
  137.6 1.9 %fusion.14 = f32[192,1024]{1,0:T(8,128)S(1)} fusion(bf16[4096,1024]{1,0:T(8,128)(2,1)S(1)} %constant_dynamic-update-slice_fusion.5, bf16[64,4096]{1,0:T(8,128)(2,1)S(1)} %bitcast.124, bf16[64,4096]{1,0:T(8,128)(2,1)S(1)} %bitcast.125, bf16[64,4096]{1,0:T(8,128)(2,1)S(1)} %bitcast.100), kind=kOutput, calls=%fused_computation.18 | convolution fusion | flops 1615331328 | bytes 10747904 | tf_op jit(solution)/shard_map/dot_general | solution.py:250
  140.3 1.6 %fusion.20 = f32[1,4,2,8,1024]{4,3,1,2,0:T(8,128)S(1)} fusion(bf16[4096,1024]{1,0:T(8,128)(2,1)S(1)} %constant_dynamic-update-slice_fusion.5, bf16[4,2,8,4096]{3,2,1,0:T(8,128)(2,1)S(1)} %collective-permute-done.38), kind=kOutput, calls=%fused_computation.26 | convolution fusion | flops 536870912 | bytes 9175040 | tf_op jit(solution)/shard_map/dot_general | solution.py:250
  142.6 3.5 %collective-permute-start.39 = (f32[1,4,8,1024]{3,2,1,0:T(8,128)S(1)}, f32[1,4,8,1024]{3,2,1,0:T(8,128)S(1)}, u32[]{:S(2)}, u32[]{:S(2)}) collective-permute-start(f32[1,4,8,1024]{3,2,1,0:T(8,128)S(1)} %get-tuple-element.83), channel_id=1, source_target_pairs={{0,64},{1,65},{2,66},{3,67},{4,68},{5,69},{6,70},{7,71},{8,72},{9,... | collective-permute-start | bytes 393224 | tf_op jit(solution)/shard_map/ppermute | solution.py:42
  146.1 4.9 %collective-permute-done.39.refs_5_ = f32[1,4,8,1024]{3,2,1,0:T(8,128)S(1)} collective-permute-done((f32[1,4,8,1024]{3,2,1,0:T(8,128)S(1)}, f32[1,4,8,1024]{3,2,1,0:T(8,128)S(1)}, u32[]{:S(2)}, u32[]{:S(2)}) %collective-permute-start.39) | collective-permute-done | bytes 131104 | tf_op jit(solution)/shard_map/ppermute | solution.py:42
  151.8 2.3 %add_up.1 = bf16[16,8,1024]{2,1,0:T(8,128)(2,1)} custom-call(s32[3]{0:T(128)} %pad_add_fusion.place, f32[4,4,8,1024]{3,2,1,0:T(8,128)} %copy-done.4, f32[4,4,8,1024]{3,2,1,0:T(8,128)} %copy-done.5, f32[3,4,8,1024]{3,2,1,0:T(8,128)} %get-tuple-element.68.refs_2_, f32[3,4,8,1024]{3,2,1,0:T(8,128)} %copy-done.6, f32[1,4,8,1024]{3,2,1,0:T(8,128)} %get-tuple-element.84.refs_4_, ...), custom_call_target="tpu_custom_call" | custom-call | flops 524288 | bytes 2097152 | tf_op jit(solution)/shard_map/add_up/pallas_call | solution.py:237
  (121 shorter events, 18.0 us)
Async XLA Ops:
  0.6 14.9 %collective-permute-start.1 = (bf16[1024,2048]{1,0:T(8,128)(2,1)}, bf16[1024,2048]{1,0:T(8,128)(2,1)}, u32[]{:S(2)}, u32[]{:S(2)}) collective-permute-start(bf16[1024,2048]{1,0:T(8,128)(2,1)} %param.10), channel_id=1, source_target_pairs={{0,16},{1,17},{2,18},{3,19},{4,20},{5,21},{6,22},{7,23},{8,24},{9,... | collective-permute-start | bytes 12582920 | tf_op jit(solution)/shard_map/ppermute | solution.py:42
  3.1 8.9 %collective-permute-start = (bf16[4,4,8,1024]{3,2,1,0:T(8,128)(2,1)}, bf16[4,4,8,1024]{3,2,1,0:T(8,128)(2,1)S(1)}, u32[]{:S(2)}, u32[]{:S(2)}) collective-permute-start(bf16[4,4,8,1024]{3,2,1,0:T(8,128)(2,1)} %order_rows.1), channel_id=1, source_target_pairs={{0,32},{1,33},{2,34},{3,35},{4,36},{5,37},{6,38},{7,39},{8,40},{9,... | collective-permute-start | bytes 786440 | tf_op jit(solution)/shard_map/ppermute | solution.py:42
  4.6 8.6 %collective-permute-start.3 = (bf16[4,4,8,1024]{3,2,1,0:T(8,128)(2,1)}, bf16[4,4,8,1024]{3,2,1,0:T(8,128)(2,1)S(1)}, u32[]{:S(2)}, u32[]{:S(2)}) collective-permute-start(bf16[4,4,8,1024]{3,2,1,0:T(8,128)(2,1)} %order_rows.1), channel_id=1, source_target_pairs={{0,96},{1,97},{2,98},{3,99},{4,100},{5,101},{6,102},{7,103},{8,104... | collective-permute-start | bytes 786440 | tf_op jit(solution)/shard_map/ppermute | solution.py:42
  6.2 11.9 %collective-permute-start.2 = (bf16[1024,256]{1,0:T(8,128)(2,1)S(1)}, bf16[1024,256]{1,0:T(8,128)(2,1)S(1)}, u32[]{:S(2)}, u32[]{:S(2)}) collective-permute-start(bf16[1024,256]{1,0:T(8,128)(2,1)S(1)} %pad_maximum_fusion), channel_id=1, source_target_pairs={{0,16},{1,17},{2,18},{3,19},{4,20},{5,21},{6,22},{7,23},{8,24},{9,... | collective-permute-start | bytes 1572872 | tf_op jit(solution)/shard_map/ppermute | solution.py:42
  7.4 2.8 %copy-start.3 = (bf16[1024,128]{1,0:T(8,128)(2,1)S(1)}, bf16[1024,128]{1,0:T(8,128)(2,1)}, u32[]{:S(2)}) copy-start(bf16[1024,128]{1,0:T(8,128)(2,1)} %param.12) | copy-start | bytes 786436
  7.4 3.6 %copy-start = (bf16[2048,1024]{1,0:T(8,128)(2,1)S(1)}, bf16[2048,1024]{1,0:T(8,128)(2,1)}, u32[]{:S(2)}) copy-start(bf16[2048,1024]{1,0:T(8,128)(2,1)} %param.13) | copy-start | bytes 12582916
  13.2 13.7 %collective-permute-start.23 = (bf16[4,4,8,1024]{3,2,1,0:T(8,128)(2,1)S(1)}, bf16[4,4,8,1024]{3,2,1,0:T(8,128)(2,1)S(1)}, u32[]{:S(2)}, u32[]{:S(2)}) collective-permute-start(bf16[4,4,8,1024]{3,2,1,0:T(8,128)(2,1)S(1)} %copy-done.1), channel_id=1, source_target_pairs={{0,64},{1,65},{2,66},{3,67},{4,68},{5,69},{6,70},{7,71},{8,72},{9,... | collective-permute-start | bytes 786440 | tf_op jit(solution)/shard_map/ppermute | solution.py:42
  15.5 25.2 %collective-permute-start.4 = (bf16[2048,1024]{1,0:T(8,128)(2,1)S(1)}, bf16[2048,1024]{1,0:T(8,128)(2,1)S(1)}, u32[]{:S(2)}, u32[]{:S(2)}) collective-permute-start(bf16[2048,1024]{1,0:T(8,128)(2,1)S(1)} %copy-done), channel_id=1, source_target_pairs={{0,16},{1,17},{2,18},{3,19},{4,20},{5,21},{6,22},{7,23},{8,24},{9,... | collective-permute-start | bytes 12582920 | tf_op jit(solution)/shard_map/ppermute | solution.py:42
  19.9 11.5 %collective-permute-start.7 = (f16[64,4608]{1,0:T(8,128)(2,1)S(1)}, f16[64,4608]{1,0:T(8,128)(2,1)S(1)}, u32[]{:S(2)}, u32[]{:S(2)}) collective-permute-start(f16[64,4608]{1,0:T(8,128)(2,1)S(1)} %get-tuple-element.62), channel_id=1, source_target_pairs={{0,2},{1,3},{2,0},{3,1},{4,6},{5,7},{6,4},{7,5},{8,10},{9,11},{10,... | collective-permute-start | bytes 1769480 | tf_op jit(solution)/shard_map/ppermute | solution.py:42
  24.8 13.2 %collective-permute-start.6 = (f16[64,4608]{1,0:T(8,128)(2,1)S(1)}, f16[64,4608]{1,0:T(8,128)(2,1)S(1)}, u32[]{:S(2)}, u32[]{:S(2)}) collective-permute-start(f16[64,4608]{1,0:T(8,128)(2,1)S(1)} %get-tuple-element.64), channel_id=1, source_target_pairs={{0,3},{1,0},{2,1},{3,2},{4,7},{5,4},{6,5},{7,6},{8,11},{9,8},{10,9... | collective-permute-start | bytes 1769480 | tf_op jit(solution)/shard_map/ppermute | solution.py:42
  26.0 14.7 %collective-permute-start.5 = (f16[64,4608]{1,0:T(8,128)(2,1)S(1)}, f16[64,4608]{1,0:T(8,128)(2,1)S(1)}, u32[]{:S(2)}, u32[]{:S(2)}) collective-permute-start(f16[64,4608]{1,0:T(8,128)(2,1)S(1)} %get-tuple-element.63), channel_id=1, source_target_pairs={{0,1},{1,2},{2,3},{3,0},{4,5},{5,6},{6,7},{7,4},{8,9},{9,10},{10,1... | collective-permute-start | bytes 1769480 | tf_op jit(solution)/shard_map/ppermute | solution.py:42
  31.4 12.6 %collective-permute-start.26 = (f16[64,4608]{1,0:T(8,128)(2,1)S(1)}, f16[64,4608]{1,0:T(8,128)(2,1)S(1)}, u32[]{:S(2)}, u32[]{:S(2)}) collective-permute-start(f16[64,4608]{1,0:T(8,128)(2,1)S(1)} %get-tuple-element.39), channel_id=1, source_target_pairs={{0,2},{1,3},{2,0},{3,1},{4,6},{5,7},{6,4},{7,5},{8,10},{9,11},{10,... | collective-permute-start | bytes 1769480 | tf_op jit(solution)/shard_map/ppermute | solution.py:42
  38.1 15.9 %collective-permute-start.25 = (f16[64,4608]{1,0:T(8,128)(2,1)S(1)}, f16[64,4608]{1,0:T(8,128)(2,1)}, u32[]{:S(2)}, u32[]{:S(2)}) collective-permute-start(f16[64,4608]{1,0:T(8,128)(2,1)S(1)} %get-tuple-element.38), channel_id=1, source_target_pairs={{0,3},{1,0},{2,1},{3,2},{4,7},{5,4},{6,5},{7,6},{8,11},{9,8},{10,9... | collective-permute-start | bytes 1769480 | tf_op jit(solution)/shard_map/ppermute | solution.py:42
  40.7 14.4 %collective-permute-start.24 = (f16[64,4608]{1,0:T(8,128)(2,1)S(1)}, f16[64,4608]{1,0:T(8,128)(2,1)}, u32[]{:S(2)}, u32[]{:S(2)}) collective-permute-start(f16[64,4608]{1,0:T(8,128)(2,1)S(1)} %get-tuple-element.37), channel_id=1, source_target_pairs={{0,1},{1,2},{2,3},{3,0},{4,5},{5,6},{6,7},{7,4},{8,9},{9,10},{10,1... | collective-permute-start | bytes 1769480 | tf_op jit(solution)/shard_map/ppermute | solution.py:42
  40.7 26.3 %slice-start = ((s8[7340032]{0:T(1024)(128)(4,1)}), s8[4194304]{0:T(1024)(128)(4,1)S(1)}, s32[]{:S(2)}) async-start(s8[7340032]{0:T(1024)(128)(4,1)} %bitcast.85), calls=%async_computation | async-start | bytes 8388608
  40.7 26.3 %slice-start.2 = ((s8[7340032]{0:T(1024)(128)(4,1)}), s8[4194304]{0:T(1024)(128)(4,1)S(1)}, s32[]{:S(2)}) async-start(s8[7340032]{0:T(1024)(128)(4,1)} %bitcast.87), calls=%async_computation.2 | async-start | bytes 8388608
  41.2 25.9 %slice-start.1 = ((s8[7340032]{0:T(1024)(128)(4,1)}), s8[3145728]{0:T(1024)(128)(4,1)S(1)}, s32[]{:S(2)}) async-start(s8[7340032]{0:T(1024)(128)(4,1)} %bitcast.85), calls=%async_computation.1 | async-start | bytes 6291456
  41.2 25.9 %slice-start.3 = ((s8[7340032]{0:T(1024)(128)(4,1)}), s8[3145728]{0:T(1024)(128)(4,1)S(1)}, s32[]{:S(2)}) async-start(s8[7340032]{0:T(1024)(128)(4,1)} %bitcast.87), calls=%async_computation.3 | async-start | bytes 6291456
  41.6 17.3 %collective-permute-start.10 = (f16[16,4608]{1,0:T(8,128)(2,1)S(1)}, f16[16,4608]{1,0:T(8,128)(2,1)S(1)}, u32[]{:S(2)}, u32[]{:S(2)}) collective-permute-start(f16[16,4608]{1,0:T(8,128)(2,1)S(1)} %get-tuple-element.73), channel_id=1, source_target_pairs={{0,12},{1,13},{2,14},{3,15},{4,0},{5,1},{6,2},{7,3},{8,4},{9,5},{1... | collective-permute-start | bytes 442376 | tf_op jit(solution)/shard_map/ppermute | solution.py:42
  41.8 18.8 %collective-permute-start.9 = (f16[16,4608]{1,0:T(8,128)(2,1)S(1)}, f16[16,4608]{1,0:T(8,128)(2,1)S(1)}, u32[]{:S(2)}, u32[]{:S(2)}) collective-permute-start(f16[16,4608]{1,0:T(8,128)(2,1)S(1)} %get-tuple-element.74), channel_id=1, source_target_pairs={{0,4},{1,5},{2,6},{3,7},{4,8},{5,9},{6,10},{7,11},{8,12},{9,13},{1... | collective-permute-start | bytes 442376 | tf_op jit(solution)/shard_map/ppermute | solution.py:42
  44.0 16.6 %collective-permute-start.8 = (f16[16,4608]{1,0:T(8,128)(2,1)S(1)}, f16[16,4608]{1,0:T(8,128)(2,1)S(1)}, u32[]{:S(2)}, u32[]{:S(2)}) collective-permute-start(f16[16,4608]{1,0:T(8,128)(2,1)S(1)} %get-tuple-element.72), channel_id=1, source_target_pairs={{0,8},{1,9},{2,10},{3,11},{4,12},{5,13},{6,14},{7,15},{8,0},{9,1},... | collective-permute-start | bytes 442376 | tf_op jit(solution)/shard_map/ppermute | solution.py:42
  56.8 6.0 %collective-permute-start.29 = (f16[16,4608]{1,0:T(8,128)(2,1)S(1)}, f16[16,4608]{1,0:T(8,128)(2,1)S(1)}, u32[]{:S(2)}, u32[]{:S(2)}) collective-permute-start(f16[16,4608]{1,0:T(8,128)(2,1)S(1)} %get-tuple-element.70), channel_id=1, source_target_pairs={{0,12},{1,13},{2,14},{3,15},{4,0},{5,1},{6,2},{7,3},{8,4},{9,5},{1... | collective-permute-start | bytes 442376 | tf_op jit(solution)/shard_map/ppermute | solution.py:42
  57.0 5.8 %collective-permute-start.28 = (f16[16,4608]{1,0:T(8,128)(2,1)S(1)}, f16[16,4608]{1,0:T(8,128)(2,1)S(1)}, u32[]{:S(2)}, u32[]{:S(2)}) collective-permute-start(f16[16,4608]{1,0:T(8,128)(2,1)S(1)} %get-tuple-element.71), channel_id=1, source_target_pairs={{0,4},{1,5},{2,6},{3,7},{4,8},{5,9},{6,10},{7,11},{8,12},{9,13},{1... | collective-permute-start | bytes 442376 | tf_op jit(solution)/shard_map/ppermute | solution.py:42
  58.9 6.6 %collective-permute-start.27 = (f16[16,4608]{1,0:T(8,128)(2,1)S(1)}, f16[16,4608]{1,0:T(8,128)(2,1)S(1)}, u32[]{:S(2)}, u32[]{:S(2)}) collective-permute-start(f16[16,4608]{1,0:T(8,128)(2,1)S(1)} %get-tuple-element.69), channel_id=1, source_target_pairs={{0,8},{1,9},{2,10},{3,11},{4,12},{5,13},{6,14},{7,15},{8,0},{9,1},... | collective-permute-start | bytes 442376 | tf_op jit(solution)/shard_map/ppermute | solution.py:42
  60.7 6.3 %collective-permute-start.12 = (bf16[8,4608]{1,0:T(8,128)(2,1)S(1)}, bf16[8,4608]{1,0:T(8,128)(2,1)S(1)}, u32[]{:S(2)}, u32[]{:S(2)}) collective-permute-start(bf16[8,4608]{1,0:T(8,128)(2,1)S(1)} %get-tuple-element.88), channel_id=1, source_target_pairs={{0,32},{1,33},{2,34},{3,35},{4,36},{5,37},{6,38},{7,39},{8,40},{9,... | collective-permute-start | bytes 221192 | tf_op jit(solution)/shard_map/ppermute | solution.py:42
  60.8 6.2 %collective-permute-start.11 = (bf16[8,4608]{1,0:T(8,128)(2,1)S(1)}, bf16[8,4608]{1,0:T(8,128)(2,1)S(1)}, u32[]{:S(2)}, u32[]{:S(2)}) collective-permute-start(bf16[8,4608]{1,0:T(8,128)(2,1)S(1)} %get-tuple-element.87), channel_id=1, source_target_pairs={{0,96},{1,97},{2,98},{3,99},{4,100},{5,101},{6,102},{7,103},{8,104... | collective-permute-start | bytes 221192 | tf_op jit(solution)/shard_map/ppermute | solution.py:42
  65.7 8.7 %collective-permute-start.30 = (bf16[8,4608]{1,0:T(8,128)(2,1)S(1)}, bf16[8,4608]{1,0:T(8,128)(2,1)S(1)}, u32[]{:S(2)}, u32[]{:S(2)}) collective-permute-start(bf16[8,4608]{1,0:T(8,128)(2,1)S(1)} %get-tuple-element.86), channel_id=1, source_target_pairs={{0,64},{1,65},{2,66},{3,67},{4,68},{5,69},{6,70},{7,71},{8,72},{9,... | collective-permute-start | bytes 221192 | tf_op jit(solution)/shard_map/ppermute | solution.py:42
  72.3 11.8 %collective-permute-start.14 = (bf16[8,4096]{1,0:T(8,128)(2,1)S(1)}, bf16[8,4096]{1,0:T(8,128)(2,1)S(1)}, u32[]{:S(2)}, u32[]{:S(2)}) collective-permute-start(bf16[8,4096]{1,0:T(8,128)(2,1)S(1)} %get-tuple-element.92), channel_id=1, source_target_pairs={{0,96},{1,97},{2,98},{3,99},{4,100},{5,101},{6,102},{7,103},{8,104... | collective-permute-start | bytes 196616 | tf_op jit(solution)/shard_map/ppermute | solution.py:42
  73.0 11.1 %collective-permute-start.13 = (bf16[8,4096]{1,0:T(8,128)(2,1)S(1)}, bf16[8,4096]{1,0:T(8,128)(2,1)S(1)}, u32[]{:S(2)}, u32[]{:S(2)}) collective-permute-start(bf16[8,4096]{1,0:T(8,128)(2,1)S(1)} %get-tuple-element.91), channel_id=1, source_target_pairs={{0,32},{1,33},{2,34},{3,35},{4,36},{5,37},{6,38},{7,39},{8,40},{9,... | collective-permute-start | bytes 196616 | tf_op jit(solution)/shard_map/ppermute | solution.py:42
  79.6 7.7 %collective-permute-start.31 = (bf16[8,4096]{1,0:T(8,128)(2,1)S(1)}, bf16[8,4096]{1,0:T(8,128)(2,1)S(1)}, u32[]{:S(2)}, u32[]{:S(2)}) collective-permute-start(bf16[8,4096]{1,0:T(8,128)(2,1)S(1)} %get-tuple-element.90), channel_id=1, source_target_pairs={{0,64},{1,65},{2,66},{3,67},{4,68},{5,69},{6,70},{7,71},{8,72},{9,... | collective-permute-start | bytes 196616 | tf_op jit(solution)/shard_map/ppermute | solution.py:42
  84.1 7.3 %collective-permute-start.17 = (bf16[2,8,4096]{2,1,0:T(8,128)(2,1)S(1)}, bf16[2,8,4096]{2,1,0:T(8,128)(2,1)S(1)}, u32[]{:S(2)}, u32[]{:S(2)}) collective-permute-start(bf16[2,8,4096]{2,1,0:T(8,128)(2,1)S(1)} %pad_maximum_fusion.7), channel_id=1, source_target_pairs={{0,3},{1,0},{2,1},{3,2},{4,7},{5,4},{6,5},{7,6},{8,11},{9,8},{10,9... | collective-permute-start | bytes 393224 | tf_op jit(solution)/shard_map/ppermute | solution.py:42
  85.8 6.6 %collective-permute-start.16 = (bf16[2,8,4096]{2,1,0:T(8,128)(2,1)S(1)}, bf16[2,8,4096]{2,1,0:T(8,128)(2,1)S(1)}, u32[]{:S(2)}, u32[]{:S(2)}) collective-permute-start(bf16[2,8,4096]{2,1,0:T(8,128)(2,1)S(1)} %pad_maximum_fusion.7), channel_id=1, source_target_pairs={{0,2},{1,3},{2,0},{3,1},{4,6},{5,7},{6,4},{7,5},{8,10},{9,11},{10,... | collective-permute-start | bytes 393224 | tf_op jit(solution)/shard_map/ppermute | solution.py:42
  86.6 7.1 %collective-permute-start.15 = (bf16[2,8,4096]{2,1,0:T(8,128)(2,1)S(1)}, bf16[2,8,4096]{2,1,0:T(8,128)(2,1)S(1)}, u32[]{:S(2)}, u32[]{:S(2)}) collective-permute-start(bf16[2,8,4096]{2,1,0:T(8,128)(2,1)S(1)} %pad_maximum_fusion.7), channel_id=1, source_target_pairs={{0,1},{1,2},{2,3},{3,0},{4,5},{5,6},{6,7},{7,4},{8,9},{9,10},{10,1... | collective-permute-start | bytes 393224 | tf_op jit(solution)/shard_map/ppermute | solution.py:42
  87.4 13.9 %collective-permute-start.34 = (bf16[2,8,4096]{2,1,0:T(8,128)(2,1)S(1)}, bf16[2,8,4096]{2,1,0:T(8,128)(2,1)S(1)}, u32[]{:S(2)}, u32[]{:S(2)}) collective-permute-start(bf16[2,8,4096]{2,1,0:T(8,128)(2,1)S(1)} %pad_maximum_fusion.8), channel_id=1, source_target_pairs={{0,3},{1,0},{2,1},{3,2},{4,7},{5,4},{6,5},{7,6},{8,11},{9,8},{10,9... | collective-permute-start | bytes 393224 | tf_op jit(solution)/shard_map/ppermute | solution.py:42
  89.9 13.6 %collective-permute-start.33 = (bf16[2,8,4096]{2,1,0:T(8,128)(2,1)S(1)}, bf16[2,8,4096]{2,1,0:T(8,128)(2,1)S(1)}, u32[]{:S(2)}, u32[]{:S(2)}) collective-permute-start(bf16[2,8,4096]{2,1,0:T(8,128)(2,1)S(1)} %pad_maximum_fusion.8), channel_id=1, source_target_pairs={{0,2},{1,3},{2,0},{3,1},{4,6},{5,7},{6,4},{7,5},{8,10},{9,11},{10,... | collective-permute-start | bytes 393224 | tf_op jit(solution)/shard_map/ppermute | solution.py:42
  91.4 12.8 %collective-permute-start.32 = (bf16[2,8,4096]{2,1,0:T(8,128)(2,1)S(1)}, bf16[2,8,4096]{2,1,0:T(8,128)(2,1)S(1)}, u32[]{:S(2)}, u32[]{:S(2)}) collective-permute-start(bf16[2,8,4096]{2,1,0:T(8,128)(2,1)S(1)} %pad_maximum_fusion.8), channel_id=1, source_target_pairs={{0,1},{1,2},{2,3},{3,0},{4,5},{5,6},{6,7},{7,4},{8,9},{9,10},{10,1... | collective-permute-start | bytes 393224 | tf_op jit(solution)/shard_map/ppermute | solution.py:42
  93.7 19.9 %collective-permute-start.20 = (bf16[4,2,8,4096]{3,2,1,0:T(8,128)(2,1)S(1)}, bf16[4,2,8,4096]{3,2,1,0:T(8,128)(2,1)S(1)}, u32[]{:S(2)}, u32[]{:S(2)}) collective-permute-start(bf16[4,2,8,4096]{3,2,1,0:T(8,128)(2,1)S(1)} %pad_maximum_fusion.1), channel_id=1, source_target_pairs={{0,12},{1,13},{2,14},{3,15},{4,0},{5,1},{6,2},{7,3},{8,4},{9,5},{1... | collective-permute-start | bytes 1572872 | tf_op jit(solution)/shard_map/ppermute | solution.py:42
  101.3 12.3 %collective-permute-start.19 = (bf16[4,2,8,4096]{3,2,1,0:T(8,128)(2,1)S(1)}, bf16[4,2,8,4096]{3,2,1,0:T(8,128)(2,1)S(1)}, u32[]{:S(2)}, u32[]{:S(2)}) collective-permute-start(bf16[4,2,8,4096]{3,2,1,0:T(8,128)(2,1)S(1)} %pad_maximum_fusion.1), channel_id=1, source_target_pairs={{0,8},{1,9},{2,10},{3,11},{4,12},{5,13},{6,14},{7,15},{8,0},{9,1},... | collective-permute-start | bytes 1572872 | tf_op jit(solution)/shard_map/ppermute | solution.py:42
  101.3 14.8 %collective-permute-start.18 = (bf16[4,2,8,4096]{3,2,1,0:T(8,128)(2,1)S(1)}, bf16[4,2,8,4096]{3,2,1,0:T(8,128)(2,1)S(1)}, u32[]{:S(2)}, u32[]{:S(2)}) collective-permute-start(bf16[4,2,8,4096]{3,2,1,0:T(8,128)(2,1)S(1)} %pad_maximum_fusion.1), channel_id=1, source_target_pairs={{0,4},{1,5},{2,6},{3,7},{4,8},{5,9},{6,10},{7,11},{8,12},{9,13},{1... | collective-permute-start | bytes 1572872 | tf_op jit(solution)/shard_map/ppermute | solution.py:42
  118.6 9.3 %collective-permute-start.21 = (f32[4,4,8,1024]{3,2,1,0:T(8,128)S(1)}, f32[4,4,8,1024]{3,2,1,0:T(8,128)S(1)}, u32[]{:S(2)}, u32[]{:S(2)}) collective-permute-start(f32[4,4,8,1024]{3,2,1,0:T(8,128)S(1)} %get-tuple-element.66), channel_id=1, source_target_pairs={{0,96},{1,97},{2,98},{3,99},{4,100},{5,101},{6,102},{7,103},{8,104... | collective-permute-start | bytes 1572872 | tf_op jit(solution)/shard_map/ppermute | solution.py:42
  118.7 9.3 %collective-permute-start.22 = (f32[4,4,8,1024]{3,2,1,0:T(8,128)S(1)}, f32[4,4,8,1024]{3,2,1,0:T(8,128)S(1)}, u32[]{:S(2)}, u32[]{:S(2)}) collective-permute-start(f32[4,4,8,1024]{3,2,1,0:T(8,128)S(1)} %get-tuple-element.65), channel_id=1, source_target_pairs={{0,32},{1,33},{2,34},{3,35},{4,36},{5,37},{6,38},{7,39},{8,40},{9,... | collective-permute-start | bytes 1572872 | tf_op jit(solution)/shard_map/ppermute | solution.py:42
  120.7 14.5 %collective-permute-start.36 = (bf16[4,2,8,4096]{3,2,1,0:T(8,128)(2,1)S(1)}, bf16[4,2,8,4096]{3,2,1,0:T(8,128)(2,1)S(1)}, u32[]{:S(2)}, u32[]{:S(2)}) collective-permute-start(bf16[4,2,8,4096]{3,2,1,0:T(8,128)(2,1)S(1)} %pad_maximum_fusion.2), channel_id=1, source_target_pairs={{0,12},{1,13},{2,14},{3,15},{4,0},{5,1},{6,2},{7,3},{8,4},{9,5},{1... | collective-permute-start | bytes 1572872 | tf_op jit(solution)/shard_map/ppermute | solution.py:42
  122.8 14.8 %collective-permute-start.35 = (bf16[4,2,8,4096]{3,2,1,0:T(8,128)(2,1)S(1)}, bf16[4,2,8,4096]{3,2,1,0:T(8,128)(2,1)S(1)}, u32[]{:S(2)}, u32[]{:S(2)}) collective-permute-start(bf16[4,2,8,4096]{3,2,1,0:T(8,128)(2,1)S(1)} %pad_maximum_fusion.2), channel_id=1, source_target_pairs={{0,4},{1,5},{2,6},{3,7},{4,8},{5,9},{6,10},{7,11},{8,12},{9,13},{1... | collective-permute-start | bytes 1572872 | tf_op jit(solution)/shard_map/ppermute | solution.py:42
  122.8 17.5 %collective-permute-start.38 = (bf16[4,2,8,4096]{3,2,1,0:T(8,128)(2,1)S(1)}, bf16[4,2,8,4096]{3,2,1,0:T(8,128)(2,1)S(1)}, u32[]{:S(2)}, u32[]{:S(2)}) collective-permute-start(bf16[4,2,8,4096]{3,2,1,0:T(8,128)(2,1)S(1)} %pad_maximum_fusion.2), channel_id=1, source_target_pairs={{0,8},{1,9},{2,10},{3,11},{4,12},{5,13},{6,14},{7,15},{8,0},{9,1},... | collective-permute-start | bytes 1572872 | tf_op jit(solution)/shard_map/ppermute | solution.py:42
  127.8 11.6 %copy-start.4 = (f32[4,4,8,1024]{3,2,1,0:T(8,128)}, f32[4,4,8,1024]{3,2,1,0:T(8,128)S(1)}, u32[]{:S(2)}) copy-start(f32[4,4,8,1024]{3,2,1,0:T(8,128)S(1)} %collective-permute-done.21.refs_0_) | copy-start | bytes 1572868
  127.9 11.6 %copy-start.5 = (f32[4,4,8,1024]{3,2,1,0:T(8,128)}, f32[4,4,8,1024]{3,2,1,0:T(8,128)S(1)}, u32[]{:S(2)}) copy-start(f32[4,4,8,1024]{3,2,1,0:T(8,128)S(1)} %collective-permute-done.22.refs_1_) | copy-start | bytes 1572868
  140.3 10.7 %collective-permute-start.37 = (f32[3,4,8,1024]{3,2,1,0:T(8,128)S(1)}, f32[3,4,8,1024]{3,2,1,0:T(8,128)S(1)}, u32[]{:S(2)}, u32[]{:S(2)}) collective-permute-start(f32[3,4,8,1024]{3,2,1,0:T(8,128)S(1)} %get-tuple-element.67), channel_id=1, source_target_pairs={{0,64},{1,65},{2,66},{3,67},{4,68},{5,69},{6,70},{7,71},{8,72},{9,... | collective-permute-start | bytes 1179656 | tf_op jit(solution)/shard_map/ppermute | solution.py:42
  142.6 8.4 %collective-permute-start.39 = (f32[1,4,8,1024]{3,2,1,0:T(8,128)S(1)}, f32[1,4,8,1024]{3,2,1,0:T(8,128)S(1)}, u32[]{:S(2)}, u32[]{:S(2)}) collective-permute-start(f32[1,4,8,1024]{3,2,1,0:T(8,128)S(1)} %get-tuple-element.83), channel_id=1, source_target_pairs={{0,64},{1,65},{2,66},{3,67},{4,68},{5,69},{6,70},{7,71},{8,72},{9,... | collective-permute-start | bytes 393224 | tf_op jit(solution)/shard_map/ppermute | solution.py:42
  (5 other events, 7.1 us)

commit v3 on v2

--- a/solution.py
+++ b/solution.py
@@ -227,7 +227,7 @@
                 for piece in pieces:
                     if second in piece:
                         for term in terms[at : at + len(group)]:
-                            total = total + term[piece.index(second), first]
+                            total = total + term[piece.index(second), first].astype(jnp.float32)
                     at += len(group)
             out_ref[group_at(place, first, second, -1)] = total.astype(jnp.bfloat16)
 
@@ -249,7 +249,10 @@
     rows = jnp.concatenate([part.reshape(-1, part.shape[-1]) for part in parts], axis=0)
     terms = jnp.dot(rows, w_output, preferred_element_type=jnp.float32)
     terms = terms.reshape(len(parts), SIDE, len(group), ROWS, -1)
-    sent = [along_x(terms[:, :, i], -dx) if dx else terms[:, :, i] for i, dx in enumerate(group)]
+    parts = [terms[:, :, i] for i in range(len(group))]
+    sent = [
+        along_x(part.astype(jnp.bfloat16), -dx) if dx else part for part, dx in zip(parts, group)
+    ]
     return sent, terms
 
 
@@ -281,8 +284,8 @@
     new = ()
 
     terms = []
-    came, far, ready, local = {}, {}, w_in, None
-    for pieces, group in PIECES:
+    came, ready, returned = {}, w_in, []
+    for _, group in PIECES:
         rows = [after(hidden[dx], ready) for dx in group]
         summed, came, ready = sum_over_plane(rows, w_in, came, w_back)
         packed = [along_x(summed[i], -dx) if dx else summed[i] for i, dx in enumerate(group)]
@@ -290,7 +293,12 @@
         packed = jnp.stack(packed)
         mixed, *new = attention(chips, packed, cosine, sine, mask, cache_keys, cache_values, new)
         rows = [along_x(mixed[i], dx) if dx else mixed[i] for i, dx in enumerate(group)]
-        rows = after(jnp.stack(rows), to_pair(mixed[0, :, :DH]))
+        returned.append(jnp.stack(rows))
+
+    met = to_pair(mixed[0, :, :DH])
+    far, local = {}, None
+    for (pieces, group), rows in zip(PIECES, returned):
+        rows = after(rows, met)
         near = {0: rows}
         for step in (2, 1, 3):
             near[step] = along_first(rows, step)

time: 154 us -> 146 us (0.948)
  the two profiles are of different devices: /device:TPU:66 before, /device:TPU:6 now
where the time goes in v3:
time: 146 us; the launch traced here: 145 us
  starting transfers between devices  61.9 us (42%)
  waiting for transfers between devices  40 us (27%)
  Pallas kernels  14.3 us (10%)
  matrix products  11.6 us (8%)
  local copies, waits for them, and re-layouts  11.1 us (8%)
  other arithmetic  5.28 us (4%)
    ppermute x41, starting transfers between devices, permute(): return lax.ppermute(value, AXES, pairs)  61.9 us
    ppermute x41, waiting for transfers between devices, permute(): return lax.ppermute(value, AXES, pairs)  40 us
    pallas_call x2, Pallas kernels, attention(): pl.pallas_call(attention_kernel, out_shape=(jax.ShapeDtypeStruct((steps,...  10.4 us
    unnamed x31, local copies, waits for them, and re-layouts  8.06 us
    dot_general x3, matrix products, project(): terms = jnp.dot(rows, w_output, preferred_element_type=jnp.float32)  5.89 us
    dot_general x4, matrix products, sum_over_plane(): value = jnp.dot(value, weights, preferred_element_type=jnp.float32)  5.71 us
  transfers between devices with their start and end apart: 41, of which 15 were waited for; matrix products, arithmetic and copies ran while one was open for 18% of the time, Pallas kernels for 8%

profile of v3, /device:TPU:6, one launch (start us, length us, event | category | flops | bytes accessed | tf_op | source)
XLA Modules:
  0.0 145.4 jit_solution(18428735712954353277)
XLA Ops:
  1.4 1.8 %order_rows.1 = bf16[4,4,8,1024]{3,2,1,0:T(8,128)(2,1)} custom-call(s32[3]{0:T(128)} %pad_add_fusion.place, bf16[16,8,1024]{2,1,0:T(8,128)(2,1)} %bitcast.99), custom_call_target="tpu_custom_call" | custom-call | bytes 524288 | tf_op jit(solution)/shard_map/order_rows/pallas_call | solution.py:76
  3.5 1.6 %collective-permute-start.3 = (bf16[4,4,8,1024]{3,2,1,0:T(8,128)(2,1)}, bf16[4,4,8,1024]{3,2,1,0:T(8,128)(2,1)S(1)}, u32[]{:S(2)}, u32[]{:S(2)}) collective-permute-start(bf16[4,4,8,1024]{3,2,1,0:T(8,128)(2,1)} %order_rows.1), channel_id=1, source_target_pairs={{0,96},{1,97},{2,98},{3,99},{4,100},{5,101},{6,102},{7,103},{8,104... | collective-permute-start | bytes 786440 | tf_op jit(solution)/shard_map/ppermute | solution.py:42
  5.2 1.1 pad_maximum_fusion
  7.4 2.7 %constant_dynamic-update-slice_fusion.4 = bf16[1024,4608]{1,0:T(8,128)(2,1)S(1)} fusion(bf16[1024,2048]{1,0:T(8,128)(2,1)} %param.10), kind=kLoop, calls=%fused_computation.94 | loop fusion | bytes 8388608
  12.0 1.3 collective-permute-done.3
  13.3 1.3 collective-permute-start.15
  14.6 2.5 %constant_dynamic-update-slice_fusion.1 = bf16[1024,4608]{1,0:T(8,128)(2,1)S(1)} fusion(bf16[1024,4608]{1,0:T(8,128)(2,1)S(1)} %constant_dynamic-update-slice_fusion.2, bf16[1024,2048]{1,0:T(8,128)(2,1)} %collective-permute-done.1), kind=kLoop, calls=%fused_computation.91 | loop fusion | bytes 8388608
  17.3 1.4 fusion.2
  19.0 3.3 %collective-permute-start.7 = (f16[64,4608]{1,0:T(8,128)(2,1)S(1)}, f16[64,4608]{1,0:T(8,128)(2,1)S(1)}, u32[]{:S(2)}, u32[]{:S(2)}) collective-permute-start(f16[64,4608]{1,0:T(8,128)(2,1)S(1)} %get-tuple-element.66), channel_id=1, source_target_pairs={{0,2},{1,3},{2,0},{3,1},{4,6},{5,7},{6,4},{7,5},{8,10},{9,11},{10,... | collective-permute-start | bytes 1769480 | tf_op jit(solution)/shard_map/ppermute | solution.py:42
  22.3 1.4 fusion.3
  23.9 1.1 collective-permute-start.6
  26.1 1.4 fusion.4
  27.6 1.4 fusion.5
  29.4 1.1 collective-permute-done.7
  30.5 3.2 %collective-permute-start.18 = (f16[64,4608]{1,0:T(8,128)(2,1)S(1)}, f16[64,4608]{1,0:T(8,128)(2,1)S(1)}, u32[]{:S(2)}, u32[]{:S(2)}) collective-permute-start(f16[64,4608]{1,0:T(8,128)(2,1)S(1)} %get-tuple-element.41), channel_id=1, source_target_pairs={{0,2},{1,3},{2,0},{3,1},{4,6},{5,7},{6,4},{7,5},{8,10},{9,11},{10,... | collective-permute-start | bytes 1769480 | tf_op jit(solution)/shard_map/ppermute | solution.py:42
  33.7 3.4 %collective-permute-done.6 = f16[64,4608]{1,0:T(8,128)(2,1)S(1)} collective-permute-done((f16[64,4608]{1,0:T(8,128)(2,1)S(1)}, f16[64,4608]{1,0:T(8,128)(2,1)S(1)}, u32[]{:S(2)}, u32[]{:S(2)}) %collective-permute-start.6) | collective-permute-done | bytes 589856 | tf_op jit(solution)/shard_map/ppermute | solution.py:42
  37.1 2.6 %collective-permute-start.17 = (f16[64,4608]{1,0:T(8,128)(2,1)S(1)}, f16[64,4608]{1,0:T(8,128)(2,1)}, u32[]{:S(2)}, u32[]{:S(2)}) collective-permute-start(f16[64,4608]{1,0:T(8,128)(2,1)S(1)} %get-tuple-element.40), channel_id=1, source_target_pairs={{0,3},{1,0},{2,1},{3,2},{4,7},{5,4},{6,5},{7,6},{8,11},{9,8},{10,9... | collective-permute-start | bytes 1769480 | tf_op jit(solution)/shard_map/ppermute | solution.py:42
  40.7 4.1 %collective-permute-start.10 = (f16[16,4608]{1,0:T(8,128)(2,1)S(1)}, f16[16,4608]{1,0:T(8,128)(2,1)S(1)}, u32[]{:S(2)}, u32[]{:S(2)}) collective-permute-start(f16[16,4608]{1,0:T(8,128)(2,1)S(1)} %get-tuple-element.73), channel_id=1, source_target_pairs={{0,12},{1,13},{2,14},{3,15},{4,0},{5,1},{6,2},{7,3},{8,4},{9,5},{1... | collective-permute-start | bytes 442376 | tf_op jit(solution)/shard_map/ppermute | solution.py:42
  44.8 2.1 %collective-permute-start.8 = (f16[16,4608]{1,0:T(8,128)(2,1)S(1)}, f16[16,4608]{1,0:T(8,128)(2,1)S(1)}, u32[]{:S(2)}, u32[]{:S(2)}) collective-permute-start(f16[16,4608]{1,0:T(8,128)(2,1)S(1)} %get-tuple-element.72), channel_id=1, source_target_pairs={{0,8},{1,9},{2,10},{3,11},{4,12},{5,13},{6,14},{7,15},{8,0},{9,1},... | collective-permute-start | bytes 442376 | tf_op jit(solution)/shard_map/ppermute | solution.py:42
  47.0 6.1 %collective-permute-done.17 = f16[64,4608]{1,0:T(8,128)(2,1)} collective-permute-done((f16[64,4608]{1,0:T(8,128)(2,1)S(1)}, f16[64,4608]{1,0:T(8,128)(2,1)}, u32[]{:S(2)}, u32[]{:S(2)}) %collective-permute-start.17) | collective-permute-done | bytes 589856 | tf_op jit(solution)/shard_map/ppermute | solution.py:42
  53.1 1.1 collective-permute-done.16
  54.1 1.7 %fusion.60 = (f16[64,4608]{1,0:T(8,128)(2,1)S(1)}, f32[64,4608]{1,0:T(8,128)S(1)}) fusion(f16[64,4608]{1,0:T(8,128)(2,1)S(1)} %collective-permute-done.18, f16[64,4608]{1,0:T(8,128)(2,1)} %collective-permute-done.17, f16[64,4608]{1,0:T(8,128)(2,1)} %collective-permute-done.16, f16[64,4608]{1,0:T(8,128)(2,1)S(1)} %get-tuple-element.38), kind=kLoop, calls=%fused_computation.116 | loop fusion | flops 2359296 | bytes 4128768 | tf_op jit(solution)/shard_map/convert.6
  55.9 4.1 %collective-permute-start.21 = (f16[16,4608]{1,0:T(8,128)(2,1)S(1)}, f16[16,4608]{1,0:T(8,128)(2,1)S(1)}, u32[]{:S(2)}, u32[]{:S(2)}) collective-permute-start(f16[16,4608]{1,0:T(8,128)(2,1)S(1)} %get-tuple-element.70), channel_id=1, source_target_pairs={{0,12},{1,13},{2,14},{3,15},{4,0},{5,1},{6,2},{7,3},{8,4},{9,5},{1... | collective-permute-start | bytes 442376 | tf_op jit(solution)/shard_map/ppermute | solution.py:42
  60.0 1.9 %collective-permute-start.19 = (f16[16,4608]{1,0:T(8,128)(2,1)S(1)}, f16[16,4608]{1,0:T(8,128)(2,1)S(1)}, u32[]{:S(2)}, u32[]{:S(2)}) collective-permute-start(f16[16,4608]{1,0:T(8,128)(2,1)S(1)} %get-tuple-element.69), channel_id=1, source_target_pairs={{0,8},{1,9},{2,10},{3,11},{4,12},{5,13},{6,14},{7,15},{8,0},{9,1},... | collective-permute-start | bytes 442376 | tf_op jit(solution)/shard_map/ppermute | solution.py:42
  62.0 1.9 %collective-permute-start.12 = (bf16[8,4608]{1,0:T(8,128)(2,1)S(1)}, bf16[8,4608]{1,0:T(8,128)(2,1)S(1)}, u32[]{:S(2)}, u32[]{:S(2)}) collective-permute-start(bf16[8,4608]{1,0:T(8,128)(2,1)S(1)} %get-tuple-element.88), channel_id=1, source_target_pairs={{0,32},{1,33},{2,34},{3,35},{4,36},{5,37},{6,38},{7,39},{8,40},{9,... | collective-permute-start | bytes 221192 | tf_op jit(solution)/shard_map/ppermute | solution.py:42
  64.1 3.9 %collective-permute-done.20 = f16[16,4608]{1,0:T(8,128)(2,1)S(1)} collective-permute-done((f16[16,4608]{1,0:T(8,128)(2,1)S(1)}, f16[16,4608]{1,0:T(8,128)(2,1)S(1)}, u32[]{:S(2)}, u32[]{:S(2)}) %collective-permute-start.20) | collective-permute-done | bytes 147488 | tf_op jit(solution)/shard_map/ppermute | solution.py:42
  68.1 2.4 %collective-permute-start.22 = (bf16[8,4608]{1,0:T(8,128)(2,1)S(1)}, bf16[8,4608]{1,0:T(8,128)(2,1)S(1)}, u32[]{:S(2)}, u32[]{:S(2)}) collective-permute-start(bf16[8,4608]{1,0:T(8,128)(2,1)S(1)} %get-tuple-element.86), channel_id=1, source_target_pairs={{0,64},{1,65},{2,66},{3,67},{4,68},{5,69},{6,70},{7,71},{8,72},{9,... | collective-permute-start | bytes 221192 | tf_op jit(solution)/shard_map/ppermute | solution.py:42
  70.6 5.2 %attention.2 = (bf16[2,8,4096]{2,1,0:T(8,128)(2,1)S(1)}, bf16[8,1024]{1,0:T(8,128)(2,1)}, bf16[8,1024]{1,0:T(8,128)(2,1)}) custom-call(s32[3]{0:T(128)S(1)} %pad_add_fusion.1.place, bf16[2,8,4608]{2,1,0:T(8,128)(2,1)S(1)} %pad_maximum_fusion.3.q_ref, f32[8,128]{1,0:T(8,128)S(1)} %get-tuple-element.96.cos_ref, f32[8,128]{1,0:T(8,128)S(1)} %get-tuple-element.97.sin_ref, ...), custom_call_target="tpu_custom_call" | custom-call | flops 117440512 | bytes 7340032 | tf_op jit(solution)/shard_map/attention/pallas_call | solution.py:187
  76.2 2.9 %collective-permute-start.13 = (bf16[8,4096]{1,0:T(8,128)(2,1)S(1)}, bf16[8,4096]{1,0:T(8,128)(2,1)S(1)}, u32[]{:S(2)}, u32[]{:S(2)}) collective-permute-start(bf16[8,4096]{1,0:T(8,128)(2,1)S(1)} %get-tuple-element.91), channel_id=1, source_target_pairs={{0,32},{1,33},{2,34},{3,35},{4,36},{5,37},{6,38},{7,39},{8,40},{9,... | collective-permute-start | bytes 196616 | tf_op jit(solution)/shard_map/ppermute | solution.py:42
  79.1 5.2 %attention.3 = (bf16[2,8,4096]{2,1,0:T(8,128)(2,1)S(1)}, bf16[8,1024]{1,0:T(8,128)(2,1)}, bf16[8,1024]{1,0:T(8,128)(2,1)}) custom-call(s32[3]{0:T(128)S(1)} %pad_add_fusion.2.place, bf16[2,8,4608]{2,1,0:T(8,128)(2,1)S(1)} %pad_maximum_fusion.4.q_ref, f32[8,128]{1,0:T(8,128)S(1)} %get-tuple-element.96.cos_ref, ...), custom_call_target="tpu_custom_call", output_to_operand_aliasing={{1}: (7, {}), {2}: (8, {})} | custom-call | flops 117440512 | bytes 7340032 | tf_op jit(solution)/shard_map/attention/pallas_call | solution.py:187
  85.6 1.6 %collective-permute-start.26 = (bf16[2,8,4096]{2,1,0:T(8,128)(2,1)S(1)}, bf16[2,8,4096]{2,1,0:T(8,128)(2,1)S(1)}, u32[]{:S(2)}, u32[]{:S(2)}) collective-permute-start(bf16[2,8,4096]{2,1,0:T(8,128)(2,1)S(1)} %pad_maximum_fusion.7), channel_id=1, source_target_pairs={{0,3},{1,0},{2,1},{3,2},{4,7},{5,4},{6,5},{7,6},{8,11},{9,8},{10,9... | collective-permute-start | bytes 393224 | tf_op jit(solution)/shard_map/ppermute | solution.py:42
  88.8 1.7 %collective-permute-done.32 = bf16[8,4096]{1,0:T(8,128)(2,1)S(1)} collective-permute-done((bf16[8,4096]{1,0:T(8,128)(2,1)S(1)}, bf16[8,4096]{1,0:T(8,128)(2,1)S(1)}, u32[]{:S(2)}, u32[]{:S(2)}) %collective-permute-start.32) | collective-permute-done | bytes 65568 | tf_op jit(solution)/shard_map/ppermute | solution.py:42
  90.5 1.7 %collective-permute-start.35 = (bf16[2,8,4096]{2,1,0:T(8,128)(2,1)S(1)}, bf16[2,8,4096]{2,1,0:T(8,128)(2,1)S(1)}, u32[]{:S(2)}, u32[]{:S(2)}) collective-permute-start(bf16[2,8,4096]{2,1,0:T(8,128)(2,1)S(1)} %pad_maximum_fusion.8), channel_id=1, source_target_pairs={{0,3},{1,0},{2,1},{3,2},{4,7},{5,4},{6,5},{7,6},{8,11},{9,8},{10,9... | collective-permute-start | bytes 393224 | tf_op jit(solution)/shard_map/ppermute | solution.py:42
  93.8 1.3 collective-permute-done.24
  95.1 2.0 %collective-permute-start.29 = (bf16[4,2,8,4096]{3,2,1,0:T(8,128)(2,1)S(1)}, bf16[4,2,8,4096]{3,2,1,0:T(8,128)(2,1)S(1)}, u32[]{:S(2)}, u32[]{:S(2)}) collective-permute-start(bf16[4,2,8,4096]{3,2,1,0:T(8,128)(2,1)S(1)} %pad_maximum_fusion.1), channel_id=1, source_target_pairs={{0,12},{1,13},{2,14},{3,15},{4,0},{5,1},{6,2},{7,3},{8,4},{9,5},{1... | collective-permute-start | bytes 1572872 | tf_op jit(solution)/shard_map/ppermute | solution.py:42
  97.2 1.7 %collective-permute-start.28 = (bf16[4,2,8,4096]{3,2,1,0:T(8,128)(2,1)S(1)}, bf16[4,2,8,4096]{3,2,1,0:T(8,128)(2,1)S(1)}, u32[]{:S(2)}, u32[]{:S(2)}) collective-permute-start(bf16[4,2,8,4096]{3,2,1,0:T(8,128)(2,1)S(1)} %pad_maximum_fusion.1), channel_id=1, source_target_pairs={{0,8},{1,9},{2,10},{3,11},{4,12},{5,13},{6,14},{7,15},{8,0},{9,1},... | collective-permute-start | bytes 1572872 | tf_op jit(solution)/shard_map/ppermute | solution.py:42
  98.9 1.6 %collective-permute-done.33 = bf16[2,8,4096]{2,1,0:T(8,128)(2,1)S(1)} collective-permute-done((bf16[2,8,4096]{2,1,0:T(8,128)(2,1)S(1)}, bf16[2,8,4096]{2,1,0:T(8,128)(2,1)S(1)}, u32[]{:S(2)}, u32[]{:S(2)}) %collective-permute-start.33) | collective-permute-done | bytes 131104 | tf_op jit(solution)/shard_map/ppermute | solution.py:42
  100.6 8.9 %collective-permute-done.29 = bf16[4,2,8,4096]{3,2,1,0:T(8,128)(2,1)S(1)} collective-permute-done((bf16[4,2,8,4096]{3,2,1,0:T(8,128)(2,1)S(1)}, bf16[4,2,8,4096]{3,2,1,0:T(8,128)(2,1)S(1)}, u32[]{:S(2)}, u32[]{:S(2)}) %collective-permute-start.29) | collective-permute-done | bytes 524320 | tf_op jit(solution)/shard_map/ppermute | solution.py:42
  109.5 3.7 %collective-permute-start.37 = (bf16[4,2,8,4096]{3,2,1,0:T(8,128)(2,1)S(1)}, bf16[4,2,8,4096]{3,2,1,0:T(8,128)(2,1)S(1)}, u32[]{:S(2)}, u32[]{:S(2)}) collective-permute-start(bf16[4,2,8,4096]{3,2,1,0:T(8,128)(2,1)S(1)} %pad_maximum_fusion.2), channel_id=1, source_target_pairs={{0,12},{1,13},{2,14},{3,15},{4,0},{5,1},{6,2},{7,3},{8,4},{9,5},{1... | collective-permute-start | bytes 1572872 | tf_op jit(solution)/shard_map/ppermute | solution.py:42
  113.2 2.4 %fusion.6 = bf16[256,1024]{1,0:T(8,128)(2,1)S(1)} fusion(bf16[4096,1024]{1,0:T(8,128)(2,1)S(1)} %constant_dynamic-update-slice_fusion.5, bf16[64,4096]{1,0:T(8,128)(2,1)S(1)} %bitcast.117, bf16[64,4096]{1,0:T(8,128)(2,1)S(1)} %bitcast.120, bf16[64,4096]{1,0:T(8,128)(2,1)S(1)} %bitcast.119, bf16[64,4096]{1,0:T(8,128)(2,1)S(1)} %bitcast.93), kind=kOutput, calls=%fused_computation.10 | convolution fusion | flops 2155872256 | bytes 11010048 | tf_op jit(solution)/shard_map/dot_general | solution.py:250
  115.7 3.2 %collective-permute-start.31 = (bf16[4,4,8,1024]{3,2,1,0:T(8,128)(2,1)S(1)}, bf16[4,4,8,1024]{3,2,1,0:T(8,128)(2,1)S(1)}, u32[]{:S(2)}, u32[]{:S(2)}) collective-permute-start(bf16[4,4,8,1024]{3,2,1,0:T(8,128)(2,1)S(1)} %get-tuple-element.75), channel_id=1, source_target_pairs={{0,32},{1,33},{2,34},{3,35},{4,36},{5,37},{6,38},{7,39},{8,40},{9,... | collective-permute-start | bytes 786440 | tf_op jit(solution)/shard_map/ppermute | solution.py:42
  119.0 1.5 %collective-permute-start.39 = (bf16[4,2,8,4096]{3,2,1,0:T(8,128)(2,1)S(1)}, bf16[4,2,8,4096]{3,2,1,0:T(8,128)(2,1)S(1)}, u32[]{:S(2)}, u32[]{:S(2)}) collective-permute-start(bf16[4,2,8,4096]{3,2,1,0:T(8,128)(2,1)S(1)} %pad_maximum_fusion.2), channel_id=1, source_target_pairs={{0,8},{1,9},{2,10},{3,11},{4,12},{5,13},{6,14},{7,15},{8,0},{9,1},... | collective-permute-start | bytes 1572872 | tf_op jit(solution)/shard_map/ppermute | solution.py:42
  120.4 2.9 %collective-permute-done.30.refs_0_ = bf16[4,4,8,1024]{3,2,1,0:T(8,128)(2,1)S(1)} collective-permute-done((bf16[4,4,8,1024]{3,2,1,0:T(8,128)(2,1)S(1)}, bf16[4,4,8,1024]{3,2,1,0:T(8,128)(2,1)S(1)}, u32[]{:S(2)}, u32[]{:S(2)}) %collective-permute-start.30) | collective-permute-done | bytes 262176 | tf_op jit(solution)/shard_map/ppermute | solution.py:42
  123.6 1.9 %fusion.14 = f32[192,1024]{1,0:T(8,128)S(1)} fusion(bf16[4096,1024]{1,0:T(8,128)(2,1)S(1)} %constant_dynamic-update-slice_fusion.5, bf16[64,4096]{1,0:T(8,128)(2,1)S(1)} %bitcast.116, bf16[64,4096]{1,0:T(8,128)(2,1)S(1)} %bitcast.118, bf16[64,4096]{1,0:T(8,128)(2,1)S(1)} %bitcast.92), kind=kOutput, calls=%fused_computation.18 | convolution fusion | flops 1615331328 | bytes 10747904 | tf_op jit(solution)/shard_map/dot_general | solution.py:250
  125.5 8.3 %collective-permute-start.38 = (bf16[3,4,8,1024]{3,2,1,0:T(8,128)(2,1)S(1)}, bf16[3,4,8,1024]{3,2,1,0:T(8,128)(2,1)S(1)}, u32[]{:S(2)}, u32[]{:S(2)}) collective-permute-start(bf16[3,4,8,1024]{3,2,1,0:T(8,128)(2,1)S(1)} %fusion.44), channel_id=1, source_target_pairs={{0,64},{1,65},{2,66},{3,67},{4,68},{5,69},{6,70},{7,71},{8,72},{9,... | collective-permute-start | bytes 589832 | tf_op jit(solution)/shard_map/ppermute | solution.py:42
  134.5 1.6 %fusion.20 = f32[1,4,2,8,1024]{4,3,1,2,0:T(8,128)S(1)} fusion(bf16[4096,1024]{1,0:T(8,128)(2,1)S(1)} %constant_dynamic-update-slice_fusion.5, bf16[4,2,8,4096]{3,2,1,0:T(8,128)(2,1)S(1)} %collective-permute-done.39), kind=kOutput, calls=%fused_computation.26 | convolution fusion | flops 536870912 | bytes 9175040 | tf_op jit(solution)/shard_map/dot_general | solution.py:250
  136.9 5.1 %collective-permute-done.40.refs_5_ = bf16[1,4,8,1024]{3,2,1,0:T(8,128)(2,1)S(1)} collective-permute-done((bf16[1,4,8,1024]{3,2,1,0:T(8,128)(2,1)S(1)}, bf16[1,4,8,1024]{3,2,1,0:T(8,128)(2,1)S(1)}, u32[]{:S(2)}, u32[]{:S(2)}) %collective-permute-start.40) | collective-permute-done | bytes 65568 | tf_op jit(solution)/shard_map/ppermute | solution.py:42
  143.3 2.1 %add_up.1 = bf16[16,8,1024]{2,1,0:T(8,128)(2,1)} custom-call(s32[3]{0:T(128)} %pad_add_fusion.place, bf16[4,4,8,1024]{3,2,1,0:T(8,128)(2,1)} %copy-done.4, bf16[4,4,8,1024]{3,2,1,0:T(8,128)(2,1)} %copy-done.5, f32[3,4,8,1024]{3,2,1,0:T(8,128)} %copy_bitcast_fusion.refs_2_, bf16[3,4,8,1024]{3,2,1,0:T(8,128)(2,1)} %copy-done.6, ...), custom_call_target="tpu_custom_call" | custom-call | flops 524288 | bytes 2097152 | tf_op jit(solution)/shard_map/add_up/pallas_call | solution.py:237
  (126 shorter events, 15.7 us)
Async XLA Ops:
  0.6 14.0 %collective-permute-start.1 = (bf16[1024,2048]{1,0:T(8,128)(2,1)}, bf16[1024,2048]{1,0:T(8,128)(2,1)}, u32[]{:S(2)}, u32[]{:S(2)}) collective-permute-start(bf16[1024,2048]{1,0:T(8,128)(2,1)} %param.10), channel_id=1, source_target_pairs={{0,16},{1,17},{2,18},{3,19},{4,20},{5,21},{6,22},{7,23},{8,24},{9,... | collective-permute-start | bytes 12582920 | tf_op jit(solution)/shard_map/ppermute | solution.py:42
  3.1 8.9 %collective-permute-start = (bf16[4,4,8,1024]{3,2,1,0:T(8,128)(2,1)}, bf16[4,4,8,1024]{3,2,1,0:T(8,128)(2,1)S(1)}, u32[]{:S(2)}, u32[]{:S(2)}) collective-permute-start(bf16[4,4,8,1024]{3,2,1,0:T(8,128)(2,1)} %order_rows.1), channel_id=1, source_target_pairs={{0,32},{1,33},{2,34},{3,35},{4,36},{5,37},{6,38},{7,39},{8,40},{9,... | collective-permute-start | bytes 786440 | tf_op jit(solution)/shard_map/ppermute | solution.py:42
  3.5 9.8 %collective-permute-start.3 = (bf16[4,4,8,1024]{3,2,1,0:T(8,128)(2,1)}, bf16[4,4,8,1024]{3,2,1,0:T(8,128)(2,1)S(1)}, u32[]{:S(2)}, u32[]{:S(2)}) collective-permute-start(bf16[4,4,8,1024]{3,2,1,0:T(8,128)(2,1)} %order_rows.1), channel_id=1, source_target_pairs={{0,96},{1,97},{2,98},{3,99},{4,100},{5,101},{6,102},{7,103},{8,104... | collective-permute-start | bytes 786440 | tf_op jit(solution)/shard_map/ppermute | solution.py:42
  6.2 11.0 %collective-permute-start.2 = (bf16[1024,256]{1,0:T(8,128)(2,1)S(1)}, bf16[1024,256]{1,0:T(8,128)(2,1)S(1)}, u32[]{:S(2)}, u32[]{:S(2)}) collective-permute-start(bf16[1024,256]{1,0:T(8,128)(2,1)S(1)} %pad_maximum_fusion), channel_id=1, source_target_pairs={{0,16},{1,17},{2,18},{3,19},{4,20},{5,21},{6,22},{7,23},{8,24},{9,... | collective-permute-start | bytes 1572872 | tf_op jit(solution)/shard_map/ppermute | solution.py:42
  7.4 2.7 %copy-start.2 = (bf16[1024,128]{1,0:T(8,128)(2,1)S(1)}, bf16[1024,128]{1,0:T(8,128)(2,1)}, u32[]{:S(2)}) copy-start(bf16[1024,128]{1,0:T(8,128)(2,1)} %param.11) | copy-start | bytes 786436
  7.4 2.8 %copy-start.3 = (bf16[1024,128]{1,0:T(8,128)(2,1)S(1)}, bf16[1024,128]{1,0:T(8,128)(2,1)}, u32[]{:S(2)}) copy-start(bf16[1024,128]{1,0:T(8,128)(2,1)} %param.12) | copy-start | bytes 786436
  7.4 3.6 %copy-start = (bf16[2048,1024]{1,0:T(8,128)(2,1)S(1)}, bf16[2048,1024]{1,0:T(8,128)(2,1)}, u32[]{:S(2)}) copy-start(bf16[2048,1024]{1,0:T(8,128)(2,1)} %param.13) | copy-start | bytes 12582916
  13.3 12.7 %collective-permute-start.15 = (bf16[4,4,8,1024]{3,2,1,0:T(8,128)(2,1)S(1)}, bf16[4,4,8,1024]{3,2,1,0:T(8,128)(2,1)S(1)}, u32[]{:S(2)}, u32[]{:S(2)}) collective-permute-start(bf16[4,4,8,1024]{3,2,1,0:T(8,128)(2,1)S(1)} %copy-done.1), channel_id=1, source_target_pairs={{0,64},{1,65},{2,66},{3,67},{4,68},{5,69},{6,70},{7,71},{8,72},{9,... | collective-permute-start | bytes 786440 | tf_op jit(solution)/shard_map/ppermute | solution.py:42
  14.6 25.2 %collective-permute-start.4 = (bf16[2048,1024]{1,0:T(8,128)(2,1)S(1)}, bf16[2048,1024]{1,0:T(8,128)(2,1)S(1)}, u32[]{:S(2)}, u32[]{:S(2)}) collective-permute-start(bf16[2048,1024]{1,0:T(8,128)(2,1)S(1)} %copy-done), channel_id=1, source_target_pairs={{0,16},{1,17},{2,18},{3,19},{4,20},{5,21},{6,22},{7,23},{8,24},{9,... | collective-permute-start | bytes 12582920 | tf_op jit(solution)/shard_map/ppermute | solution.py:42
  19.0 11.5 %collective-permute-start.7 = (f16[64,4608]{1,0:T(8,128)(2,1)S(1)}, f16[64,4608]{1,0:T(8,128)(2,1)S(1)}, u32[]{:S(2)}, u32[]{:S(2)}) collective-permute-start(f16[64,4608]{1,0:T(8,128)(2,1)S(1)} %get-tuple-element.66), channel_id=1, source_target_pairs={{0,2},{1,3},{2,0},{3,1},{4,6},{5,7},{6,4},{7,5},{8,10},{9,11},{10,... | collective-permute-start | bytes 1769480 | tf_op jit(solution)/shard_map/ppermute | solution.py:42
  23.9 13.2 %collective-permute-start.6 = (f16[64,4608]{1,0:T(8,128)(2,1)S(1)}, f16[64,4608]{1,0:T(8,128)(2,1)S(1)}, u32[]{:S(2)}, u32[]{:S(2)}) collective-permute-start(f16[64,4608]{1,0:T(8,128)(2,1)S(1)} %get-tuple-element.68), channel_id=1, source_target_pairs={{0,3},{1,0},{2,1},{3,2},{4,7},{5,4},{6,5},{7,6},{8,11},{9,8},{10,9... | collective-permute-start | bytes 1769480 | tf_op jit(solution)/shard_map/ppermute | solution.py:42
  25.0 14.7 %collective-permute-start.5 = (f16[64,4608]{1,0:T(8,128)(2,1)S(1)}, f16[64,4608]{1,0:T(8,128)(2,1)S(1)}, u32[]{:S(2)}, u32[]{:S(2)}) collective-permute-start(f16[64,4608]{1,0:T(8,128)(2,1)S(1)} %get-tuple-element.67), channel_id=1, source_target_pairs={{0,1},{1,2},{2,3},{3,0},{4,5},{5,6},{6,7},{7,4},{8,9},{9,10},{10,1... | collective-permute-start | bytes 1769480 | tf_op jit(solution)/shard_map/ppermute | solution.py:42
  30.5 14.3 %collective-permute-start.18 = (f16[64,4608]{1,0:T(8,128)(2,1)S(1)}, f16[64,4608]{1,0:T(8,128)(2,1)S(1)}, u32[]{:S(2)}, u32[]{:S(2)}) collective-permute-start(f16[64,4608]{1,0:T(8,128)(2,1)S(1)} %get-tuple-element.41), channel_id=1, source_target_pairs={{0,2},{1,3},{2,0},{3,1},{4,6},{5,7},{6,4},{7,5},{8,10},{9,11},{10,... | collective-permute-start | bytes 1769480 | tf_op jit(solution)/shard_map/ppermute | solution.py:42
  37.1 15.9 %collective-permute-start.17 = (f16[64,4608]{1,0:T(8,128)(2,1)S(1)}, f16[64,4608]{1,0:T(8,128)(2,1)}, u32[]{:S(2)}, u32[]{:S(2)}) collective-permute-start(f16[64,4608]{1,0:T(8,128)(2,1)S(1)} %get-tuple-element.40), channel_id=1, source_target_pairs={{0,3},{1,0},{2,1},{3,2},{4,7},{5,4},{6,5},{7,6},{8,11},{9,8},{10,9... | collective-permute-start | bytes 1769480 | tf_op jit(solution)/shard_map/ppermute | solution.py:42
  39.8 14.4 %collective-permute-start.16 = (f16[64,4608]{1,0:T(8,128)(2,1)S(1)}, f16[64,4608]{1,0:T(8,128)(2,1)}, u32[]{:S(2)}, u32[]{:S(2)}) collective-permute-start(f16[64,4608]{1,0:T(8,128)(2,1)S(1)} %get-tuple-element.39), channel_id=1, source_target_pairs={{0,1},{1,2},{2,3},{3,0},{4,5},{5,6},{6,7},{7,4},{8,9},{9,10},{10,1... | collective-permute-start | bytes 1769480 | tf_op jit(solution)/shard_map/ppermute | solution.py:42
  39.8 30.7 %slice-start = ((s8[7340032]{0:T(1024)(128)(4,1)}), s8[4194304]{0:T(1024)(128)(4,1)S(1)}, s32[]{:S(2)}) async-start(s8[7340032]{0:T(1024)(128)(4,1)} %bitcast.79), calls=%async_computation | async-start | bytes 8388608
  39.8 30.7 %slice-start.2 = ((s8[7340032]{0:T(1024)(128)(4,1)}), s8[4194304]{0:T(1024)(128)(4,1)S(1)}, s32[]{:S(2)}) async-start(s8[7340032]{0:T(1024)(128)(4,1)} %bitcast.81), calls=%async_computation.2 | async-start | bytes 8388608
  40.3 30.3 %slice-start.1 = ((s8[7340032]{0:T(1024)(128)(4,1)}), s8[3145728]{0:T(1024)(128)(4,1)S(1)}, s32[]{:S(2)}) async-start(s8[7340032]{0:T(1024)(128)(4,1)} %bitcast.79), calls=%async_computation.1 | async-start | bytes 6291456
  40.3 30.3 %slice-start.3 = ((s8[7340032]{0:T(1024)(128)(4,1)}), s8[3145728]{0:T(1024)(128)(4,1)S(1)}, s32[]{:S(2)}) async-start(s8[7340032]{0:T(1024)(128)(4,1)} %bitcast.81), calls=%async_computation.3 | async-start | bytes 6291456
  40.7 19.3 %collective-permute-start.10 = (f16[16,4608]{1,0:T(8,128)(2,1)S(1)}, f16[16,4608]{1,0:T(8,128)(2,1)S(1)}, u32[]{:S(2)}, u32[]{:S(2)}) collective-permute-start(f16[16,4608]{1,0:T(8,128)(2,1)S(1)} %get-tuple-element.73), channel_id=1, source_target_pairs={{0,12},{1,13},{2,14},{3,15},{4,0},{5,1},{6,2},{7,3},{8,4},{9,5},{1... | collective-permute-start | bytes 442376 | tf_op jit(solution)/shard_map/ppermute | solution.py:42
  44.8 17.1 %collective-permute-start.9 = (f16[16,4608]{1,0:T(8,128)(2,1)S(1)}, f16[16,4608]{1,0:T(8,128)(2,1)S(1)}, u32[]{:S(2)}, u32[]{:S(2)}) collective-permute-start(f16[16,4608]{1,0:T(8,128)(2,1)S(1)} %get-tuple-element.74), channel_id=1, source_target_pairs={{0,4},{1,5},{2,6},{3,7},{4,8},{5,9},{6,10},{7,11},{8,12},{9,13},{1... | collective-permute-start | bytes 442376 | tf_op jit(solution)/shard_map/ppermute | solution.py:42
  44.8 17.1 %collective-permute-start.8 = (f16[16,4608]{1,0:T(8,128)(2,1)S(1)}, f16[16,4608]{1,0:T(8,128)(2,1)S(1)}, u32[]{:S(2)}, u32[]{:S(2)}) collective-permute-start(f16[16,4608]{1,0:T(8,128)(2,1)S(1)} %get-tuple-element.72), channel_id=1, source_target_pairs={{0,8},{1,9},{2,10},{3,11},{4,12},{5,13},{6,14},{7,15},{8,0},{9,1},... | collective-permute-start | bytes 442376 | tf_op jit(solution)/shard_map/ppermute | solution.py:42
  55.9 8.2 %collective-permute-start.21 = (f16[16,4608]{1,0:T(8,128)(2,1)S(1)}, f16[16,4608]{1,0:T(8,128)(2,1)S(1)}, u32[]{:S(2)}, u32[]{:S(2)}) collective-permute-start(f16[16,4608]{1,0:T(8,128)(2,1)S(1)} %get-tuple-element.70), channel_id=1, source_target_pairs={{0,12},{1,13},{2,14},{3,15},{4,0},{5,1},{6,2},{7,3},{8,4},{9,5},{1... | collective-permute-start | bytes 442376 | tf_op jit(solution)/shard_map/ppermute | solution.py:42
  60.0 7.9 %collective-permute-start.20 = (f16[16,4608]{1,0:T(8,128)(2,1)S(1)}, f16[16,4608]{1,0:T(8,128)(2,1)S(1)}, u32[]{:S(2)}, u32[]{:S(2)}) collective-permute-start(f16[16,4608]{1,0:T(8,128)(2,1)S(1)} %get-tuple-element.71), channel_id=1, source_target_pairs={{0,4},{1,5},{2,6},{3,7},{4,8},{5,9},{6,10},{7,11},{8,12},{9,13},{1... | collective-permute-start | bytes 442376 | tf_op jit(solution)/shard_map/ppermute | solution.py:42
  60.0 7.9 %collective-permute-start.19 = (f16[16,4608]{1,0:T(8,128)(2,1)S(1)}, f16[16,4608]{1,0:T(8,128)(2,1)S(1)}, u32[]{:S(2)}, u32[]{:S(2)}) collective-permute-start(f16[16,4608]{1,0:T(8,128)(2,1)S(1)} %get-tuple-element.69), channel_id=1, source_target_pairs={{0,8},{1,9},{2,10},{3,11},{4,12},{5,13},{6,14},{7,15},{8,0},{9,1},... | collective-permute-start | bytes 442376 | tf_op jit(solution)/shard_map/ppermute | solution.py:42
  62.0 8.5 %collective-permute-start.12 = (bf16[8,4608]{1,0:T(8,128)(2,1)S(1)}, bf16[8,4608]{1,0:T(8,128)(2,1)S(1)}, u32[]{:S(2)}, u32[]{:S(2)}) collective-permute-start(bf16[8,4608]{1,0:T(8,128)(2,1)S(1)} %get-tuple-element.88), channel_id=1, source_target_pairs={{0,32},{1,33},{2,34},{3,35},{4,36},{5,37},{6,38},{7,39},{8,40},{9,... | collective-permute-start | bytes 221192 | tf_op jit(solution)/shard_map/ppermute | solution.py:42
  63.9 6.6 %collective-permute-start.11 = (bf16[8,4608]{1,0:T(8,128)(2,1)S(1)}, bf16[8,4608]{1,0:T(8,128)(2,1)S(1)}, u32[]{:S(2)}, u32[]{:S(2)}) collective-permute-start(bf16[8,4608]{1,0:T(8,128)(2,1)S(1)} %get-tuple-element.87), channel_id=1, source_target_pairs={{0,96},{1,97},{2,98},{3,99},{4,100},{5,101},{6,102},{7,103},{8,104... | collective-permute-start | bytes 221192 | tf_op jit(solution)/shard_map/ppermute | solution.py:42
  68.1 11.0 %collective-permute-start.22 = (bf16[8,4608]{1,0:T(8,128)(2,1)S(1)}, bf16[8,4608]{1,0:T(8,128)(2,1)S(1)}, u32[]{:S(2)}, u32[]{:S(2)}) collective-permute-start(bf16[8,4608]{1,0:T(8,128)(2,1)S(1)} %get-tuple-element.86), channel_id=1, source_target_pairs={{0,64},{1,65},{2,66},{3,67},{4,68},{5,69},{6,70},{7,71},{8,72},{9,... | collective-permute-start | bytes 221192 | tf_op jit(solution)/shard_map/ppermute | solution.py:42
  75.8 8.7 %collective-permute-start.14 = (bf16[8,4096]{1,0:T(8,128)(2,1)S(1)}, bf16[8,4096]{1,0:T(8,128)(2,1)S(1)}, u32[]{:S(2)}, u32[]{:S(2)}) collective-permute-start(bf16[8,4096]{1,0:T(8,128)(2,1)S(1)} %get-tuple-element.92), channel_id=1, source_target_pairs={{0,96},{1,97},{2,98},{3,99},{4,100},{5,101},{6,102},{7,103},{8,104... | collective-permute-start | bytes 196616 | tf_op jit(solution)/shard_map/ppermute | solution.py:42
  76.2 8.3 %collective-permute-start.13 = (bf16[8,4096]{1,0:T(8,128)(2,1)S(1)}, bf16[8,4096]{1,0:T(8,128)(2,1)S(1)}, u32[]{:S(2)}, u32[]{:S(2)}) collective-permute-start(bf16[8,4096]{1,0:T(8,128)(2,1)S(1)} %get-tuple-element.91), channel_id=1, source_target_pairs={{0,32},{1,33},{2,34},{3,35},{4,36},{5,37},{6,38},{7,39},{8,40},{9,... | collective-permute-start | bytes 196616 | tf_op jit(solution)/shard_map/ppermute | solution.py:42
  84.4 1.2 collective-permute-start.23
  84.4 6.0 %collective-permute-start.32 = (bf16[8,4096]{1,0:T(8,128)(2,1)S(1)}, bf16[8,4096]{1,0:T(8,128)(2,1)S(1)}, u32[]{:S(2)}, u32[]{:S(2)}) collective-permute-start(bf16[8,4096]{1,0:T(8,128)(2,1)S(1)} %get-tuple-element.90), channel_id=1, source_target_pairs={{0,64},{1,65},{2,66},{3,67},{4,68},{5,69},{6,70},{7,71},{8,72},{9,... | collective-permute-start | bytes 196616 | tf_op jit(solution)/shard_map/ppermute | solution.py:42
  85.6 7.3 %collective-permute-start.26 = (bf16[2,8,4096]{2,1,0:T(8,128)(2,1)S(1)}, bf16[2,8,4096]{2,1,0:T(8,128)(2,1)S(1)}, u32[]{:S(2)}, u32[]{:S(2)}) collective-permute-start(bf16[2,8,4096]{2,1,0:T(8,128)(2,1)S(1)} %pad_maximum_fusion.7), channel_id=1, source_target_pairs={{0,3},{1,0},{2,1},{3,2},{4,7},{5,4},{6,5},{7,6},{8,11},{9,8},{10,9... | collective-permute-start | bytes 393224 | tf_op jit(solution)/shard_map/ppermute | solution.py:42
  87.2 6.6 %collective-permute-start.25 = (bf16[2,8,4096]{2,1,0:T(8,128)(2,1)S(1)}, bf16[2,8,4096]{2,1,0:T(8,128)(2,1)S(1)}, u32[]{:S(2)}, u32[]{:S(2)}) collective-permute-start(bf16[2,8,4096]{2,1,0:T(8,128)(2,1)S(1)} %pad_maximum_fusion.7), channel_id=1, source_target_pairs={{0,2},{1,3},{2,0},{3,1},{4,6},{5,7},{6,4},{7,5},{8,10},{9,11},{10,... | collective-permute-start | bytes 393224 | tf_op jit(solution)/shard_map/ppermute | solution.py:42
  88.0 7.1 %collective-permute-start.24 = (bf16[2,8,4096]{2,1,0:T(8,128)(2,1)S(1)}, bf16[2,8,4096]{2,1,0:T(8,128)(2,1)S(1)}, u32[]{:S(2)}, u32[]{:S(2)}) collective-permute-start(bf16[2,8,4096]{2,1,0:T(8,128)(2,1)S(1)} %pad_maximum_fusion.7), channel_id=1, source_target_pairs={{0,1},{1,2},{2,3},{3,0},{4,5},{5,6},{6,7},{7,4},{8,9},{9,10},{10,1... | collective-permute-start | bytes 393224 | tf_op jit(solution)/shard_map/ppermute | solution.py:42
  90.5 6.7 %collective-permute-start.35 = (bf16[2,8,4096]{2,1,0:T(8,128)(2,1)S(1)}, bf16[2,8,4096]{2,1,0:T(8,128)(2,1)S(1)}, u32[]{:S(2)}, u32[]{:S(2)}) collective-permute-start(bf16[2,8,4096]{2,1,0:T(8,128)(2,1)S(1)} %pad_maximum_fusion.8), channel_id=1, source_target_pairs={{0,3},{1,0},{2,1},{3,2},{4,7},{5,4},{6,5},{7,6},{8,11},{9,8},{10,9... | collective-permute-start | bytes 393224 | tf_op jit(solution)/shard_map/ppermute | solution.py:42
  92.1 6.8 %collective-permute-start.34 = (bf16[2,8,4096]{2,1,0:T(8,128)(2,1)S(1)}, bf16[2,8,4096]{2,1,0:T(8,128)(2,1)S(1)}, u32[]{:S(2)}, u32[]{:S(2)}) collective-permute-start(bf16[2,8,4096]{2,1,0:T(8,128)(2,1)S(1)} %pad_maximum_fusion.8), channel_id=1, source_target_pairs={{0,2},{1,3},{2,0},{3,1},{4,6},{5,7},{6,4},{7,5},{8,10},{9,11},{10,... | collective-permute-start | bytes 393224 | tf_op jit(solution)/shard_map/ppermute | solution.py:42
  92.9 7.6 %collective-permute-start.33 = (bf16[2,8,4096]{2,1,0:T(8,128)(2,1)S(1)}, bf16[2,8,4096]{2,1,0:T(8,128)(2,1)S(1)}, u32[]{:S(2)}, u32[]{:S(2)}) collective-permute-start(bf16[2,8,4096]{2,1,0:T(8,128)(2,1)S(1)} %pad_maximum_fusion.8), channel_id=1, source_target_pairs={{0,1},{1,2},{2,3},{3,0},{4,5},{5,6},{6,7},{7,4},{8,9},{9,10},{10,1... | collective-permute-start | bytes 393224 | tf_op jit(solution)/shard_map/ppermute | solution.py:42
  95.1 14.4 %collective-permute-start.29 = (bf16[4,2,8,4096]{3,2,1,0:T(8,128)(2,1)S(1)}, bf16[4,2,8,4096]{3,2,1,0:T(8,128)(2,1)S(1)}, u32[]{:S(2)}, u32[]{:S(2)}) collective-permute-start(bf16[4,2,8,4096]{3,2,1,0:T(8,128)(2,1)S(1)} %pad_maximum_fusion.1), channel_id=1, source_target_pairs={{0,12},{1,13},{2,14},{3,15},{4,0},{5,1},{6,2},{7,3},{8,4},{9,5},{1... | collective-permute-start | bytes 1572872 | tf_op jit(solution)/shard_map/ppermute | solution.py:42
  97.1 16.0 %collective-permute-start.27 = (bf16[4,2,8,4096]{3,2,1,0:T(8,128)(2,1)S(1)}, bf16[4,2,8,4096]{3,2,1,0:T(8,128)(2,1)S(1)}, u32[]{:S(2)}, u32[]{:S(2)}) collective-permute-start(bf16[4,2,8,4096]{3,2,1,0:T(8,128)(2,1)S(1)} %pad_maximum_fusion.1), channel_id=1, source_target_pairs={{0,4},{1,5},{2,6},{3,7},{4,8},{5,9},{6,10},{7,11},{8,12},{9,13},{1... | collective-permute-start | bytes 1572872 | tf_op jit(solution)/shard_map/ppermute | solution.py:42
  97.2 15.9 %collective-permute-start.28 = (bf16[4,2,8,4096]{3,2,1,0:T(8,128)(2,1)S(1)}, bf16[4,2,8,4096]{3,2,1,0:T(8,128)(2,1)S(1)}, u32[]{:S(2)}, u32[]{:S(2)}) collective-permute-start(bf16[4,2,8,4096]{3,2,1,0:T(8,128)(2,1)S(1)} %pad_maximum_fusion.1), channel_id=1, source_target_pairs={{0,8},{1,9},{2,10},{3,11},{4,12},{5,13},{6,14},{7,15},{8,0},{9,1},... | collective-permute-start | bytes 1572872 | tf_op jit(solution)/shard_map/ppermute | solution.py:42
  109.5 13.9 %collective-permute-start.37 = (bf16[4,2,8,4096]{3,2,1,0:T(8,128)(2,1)S(1)}, bf16[4,2,8,4096]{3,2,1,0:T(8,128)(2,1)S(1)}, u32[]{:S(2)}, u32[]{:S(2)}) collective-permute-start(bf16[4,2,8,4096]{3,2,1,0:T(8,128)(2,1)S(1)} %pad_maximum_fusion.2), channel_id=1, source_target_pairs={{0,12},{1,13},{2,14},{3,15},{4,0},{5,1},{6,2},{7,3},{8,4},{9,5},{1... | collective-permute-start | bytes 1572872 | tf_op jit(solution)/shard_map/ppermute | solution.py:42
  113.2 10.4 %collective-permute-start.36 = (bf16[4,2,8,4096]{3,2,1,0:T(8,128)(2,1)S(1)}, bf16[4,2,8,4096]{3,2,1,0:T(8,128)(2,1)S(1)}, u32[]{:S(2)}, u32[]{:S(2)}) collective-permute-start(bf16[4,2,8,4096]{3,2,1,0:T(8,128)(2,1)S(1)} %pad_maximum_fusion.2), channel_id=1, source_target_pairs={{0,4},{1,5},{2,6},{3,7},{4,8},{5,9},{6,10},{7,11},{8,12},{9,13},{1... | collective-permute-start | bytes 1572872 | tf_op jit(solution)/shard_map/ppermute | solution.py:42
  115.6 7.7 %collective-permute-start.30 = (bf16[4,4,8,1024]{3,2,1,0:T(8,128)(2,1)S(1)}, bf16[4,4,8,1024]{3,2,1,0:T(8,128)(2,1)S(1)}, u32[]{:S(2)}, u32[]{:S(2)}) collective-permute-start(bf16[4,4,8,1024]{3,2,1,0:T(8,128)(2,1)S(1)} %get-tuple-element.76), channel_id=1, source_target_pairs={{0,96},{1,97},{2,98},{3,99},{4,100},{5,101},{6,102},{7,103},{8,104... | collective-permute-start | bytes 786440 | tf_op jit(solution)/shard_map/ppermute | solution.py:42
  115.7 7.6 %collective-permute-start.31 = (bf16[4,4,8,1024]{3,2,1,0:T(8,128)(2,1)S(1)}, bf16[4,4,8,1024]{3,2,1,0:T(8,128)(2,1)S(1)}, u32[]{:S(2)}, u32[]{:S(2)}) collective-permute-start(bf16[4,4,8,1024]{3,2,1,0:T(8,128)(2,1)S(1)} %get-tuple-element.75), channel_id=1, source_target_pairs={{0,32},{1,33},{2,34},{3,35},{4,36},{5,37},{6,38},{7,39},{8,40},{9,... | collective-permute-start | bytes 786440 | tf_op jit(solution)/shard_map/ppermute | solution.py:42
  119.0 15.6 %collective-permute-start.39 = (bf16[4,2,8,4096]{3,2,1,0:T(8,128)(2,1)S(1)}, bf16[4,2,8,4096]{3,2,1,0:T(8,128)(2,1)S(1)}, u32[]{:S(2)}, u32[]{:S(2)}) collective-permute-start(bf16[4,2,8,4096]{3,2,1,0:T(8,128)(2,1)S(1)} %pad_maximum_fusion.2), channel_id=1, source_target_pairs={{0,8},{1,9},{2,10},{3,11},{4,12},{5,13},{6,14},{7,15},{8,0},{9,1},... | collective-permute-start | bytes 1572872 | tf_op jit(solution)/shard_map/ppermute | solution.py:42
  125.5 16.6 %collective-permute-start.38 = (bf16[3,4,8,1024]{3,2,1,0:T(8,128)(2,1)S(1)}, bf16[3,4,8,1024]{3,2,1,0:T(8,128)(2,1)S(1)}, u32[]{:S(2)}, u32[]{:S(2)}) collective-permute-start(bf16[3,4,8,1024]{3,2,1,0:T(8,128)(2,1)S(1)} %fusion.44), channel_id=1, source_target_pairs={{0,64},{1,65},{2,66},{3,67},{4,68},{5,69},{6,70},{7,71},{8,72},{9,... | collective-permute-start | bytes 589832 | tf_op jit(solution)/shard_map/ppermute | solution.py:42
  136.2 5.8 %collective-permute-start.40 = (bf16[1,4,8,1024]{3,2,1,0:T(8,128)(2,1)S(1)}, bf16[1,4,8,1024]{3,2,1,0:T(8,128)(2,1)S(1)}, u32[]{:S(2)}, u32[]{:S(2)}) collective-permute-start(bf16[1,4,8,1024]{3,2,1,0:T(8,128)(2,1)S(1)} %fusion.51), channel_id=1, source_target_pairs={{0,64},{1,65},{2,66},{3,67},{4,68},{5,69},{6,70},{7,71},{8,72},{9,... | collective-permute-start | bytes 196616 | tf_op jit(solution)/shard_map/ppermute | solution.py:42
  (6 other events, 8.5 us)

commit v4 on v3

--- a/solution.py
+++ b/solution.py
@@ -240,6 +240,7 @@
         in_specs=[pl.BlockSpec(memory_space=pltpu.SMEM)]
         + [pl.BlockSpec(memory_space=pltpu.VMEM)] * len(terms),
         out_specs=pl.BlockSpec(memory_space=pltpu.VMEM),
+        compiler_params=pltpu.CompilerParams(vmem_limit_bytes=6 * 2**20),
         cost_estimate=pl.CostEstimate(flops=2**19, bytes_accessed=2**21, transcendentals=0),
         name="add_up",
     )(place, *terms)

time: 146 us -> 143 us (0.979)
  local copies, waits for them, and re-layouts: 11.1 us -> 8.4 us
    unnamed x31 -> x25, local copies, waits for them, and re-layouts: 8.06 us -> 6.74 us
  transfers between devices with their start and end apart: 41 -> 41, of which waited for: 15 -> 15; matrix products, arithmetic and copies ran while one was open for 18% -> 17% of each run, Pallas kernels for 8% -> 9%
where the time goes in v4:
time: 143 us
  starting transfers between devices  61.9 us (43%)
  waiting for transfers between devices  40.6 us (28%)
  Pallas kernels  13.5 us (9%)
  matrix products  11.6 us (8%)
  local copies, waits for them, and re-layouts  8.4 us (6%)
  other arithmetic  5.26 us (4%)
    ppermute x41, starting transfers between devices, permute(): return lax.ppermute(value, AXES, pairs)  61.9 us
    ppermute x41, waiting for transfers between devices, permute(): return lax.ppermute(value, AXES, pairs)  40.6 us
    pallas_call x2, Pallas kernels, attention(): pl.pallas_call(attention_kernel, out_shape=(jax.ShapeDtypeStruct((steps,...  10.4 us
    unnamed x25, local copies, waits for them, and re-layouts  6.74 us
    dot_general x3, matrix products, project(): terms = jnp.dot(rows, w_output, preferred_element_type=jnp.float32)  5.9 us
    dot_general x4, matrix products, sum_over_plane(): value = jnp.dot(value, weights, preferred_element_type=jnp.float32)  5.71 us
  transfers between devices with their start and end apart: 41, of which 15 were waited for; matrix products, arithmetic and copies ran while one was open for 17% of the time, Pallas kernels for 9%

profile of v4, /device:TPU:6, one launch (start us, length us, event | category | flops | bytes accessed | tf_op | source)
XLA Modules:
  0.0 142.6 jit_solution(16886004538931702241)
XLA Ops:
  1.3 1.8 %order_rows.1 = bf16[4,4,8,1024]{3,2,1,0:T(8,128)(2,1)} custom-call(s32[3]{0:T(128)} %pad_add_fusion.place, bf16[16,8,1024]{2,1,0:T(8,128)(2,1)} %bitcast.99), custom_call_target="tpu_custom_call" | custom-call | bytes 524288 | tf_op jit(solution)/shard_map/order_rows/pallas_call | solution.py:76
  3.5 1.6 %collective-permute-start.3 = (bf16[4,4,8,1024]{3,2,1,0:T(8,128)(2,1)}, bf16[4,4,8,1024]{3,2,1,0:T(8,128)(2,1)S(1)}, u32[]{:S(2)}, u32[]{:S(2)}) collective-permute-start(bf16[4,4,8,1024]{3,2,1,0:T(8,128)(2,1)} %order_rows.1), channel_id=1, source_target_pairs={{0,96},{1,97},{2,98},{3,99},{4,100},{5,101},{6,102},{7,103},{8,104... | collective-permute-start | bytes 786440 | tf_op jit(solution)/shard_map/ppermute | solution.py:42
  5.1 1.1 pad_maximum_fusion
  7.3 2.7 %constant_dynamic-update-slice_fusion.4 = bf16[1024,4608]{1,0:T(8,128)(2,1)S(1)} fusion(bf16[1024,2048]{1,0:T(8,128)(2,1)} %param.10), kind=kLoop, calls=%fused_computation.94 | loop fusion | bytes 8388608
  12.0 1.3 collective-permute-done.3
  13.3 1.3 collective-permute-start.15
  14.6 2.5 %constant_dynamic-update-slice_fusion.1 = bf16[1024,4608]{1,0:T(8,128)(2,1)S(1)} fusion(bf16[1024,4608]{1,0:T(8,128)(2,1)S(1)} %constant_dynamic-update-slice_fusion.2, bf16[1024,2048]{1,0:T(8,128)(2,1)} %collective-permute-done.1), kind=kLoop, calls=%fused_computation.91 | loop fusion | bytes 8388608
  17.3 1.4 %fusion.2 = f16[128,4608]{1,0:T(8,128)(2,1)S(1)} fusion(bf16[1024,4608]{1,0:T(8,128)(2,1)S(1)} %constant_dynamic-update-slice_fusion, bf16[64,1024]{1,0:T(8,128)(2,1)S(1)} %bitcast.89, bf16[64,1024]{1,0:T(8,128)(2,1)S(1)} %bitcast.90), kind=kOutput, calls=%fused_computation.6 | convolution fusion | flops 1209663488 | bytes 10878976 | tf_op jit(solution)/shard_map/dot_general | solution.py:104
  19.0 3.3 %collective-permute-start.7 = (f16[64,4608]{1,0:T(8,128)(2,1)S(1)}, f16[64,4608]{1,0:T(8,128)(2,1)S(1)}, u32[]{:S(2)}, u32[]{:S(2)}) collective-permute-start(f16[64,4608]{1,0:T(8,128)(2,1)S(1)} %get-tuple-element.66), channel_id=1, source_target_pairs={{0,2},{1,3},{2,0},{3,1},{4,6},{5,7},{6,4},{7,5},{8,10},{9,11},{10,... | collective-permute-start | bytes 1769480 | tf_op jit(solution)/shard_map/ppermute | solution.py:42
  22.3 1.4 fusion.3
  23.9 1.1 collective-permute-start.6
  26.1 1.4 %fusion.4 = f16[128,4608]{1,0:T(8,128)(2,1)S(1)} fusion(bf16[1024,4608]{1,0:T(8,128)(2,1)S(1)} %constant_dynamic-update-slice_fusion, bf16[64,1024]{1,0:T(8,128)(2,1)S(1)} %bitcast.84, bf16[64,1024]{1,0:T(8,128)(2,1)S(1)} %bitcast.86), kind=kOutput, calls=%fused_computation.8 | convolution fusion | flops 1209663488 | bytes 10878976 | tf_op jit(solution)/shard_map/dot_general | solution.py:104
  27.6 1.4 %fusion.5 = f16[128,4608]{1,0:T(8,128)(2,1)S(1)} fusion(bf16[1024,4608]{1,0:T(8,128)(2,1)S(1)} %constant_dynamic-update-slice_fusion, bf16[64,1024]{1,0:T(8,128)(2,1)S(1)} %bitcast.85, bf16[64,1024]{1,0:T(8,128)(2,1)S(1)} %bitcast.87), kind=kOutput, calls=%fused_computation.9 | convolution fusion | flops 1209663488 | bytes 10878976 | tf_op jit(solution)/shard_map/dot_general | solution.py:104
  29.4 1.1 collective-permute-done.7
  30.5 3.2 %collective-permute-start.18 = (f16[64,4608]{1,0:T(8,128)(2,1)S(1)}, f16[64,4608]{1,0:T(8,128)(2,1)S(1)}, u32[]{:S(2)}, u32[]{:S(2)}) collective-permute-start(f16[64,4608]{1,0:T(8,128)(2,1)S(1)} %get-tuple-element.41), channel_id=1, source_target_pairs={{0,2},{1,3},{2,0},{3,1},{4,6},{5,7},{6,4},{7,5},{8,10},{9,11},{10,... | collective-permute-start | bytes 1769480 | tf_op jit(solution)/shard_map/ppermute | solution.py:42
  33.7 3.4 %collective-permute-done.6 = f16[64,4608]{1,0:T(8,128)(2,1)S(1)} collective-permute-done((f16[64,4608]{1,0:T(8,128)(2,1)S(1)}, f16[64,4608]{1,0:T(8,128)(2,1)S(1)}, u32[]{:S(2)}, u32[]{:S(2)}) %collective-permute-start.6) | collective-permute-done | bytes 589856 | tf_op jit(solution)/shard_map/ppermute | solution.py:42
  37.1 2.6 %collective-permute-start.17 = (f16[64,4608]{1,0:T(8,128)(2,1)S(1)}, f16[64,4608]{1,0:T(8,128)(2,1)}, u32[]{:S(2)}, u32[]{:S(2)}) collective-permute-start(f16[64,4608]{1,0:T(8,128)(2,1)S(1)} %get-tuple-element.40), channel_id=1, source_target_pairs={{0,3},{1,0},{2,1},{3,2},{4,7},{5,4},{6,5},{7,6},{8,11},{9,8},{10,9... | collective-permute-start | bytes 1769480 | tf_op jit(solution)/shard_map/ppermute | solution.py:42
  40.7 4.1 %collective-permute-start.10 = (f16[16,4608]{1,0:T(8,128)(2,1)S(1)}, f16[16,4608]{1,0:T(8,128)(2,1)S(1)}, u32[]{:S(2)}, u32[]{:S(2)}) collective-permute-start(f16[16,4608]{1,0:T(8,128)(2,1)S(1)} %get-tuple-element.73), channel_id=1, source_target_pairs={{0,12},{1,13},{2,14},{3,15},{4,0},{5,1},{6,2},{7,3},{8,4},{9,5},{1... | collective-permute-start | bytes 442376 | tf_op jit(solution)/shard_map/ppermute | solution.py:42
  44.8 2.1 %collective-permute-start.8 = (f16[16,4608]{1,0:T(8,128)(2,1)S(1)}, f16[16,4608]{1,0:T(8,128)(2,1)S(1)}, u32[]{:S(2)}, u32[]{:S(2)}) collective-permute-start(f16[16,4608]{1,0:T(8,128)(2,1)S(1)} %get-tuple-element.72), channel_id=1, source_target_pairs={{0,8},{1,9},{2,10},{3,11},{4,12},{5,13},{6,14},{7,15},{8,0},{9,1},... | collective-permute-start | bytes 442376 | tf_op jit(solution)/shard_map/ppermute | solution.py:42
  46.9 6.1 %collective-permute-done.17 = f16[64,4608]{1,0:T(8,128)(2,1)} collective-permute-done((f16[64,4608]{1,0:T(8,128)(2,1)S(1)}, f16[64,4608]{1,0:T(8,128)(2,1)}, u32[]{:S(2)}, u32[]{:S(2)}) %collective-permute-start.17) | collective-permute-done | bytes 589856 | tf_op jit(solution)/shard_map/ppermute | solution.py:42
  53.0 1.1 collective-permute-done.16
  54.1 1.7 %fusion.60 = (f16[64,4608]{1,0:T(8,128)(2,1)S(1)}, f32[64,4608]{1,0:T(8,128)S(1)}) fusion(f16[64,4608]{1,0:T(8,128)(2,1)S(1)} %collective-permute-done.18, f16[64,4608]{1,0:T(8,128)(2,1)} %collective-permute-done.17, f16[64,4608]{1,0:T(8,128)(2,1)} %collective-permute-done.16, f16[64,4608]{1,0:T(8,128)(2,1)S(1)} %get-tuple-element.38), kind=kLoop, calls=%fused_computation.116 | loop fusion | flops 2359296 | bytes 4128768 | tf_op jit(solution)/shard_map/convert.6
  55.9 4.1 %collective-permute-start.21 = (f16[16,4608]{1,0:T(8,128)(2,1)S(1)}, f16[16,4608]{1,0:T(8,128)(2,1)S(1)}, u32[]{:S(2)}, u32[]{:S(2)}) collective-permute-start(f16[16,4608]{1,0:T(8,128)(2,1)S(1)} %get-tuple-element.70), channel_id=1, source_target_pairs={{0,12},{1,13},{2,14},{3,15},{4,0},{5,1},{6,2},{7,3},{8,4},{9,5},{1... | collective-permute-start | bytes 442376 | tf_op jit(solution)/shard_map/ppermute | solution.py:42
  60.0 1.9 %collective-permute-start.19 = (f16[16,4608]{1,0:T(8,128)(2,1)S(1)}, f16[16,4608]{1,0:T(8,128)(2,1)S(1)}, u32[]{:S(2)}, u32[]{:S(2)}) collective-permute-start(f16[16,4608]{1,0:T(8,128)(2,1)S(1)} %get-tuple-element.69), channel_id=1, source_target_pairs={{0,8},{1,9},{2,10},{3,11},{4,12},{5,13},{6,14},{7,15},{8,0},{9,1},... | collective-permute-start | bytes 442376 | tf_op jit(solution)/shard_map/ppermute | solution.py:42
  62.0 1.9 %collective-permute-start.12 = (bf16[8,4608]{1,0:T(8,128)(2,1)S(1)}, bf16[8,4608]{1,0:T(8,128)(2,1)S(1)}, u32[]{:S(2)}, u32[]{:S(2)}) collective-permute-start(bf16[8,4608]{1,0:T(8,128)(2,1)S(1)} %get-tuple-element.88), channel_id=1, source_target_pairs={{0,32},{1,33},{2,34},{3,35},{4,36},{5,37},{6,38},{7,39},{8,40},{9,... | collective-permute-start | bytes 221192 | tf_op jit(solution)/shard_map/ppermute | solution.py:42
  64.1 3.9 %collective-permute-done.20 = f16[16,4608]{1,0:T(8,128)(2,1)S(1)} collective-permute-done((f16[16,4608]{1,0:T(8,128)(2,1)S(1)}, f16[16,4608]{1,0:T(8,128)(2,1)S(1)}, u32[]{:S(2)}, u32[]{:S(2)}) %collective-permute-start.20) | collective-permute-done | bytes 147488 | tf_op jit(solution)/shard_map/ppermute | solution.py:42
  68.1 2.4 %collective-permute-start.22 = (bf16[8,4608]{1,0:T(8,128)(2,1)S(1)}, bf16[8,4608]{1,0:T(8,128)(2,1)S(1)}, u32[]{:S(2)}, u32[]{:S(2)}) collective-permute-start(bf16[8,4608]{1,0:T(8,128)(2,1)S(1)} %get-tuple-element.86), channel_id=1, source_target_pairs={{0,64},{1,65},{2,66},{3,67},{4,68},{5,69},{6,70},{7,71},{8,72},{9,... | collective-permute-start | bytes 221192 | tf_op jit(solution)/shard_map/ppermute | solution.py:42
  70.6 5.2 %attention.2 = (bf16[2,8,4096]{2,1,0:T(8,128)(2,1)S(1)}, bf16[8,1024]{1,0:T(8,128)(2,1)}, bf16[8,1024]{1,0:T(8,128)(2,1)}) custom-call(s32[3]{0:T(128)S(1)} %pad_add_fusion.1.place, bf16[2,8,4608]{2,1,0:T(8,128)(2,1)S(1)} %pad_maximum_fusion.3.q_ref, f32[8,128]{1,0:T(8,128)S(1)} %get-tuple-element.96.cos_ref, f32[8,128]{1,0:T(8,128)S(1)} %get-tuple-element.97.sin_ref, ...), custom_call_target="tpu_custom_call" | custom-call | flops 117440512 | bytes 7340032 | tf_op jit(solution)/shard_map/attention/pallas_call | solution.py:187
  76.2 2.9 %collective-permute-start.13 = (bf16[8,4096]{1,0:T(8,128)(2,1)S(1)}, bf16[8,4096]{1,0:T(8,128)(2,1)S(1)}, u32[]{:S(2)}, u32[]{:S(2)}) collective-permute-start(bf16[8,4096]{1,0:T(8,128)(2,1)S(1)} %get-tuple-element.91), channel_id=1, source_target_pairs={{0,32},{1,33},{2,34},{3,35},{4,36},{5,37},{6,38},{7,39},{8,40},{9,... | collective-permute-start | bytes 196616 | tf_op jit(solution)/shard_map/ppermute | solution.py:42
  79.1 5.2 %attention.3 = (bf16[2,8,4096]{2,1,0:T(8,128)(2,1)S(1)}, bf16[8,1024]{1,0:T(8,128)(2,1)}, bf16[8,1024]{1,0:T(8,128)(2,1)}) custom-call(s32[3]{0:T(128)S(1)} %pad_add_fusion.2.place, bf16[2,8,4608]{2,1,0:T(8,128)(2,1)S(1)} %pad_maximum_fusion.4.q_ref, f32[8,128]{1,0:T(8,128)S(1)} %get-tuple-element.96.cos_ref, ...), custom_call_target="tpu_custom_call", output_to_operand_aliasing={{1}: (7, {}), {2}: (8, {})} | custom-call | flops 117440512 | bytes 7340032 | tf_op jit(solution)/shard_map/attention/pallas_call | solution.py:187
  85.6 1.6 %collective-permute-start.26 = (bf16[2,8,4096]{2,1,0:T(8,128)(2,1)S(1)}, bf16[2,8,4096]{2,1,0:T(8,128)(2,1)S(1)}, u32[]{:S(2)}, u32[]{:S(2)}) collective-permute-start(bf16[2,8,4096]{2,1,0:T(8,128)(2,1)S(1)} %pad_maximum_fusion.7), channel_id=1, source_target_pairs={{0,3},{1,0},{2,1},{3,2},{4,7},{5,4},{6,5},{7,6},{8,11},{9,8},{10,9... | collective-permute-start | bytes 393224 | tf_op jit(solution)/shard_map/ppermute | solution.py:42
  88.8 1.7 %collective-permute-done.32 = bf16[8,4096]{1,0:T(8,128)(2,1)S(1)} collective-permute-done((bf16[8,4096]{1,0:T(8,128)(2,1)S(1)}, bf16[8,4096]{1,0:T(8,128)(2,1)S(1)}, u32[]{:S(2)}, u32[]{:S(2)}) %collective-permute-start.32) | collective-permute-done | bytes 65568 | tf_op jit(solution)/shard_map/ppermute | solution.py:42
  90.5 1.7 %collective-permute-start.35 = (bf16[2,8,4096]{2,1,0:T(8,128)(2,1)S(1)}, bf16[2,8,4096]{2,1,0:T(8,128)(2,1)S(1)}, u32[]{:S(2)}, u32[]{:S(2)}) collective-permute-start(bf16[2,8,4096]{2,1,0:T(8,128)(2,1)S(1)} %pad_maximum_fusion.8), channel_id=1, source_target_pairs={{0,3},{1,0},{2,1},{3,2},{4,7},{5,4},{6,5},{7,6},{8,11},{9,8},{10,9... | collective-permute-start | bytes 393224 | tf_op jit(solution)/shard_map/ppermute | solution.py:42
  93.7 1.3 collective-permute-done.24
  95.1 2.0 %collective-permute-start.29 = (bf16[4,2,8,4096]{3,2,1,0:T(8,128)(2,1)S(1)}, bf16[4,2,8,4096]{3,2,1,0:T(8,128)(2,1)S(1)}, u32[]{:S(2)}, u32[]{:S(2)}) collective-permute-start(bf16[4,2,8,4096]{3,2,1,0:T(8,128)(2,1)S(1)} %pad_maximum_fusion.1), channel_id=1, source_target_pairs={{0,12},{1,13},{2,14},{3,15},{4,0},{5,1},{6,2},{7,3},{8,4},{9,5},{1... | collective-permute-start | bytes 1572872 | tf_op jit(solution)/shard_map/ppermute | solution.py:42
  97.2 1.7 %collective-permute-start.28 = (bf16[4,2,8,4096]{3,2,1,0:T(8,128)(2,1)S(1)}, bf16[4,2,8,4096]{3,2,1,0:T(8,128)(2,1)S(1)}, u32[]{:S(2)}, u32[]{:S(2)}) collective-permute-start(bf16[4,2,8,4096]{3,2,1,0:T(8,128)(2,1)S(1)} %pad_maximum_fusion.1), channel_id=1, source_target_pairs={{0,8},{1,9},{2,10},{3,11},{4,12},{5,13},{6,14},{7,15},{8,0},{9,1},... | collective-permute-start | bytes 1572872 | tf_op jit(solution)/shard_map/ppermute | solution.py:42
  98.9 1.6 %collective-permute-done.33 = bf16[2,8,4096]{2,1,0:T(8,128)(2,1)S(1)} collective-permute-done((bf16[2,8,4096]{2,1,0:T(8,128)(2,1)S(1)}, bf16[2,8,4096]{2,1,0:T(8,128)(2,1)S(1)}, u32[]{:S(2)}, u32[]{:S(2)}) %collective-permute-start.33) | collective-permute-done | bytes 131104 | tf_op jit(solution)/shard_map/ppermute | solution.py:42
  100.6 8.9 %collective-permute-done.29 = bf16[4,2,8,4096]{3,2,1,0:T(8,128)(2,1)S(1)} collective-permute-done((bf16[4,2,8,4096]{3,2,1,0:T(8,128)(2,1)S(1)}, bf16[4,2,8,4096]{3,2,1,0:T(8,128)(2,1)S(1)}, u32[]{:S(2)}, u32[]{:S(2)}) %collective-permute-start.29) | collective-permute-done | bytes 524320 | tf_op jit(solution)/shard_map/ppermute | solution.py:42
  109.5 3.7 %collective-permute-start.37 = (bf16[4,2,8,4096]{3,2,1,0:T(8,128)(2,1)S(1)}, bf16[4,2,8,4096]{3,2,1,0:T(8,128)(2,1)S(1)}, u32[]{:S(2)}, u32[]{:S(2)}) collective-permute-start(bf16[4,2,8,4096]{3,2,1,0:T(8,128)(2,1)S(1)} %pad_maximum_fusion.2), channel_id=1, source_target_pairs={{0,12},{1,13},{2,14},{3,15},{4,0},{5,1},{6,2},{7,3},{8,4},{9,5},{1... | collective-permute-start | bytes 1572872 | tf_op jit(solution)/shard_map/ppermute | solution.py:42
  113.2 2.4 %fusion.6 = bf16[256,1024]{1,0:T(8,128)(2,1)S(1)} fusion(bf16[4096,1024]{1,0:T(8,128)(2,1)S(1)} %constant_dynamic-update-slice_fusion.5, bf16[64,4096]{1,0:T(8,128)(2,1)S(1)} %bitcast.117, bf16[64,4096]{1,0:T(8,128)(2,1)S(1)} %bitcast.120, bf16[64,4096]{1,0:T(8,128)(2,1)S(1)} %bitcast.119, bf16[64,4096]{1,0:T(8,128)(2,1)S(1)} %bitcast.93), kind=kOutput, calls=%fused_computation.10 | convolution fusion | flops 2155872256 | bytes 11010048 | tf_op jit(solution)/shard_map/dot_general | solution.py:251
  115.7 3.2 %collective-permute-start.31 = (bf16[4,4,8,1024]{3,2,1,0:T(8,128)(2,1)S(1)}, bf16[4,4,8,1024]{3,2,1,0:T(8,128)(2,1)S(1)}, u32[]{:S(2)}, u32[]{:S(2)}) collective-permute-start(bf16[4,4,8,1024]{3,2,1,0:T(8,128)(2,1)S(1)} %get-tuple-element.75), channel_id=1, source_target_pairs={{0,32},{1,33},{2,34},{3,35},{4,36},{5,37},{6,38},{7,39},{8,40},{9,... | collective-permute-start | bytes 786440 | tf_op jit(solution)/shard_map/ppermute | solution.py:42
  118.9 1.5 %collective-permute-start.39 = (bf16[4,2,8,4096]{3,2,1,0:T(8,128)(2,1)S(1)}, bf16[4,2,8,4096]{3,2,1,0:T(8,128)(2,1)S(1)}, u32[]{:S(2)}, u32[]{:S(2)}) collective-permute-start(bf16[4,2,8,4096]{3,2,1,0:T(8,128)(2,1)S(1)} %pad_maximum_fusion.2), channel_id=1, source_target_pairs={{0,8},{1,9},{2,10},{3,11},{4,12},{5,13},{6,14},{7,15},{8,0},{9,1},... | collective-permute-start | bytes 1572872 | tf_op jit(solution)/shard_map/ppermute | solution.py:42
  120.4 2.9 %collective-permute-done.30.refs_0_ = bf16[4,4,8,1024]{3,2,1,0:T(8,128)(2,1)S(1)} collective-permute-done((bf16[4,4,8,1024]{3,2,1,0:T(8,128)(2,1)S(1)}, bf16[4,4,8,1024]{3,2,1,0:T(8,128)(2,1)S(1)}, u32[]{:S(2)}, u32[]{:S(2)}) %collective-permute-start.30) | collective-permute-done | bytes 262176 | tf_op jit(solution)/shard_map/ppermute | solution.py:42
  123.5 1.9 %fusion.14 = f32[192,1024]{1,0:T(8,128)S(1)} fusion(bf16[4096,1024]{1,0:T(8,128)(2,1)S(1)} %constant_dynamic-update-slice_fusion.5, bf16[64,4096]{1,0:T(8,128)(2,1)S(1)} %bitcast.116, bf16[64,4096]{1,0:T(8,128)(2,1)S(1)} %bitcast.118, bf16[64,4096]{1,0:T(8,128)(2,1)S(1)} %bitcast.92), kind=kOutput, calls=%fused_computation.18 | convolution fusion | flops 1615331328 | bytes 10747904 | tf_op jit(solution)/shard_map/dot_general | solution.py:251
  125.4 8.3 %collective-permute-start.38 = (bf16[3,4,8,1024]{3,2,1,0:T(8,128)(2,1)S(1)}, bf16[3,4,8,1024]{3,2,1,0:T(8,128)(2,1)S(1)}, u32[]{:S(2)}, u32[]{:S(2)}) collective-permute-start(bf16[3,4,8,1024]{3,2,1,0:T(8,128)(2,1)S(1)} %fusion.44), channel_id=1, source_target_pairs={{0,64},{1,65},{2,66},{3,67},{4,68},{5,69},{6,70},{7,71},{8,72},{9,... | collective-permute-start | bytes 589832 | tf_op jit(solution)/shard_map/ppermute | solution.py:42
  133.8 1.6 %fusion.20 = f32[1,4,2,8,1024]{4,3,1,2,0:T(8,128)S(1)} fusion(bf16[4096,1024]{1,0:T(8,128)(2,1)S(1)} %constant_dynamic-update-slice_fusion.5, bf16[4,2,8,4096]{3,2,1,0:T(8,128)(2,1)S(1)} %collective-permute-done.39), kind=kOutput, calls=%fused_computation.26 | convolution fusion | flops 536870912 | bytes 9175040 | tf_op jit(solution)/shard_map/dot_general | solution.py:251
  135.5 5.7 %collective-permute-done.40.refs_5_ = bf16[1,4,8,1024]{3,2,1,0:T(8,128)(2,1)S(1)} collective-permute-done((bf16[1,4,8,1024]{3,2,1,0:T(8,128)(2,1)S(1)}, bf16[1,4,8,1024]{3,2,1,0:T(8,128)(2,1)S(1)}, u32[]{:S(2)}, u32[]{:S(2)}) %collective-permute-start.40) | collective-permute-done | bytes 65568 | tf_op jit(solution)/shard_map/ppermute | solution.py:42
  141.3 1.4 add_up.1
  (120 shorter events, 13.0 us)
Async XLA Ops:
  0.6 14.0 %collective-permute-start.1 = (bf16[1024,2048]{1,0:T(8,128)(2,1)}, bf16[1024,2048]{1,0:T(8,128)(2,1)}, u32[]{:S(2)}, u32[]{:S(2)}) collective-permute-start(bf16[1024,2048]{1,0:T(8,128)(2,1)} %param.10), channel_id=1, source_target_pairs={{0,16},{1,17},{2,18},{3,19},{4,20},{5,21},{6,22},{7,23},{8,24},{9,... | collective-permute-start | bytes 12582920 | tf_op jit(solution)/shard_map/ppermute | solution.py:42
  3.1 8.9 %collective-permute-start = (bf16[4,4,8,1024]{3,2,1,0:T(8,128)(2,1)}, bf16[4,4,8,1024]{3,2,1,0:T(8,128)(2,1)S(1)}, u32[]{:S(2)}, u32[]{:S(2)}) collective-permute-start(bf16[4,4,8,1024]{3,2,1,0:T(8,128)(2,1)} %order_rows.1), channel_id=1, source_target_pairs={{0,32},{1,33},{2,34},{3,35},{4,36},{5,37},{6,38},{7,39},{8,40},{9,... | collective-permute-start | bytes 786440 | tf_op jit(solution)/shard_map/ppermute | solution.py:42
  3.5 9.8 %collective-permute-start.3 = (bf16[4,4,8,1024]{3,2,1,0:T(8,128)(2,1)}, bf16[4,4,8,1024]{3,2,1,0:T(8,128)(2,1)S(1)}, u32[]{:S(2)}, u32[]{:S(2)}) collective-permute-start(bf16[4,4,8,1024]{3,2,1,0:T(8,128)(2,1)} %order_rows.1), channel_id=1, source_target_pairs={{0,96},{1,97},{2,98},{3,99},{4,100},{5,101},{6,102},{7,103},{8,104... | collective-permute-start | bytes 786440 | tf_op jit(solution)/shard_map/ppermute | solution.py:42
  6.2 11.0 %collective-permute-start.2 = (bf16[1024,256]{1,0:T(8,128)(2,1)S(1)}, bf16[1024,256]{1,0:T(8,128)(2,1)S(1)}, u32[]{:S(2)}, u32[]{:S(2)}) collective-permute-start(bf16[1024,256]{1,0:T(8,128)(2,1)S(1)} %pad_maximum_fusion), channel_id=1, source_target_pairs={{0,16},{1,17},{2,18},{3,19},{4,20},{5,21},{6,22},{7,23},{8,24},{9,... | collective-permute-start | bytes 1572872 | tf_op jit(solution)/shard_map/ppermute | solution.py:42
  7.3 2.8 %copy-start.4 = (bf16[1024,128]{1,0:T(8,128)(2,1)S(1)}, bf16[1024,128]{1,0:T(8,128)(2,1)}, u32[]{:S(2)}) copy-start(bf16[1024,128]{1,0:T(8,128)(2,1)} %param.12) | copy-start | bytes 786436
  7.3 3.6 %copy-start.1 = (bf16[2048,1024]{1,0:T(8,128)(2,1)S(1)}, bf16[2048,1024]{1,0:T(8,128)(2,1)}, u32[]{:S(2)}) copy-start(bf16[2048,1024]{1,0:T(8,128)(2,1)} %param.13) | copy-start | bytes 12582916
  13.3 12.7 %collective-permute-start.15 = (bf16[4,4,8,1024]{3,2,1,0:T(8,128)(2,1)S(1)}, bf16[4,4,8,1024]{3,2,1,0:T(8,128)(2,1)S(1)}, u32[]{:S(2)}, u32[]{:S(2)}) collective-permute-start(bf16[4,4,8,1024]{3,2,1,0:T(8,128)(2,1)S(1)} %copy-done.2), channel_id=1, source_target_pairs={{0,64},{1,65},{2,66},{3,67},{4,68},{5,69},{6,70},{7,71},{8,72},{9,... | collective-permute-start | bytes 786440 | tf_op jit(solution)/shard_map/ppermute | solution.py:42
  14.6 25.2 %collective-permute-start.4 = (bf16[2048,1024]{1,0:T(8,128)(2,1)S(1)}, bf16[2048,1024]{1,0:T(8,128)(2,1)S(1)}, u32[]{:S(2)}, u32[]{:S(2)}) collective-permute-start(bf16[2048,1024]{1,0:T(8,128)(2,1)S(1)} %copy-done.1), channel_id=1, source_target_pairs={{0,16},{1,17},{2,18},{3,19},{4,20},{5,21},{6,22},{7,23},{8,24},{9,... | collective-permute-start | bytes 12582920 | tf_op jit(solution)/shard_map/ppermute | solution.py:42
  19.0 11.5 %collective-permute-start.7 = (f16[64,4608]{1,0:T(8,128)(2,1)S(1)}, f16[64,4608]{1,0:T(8,128)(2,1)S(1)}, u32[]{:S(2)}, u32[]{:S(2)}) collective-permute-start(f16[64,4608]{1,0:T(8,128)(2,1)S(1)} %get-tuple-element.66), channel_id=1, source_target_pairs={{0,2},{1,3},{2,0},{3,1},{4,6},{5,7},{6,4},{7,5},{8,10},{9,11},{10,... | collective-permute-start | bytes 1769480 | tf_op jit(solution)/shard_map/ppermute | solution.py:42
  23.9 13.2 %collective-permute-start.6 = (f16[64,4608]{1,0:T(8,128)(2,1)S(1)}, f16[64,4608]{1,0:T(8,128)(2,1)S(1)}, u32[]{:S(2)}, u32[]{:S(2)}) collective-permute-start(f16[64,4608]{1,0:T(8,128)(2,1)S(1)} %get-tuple-element.68), channel_id=1, source_target_pairs={{0,3},{1,0},{2,1},{3,2},{4,7},{5,4},{6,5},{7,6},{8,11},{9,8},{10,9... | collective-permute-start | bytes 1769480 | tf_op jit(solution)/shard_map/ppermute | solution.py:42
  25.0 14.7 %collective-permute-start.5 = (f16[64,4608]{1,0:T(8,128)(2,1)S(1)}, f16[64,4608]{1,0:T(8,128)(2,1)S(1)}, u32[]{:S(2)}, u32[]{:S(2)}) collective-permute-start(f16[64,4608]{1,0:T(8,128)(2,1)S(1)} %get-tuple-element.67), channel_id=1, source_target_pairs={{0,1},{1,2},{2,3},{3,0},{4,5},{5,6},{6,7},{7,4},{8,9},{9,10},{10,1... | collective-permute-start | bytes 1769480 | tf_op jit(solution)/shard_map/ppermute | solution.py:42
  30.5 14.3 %collective-permute-start.18 = (f16[64,4608]{1,0:T(8,128)(2,1)S(1)}, f16[64,4608]{1,0:T(8,128)(2,1)S(1)}, u32[]{:S(2)}, u32[]{:S(2)}) collective-permute-start(f16[64,4608]{1,0:T(8,128)(2,1)S(1)} %get-tuple-element.41), channel_id=1, source_target_pairs={{0,2},{1,3},{2,0},{3,1},{4,6},{5,7},{6,4},{7,5},{8,10},{9,11},{10,... | collective-permute-start | bytes 1769480 | tf_op jit(solution)/shard_map/ppermute | solution.py:42
  37.1 15.9 %collective-permute-start.17 = (f16[64,4608]{1,0:T(8,128)(2,1)S(1)}, f16[64,4608]{1,0:T(8,128)(2,1)}, u32[]{:S(2)}, u32[]{:S(2)}) collective-permute-start(f16[64,4608]{1,0:T(8,128)(2,1)S(1)} %get-tuple-element.40), channel_id=1, source_target_pairs={{0,3},{1,0},{2,1},{3,2},{4,7},{5,4},{6,5},{7,6},{8,11},{9,8},{10,9... | collective-permute-start | bytes 1769480 | tf_op jit(solution)/shard_map/ppermute | solution.py:42
  39.8 14.4 %collective-permute-start.16 = (f16[64,4608]{1,0:T(8,128)(2,1)S(1)}, f16[64,4608]{1,0:T(8,128)(2,1)}, u32[]{:S(2)}, u32[]{:S(2)}) collective-permute-start(f16[64,4608]{1,0:T(8,128)(2,1)S(1)} %get-tuple-element.39), channel_id=1, source_target_pairs={{0,1},{1,2},{2,3},{3,0},{4,5},{5,6},{6,7},{7,4},{8,9},{9,10},{10,1... | collective-permute-start | bytes 1769480 | tf_op jit(solution)/shard_map/ppermute | solution.py:42
  39.8 30.7 %slice-start = ((s8[7340032]{0:T(1024)(128)(4,1)}), s8[4194304]{0:T(1024)(128)(4,1)S(1)}, s32[]{:S(2)}) async-start(s8[7340032]{0:T(1024)(128)(4,1)} %bitcast.79), calls=%async_computation | async-start | bytes 8388608
  39.8 30.7 %slice-start.2 = ((s8[7340032]{0:T(1024)(128)(4,1)}), s8[4194304]{0:T(1024)(128)(4,1)S(1)}, s32[]{:S(2)}) async-start(s8[7340032]{0:T(1024)(128)(4,1)} %bitcast.81), calls=%async_computation.2 | async-start | bytes 8388608
  40.2 30.3 %slice-start.1 = ((s8[7340032]{0:T(1024)(128)(4,1)}), s8[3145728]{0:T(1024)(128)(4,1)S(1)}, s32[]{:S(2)}) async-start(s8[7340032]{0:T(1024)(128)(4,1)} %bitcast.79), calls=%async_computation.1 | async-start | bytes 6291456
  40.3 30.3 %slice-start.3 = ((s8[7340032]{0:T(1024)(128)(4,1)}), s8[3145728]{0:T(1024)(128)(4,1)S(1)}, s32[]{:S(2)}) async-start(s8[7340032]{0:T(1024)(128)(4,1)} %bitcast.81), calls=%async_computation.3 | async-start | bytes 6291456
  40.7 19.3 %collective-permute-start.10 = (f16[16,4608]{1,0:T(8,128)(2,1)S(1)}, f16[16,4608]{1,0:T(8,128)(2,1)S(1)}, u32[]{:S(2)}, u32[]{:S(2)}) collective-permute-start(f16[16,4608]{1,0:T(8,128)(2,1)S(1)} %get-tuple-element.73), channel_id=1, source_target_pairs={{0,12},{1,13},{2,14},{3,15},{4,0},{5,1},{6,2},{7,3},{8,4},{9,5},{1... | collective-permute-start | bytes 442376 | tf_op jit(solution)/shard_map/ppermute | solution.py:42
  44.8 17.1 %collective-permute-start.9 = (f16[16,4608]{1,0:T(8,128)(2,1)S(1)}, f16[16,4608]{1,0:T(8,128)(2,1)S(1)}, u32[]{:S(2)}, u32[]{:S(2)}) collective-permute-start(f16[16,4608]{1,0:T(8,128)(2,1)S(1)} %get-tuple-element.74), channel_id=1, source_target_pairs={{0,4},{1,5},{2,6},{3,7},{4,8},{5,9},{6,10},{7,11},{8,12},{9,13},{1... | collective-permute-start | bytes 442376 | tf_op jit(solution)/shard_map/ppermute | solution.py:42
  44.8 17.1 %collective-permute-start.8 = (f16[16,4608]{1,0:T(8,128)(2,1)S(1)}, f16[16,4608]{1,0:T(8,128)(2,1)S(1)}, u32[]{:S(2)}, u32[]{:S(2)}) collective-permute-start(f16[16,4608]{1,0:T(8,128)(2,1)S(1)} %get-tuple-element.72), channel_id=1, source_target_pairs={{0,8},{1,9},{2,10},{3,11},{4,12},{5,13},{6,14},{7,15},{8,0},{9,1},... | collective-permute-start | bytes 442376 | tf_op jit(solution)/shard_map/ppermute | solution.py:42
  55.9 8.2 %collective-permute-start.21 = (f16[16,4608]{1,0:T(8,128)(2,1)S(1)}, f16[16,4608]{1,0:T(8,128)(2,1)S(1)}, u32[]{:S(2)}, u32[]{:S(2)}) collective-permute-start(f16[16,4608]{1,0:T(8,128)(2,1)S(1)} %get-tuple-element.70), channel_id=1, source_target_pairs={{0,12},{1,13},{2,14},{3,15},{4,0},{5,1},{6,2},{7,3},{8,4},{9,5},{1... | collective-permute-start | bytes 442376 | tf_op jit(solution)/shard_map/ppermute | solution.py:42
  60.0 7.9 %collective-permute-start.20 = (f16[16,4608]{1,0:T(8,128)(2,1)S(1)}, f16[16,4608]{1,0:T(8,128)(2,1)S(1)}, u32[]{:S(2)}, u32[]{:S(2)}) collective-permute-start(f16[16,4608]{1,0:T(8,128)(2,1)S(1)} %get-tuple-element.71), channel_id=1, source_target_pairs={{0,4},{1,5},{2,6},{3,7},{4,8},{5,9},{6,10},{7,11},{8,12},{9,13},{1... | collective-permute-start | bytes 442376 | tf_op jit(solution)/shard_map/ppermute | solution.py:42
  60.0 7.9 %collective-permute-start.19 = (f16[16,4608]{1,0:T(8,128)(2,1)S(1)}, f16[16,4608]{1,0:T(8,128)(2,1)S(1)}, u32[]{:S(2)}, u32[]{:S(2)}) collective-permute-start(f16[16,4608]{1,0:T(8,128)(2,1)S(1)} %get-tuple-element.69), channel_id=1, source_target_pairs={{0,8},{1,9},{2,10},{3,11},{4,12},{5,13},{6,14},{7,15},{8,0},{9,1},... | collective-permute-start | bytes 442376 | tf_op jit(solution)/shard_map/ppermute | solution.py:42
  62.0 8.5 %collective-permute-start.12 = (bf16[8,4608]{1,0:T(8,128)(2,1)S(1)}, bf16[8,4608]{1,0:T(8,128)(2,1)S(1)}, u32[]{:S(2)}, u32[]{:S(2)}) collective-permute-start(bf16[8,4608]{1,0:T(8,128)(2,1)S(1)} %get-tuple-element.88), channel_id=1, source_target_pairs={{0,32},{1,33},{2,34},{3,35},{4,36},{5,37},{6,38},{7,39},{8,40},{9,... | collective-permute-start | bytes 221192 | tf_op jit(solution)/shard_map/ppermute | solution.py:42
  63.9 6.6 %collective-permute-start.11 = (bf16[8,4608]{1,0:T(8,128)(2,1)S(1)}, bf16[8,4608]{1,0:T(8,128)(2,1)S(1)}, u32[]{:S(2)}, u32[]{:S(2)}) collective-permute-start(bf16[8,4608]{1,0:T(8,128)(2,1)S(1)} %get-tuple-element.87), channel_id=1, source_target_pairs={{0,96},{1,97},{2,98},{3,99},{4,100},{5,101},{6,102},{7,103},{8,104... | collective-permute-start | bytes 221192 | tf_op jit(solution)/shard_map/ppermute | solution.py:42
  68.1 11.0 %collective-permute-start.22 = (bf16[8,4608]{1,0:T(8,128)(2,1)S(1)}, bf16[8,4608]{1,0:T(8,128)(2,1)S(1)}, u32[]{:S(2)}, u32[]{:S(2)}) collective-permute-start(bf16[8,4608]{1,0:T(8,128)(2,1)S(1)} %get-tuple-element.86), channel_id=1, source_target_pairs={{0,64},{1,65},{2,66},{3,67},{4,68},{5,69},{6,70},{7,71},{8,72},{9,... | collective-permute-start | bytes 221192 | tf_op jit(solution)/shard_map/ppermute | solution.py:42
  75.8 8.7 %collective-permute-start.14 = (bf16[8,4096]{1,0:T(8,128)(2,1)S(1)}, bf16[8,4096]{1,0:T(8,128)(2,1)S(1)}, u32[]{:S(2)}, u32[]{:S(2)}) collective-permute-start(bf16[8,4096]{1,0:T(8,128)(2,1)S(1)} %get-tuple-element.92), channel_id=1, source_target_pairs={{0,96},{1,97},{2,98},{3,99},{4,100},{5,101},{6,102},{7,103},{8,104... | collective-permute-start | bytes 196616 | tf_op jit(solution)/shard_map/ppermute | solution.py:42
  76.2 8.4 %collective-permute-start.13 = (bf16[8,4096]{1,0:T(8,128)(2,1)S(1)}, bf16[8,4096]{1,0:T(8,128)(2,1)S(1)}, u32[]{:S(2)}, u32[]{:S(2)}) collective-permute-start(bf16[8,4096]{1,0:T(8,128)(2,1)S(1)} %get-tuple-element.91), channel_id=1, source_target_pairs={{0,32},{1,33},{2,34},{3,35},{4,36},{5,37},{6,38},{7,39},{8,40},{9,... | collective-permute-start | bytes 196616 | tf_op jit(solution)/shard_map/ppermute | solution.py:42
  84.3 1.2 collective-permute-start.23
  84.4 6.0 %collective-permute-start.32 = (bf16[8,4096]{1,0:T(8,128)(2,1)S(1)}, bf16[8,4096]{1,0:T(8,128)(2,1)S(1)}, u32[]{:S(2)}, u32[]{:S(2)}) collective-permute-start(bf16[8,4096]{1,0:T(8,128)(2,1)S(1)} %get-tuple-element.90), channel_id=1, source_target_pairs={{0,64},{1,65},{2,66},{3,67},{4,68},{5,69},{6,70},{7,71},{8,72},{9,... | collective-permute-start | bytes 196616 | tf_op jit(solution)/shard_map/ppermute | solution.py:42
  85.6 7.3 %collective-permute-start.26 = (bf16[2,8,4096]{2,1,0:T(8,128)(2,1)S(1)}, bf16[2,8,4096]{2,1,0:T(8,128)(2,1)S(1)}, u32[]{:S(2)}, u32[]{:S(2)}) collective-permute-start(bf16[2,8,4096]{2,1,0:T(8,128)(2,1)S(1)} %pad_maximum_fusion.7), channel_id=1, source_target_pairs={{0,3},{1,0},{2,1},{3,2},{4,7},{5,4},{6,5},{7,6},{8,11},{9,8},{10,9... | collective-permute-start | bytes 393224 | tf_op jit(solution)/shard_map/ppermute | solution.py:42
  87.2 6.6 %collective-permute-start.25 = (bf16[2,8,4096]{2,1,0:T(8,128)(2,1)S(1)}, bf16[2,8,4096]{2,1,0:T(8,128)(2,1)S(1)}, u32[]{:S(2)}, u32[]{:S(2)}) collective-permute-start(bf16[2,8,4096]{2,1,0:T(8,128)(2,1)S(1)} %pad_maximum_fusion.7), channel_id=1, source_target_pairs={{0,2},{1,3},{2,0},{3,1},{4,6},{5,7},{6,4},{7,5},{8,10},{9,11},{10,... | collective-permute-start | bytes 393224 | tf_op jit(solution)/shard_map/ppermute | solution.py:42
  87.9 7.1 %collective-permute-start.24 = (bf16[2,8,4096]{2,1,0:T(8,128)(2,1)S(1)}, bf16[2,8,4096]{2,1,0:T(8,128)(2,1)S(1)}, u32[]{:S(2)}, u32[]{:S(2)}) collective-permute-start(bf16[2,8,4096]{2,1,0:T(8,128)(2,1)S(1)} %pad_maximum_fusion.7), channel_id=1, source_target_pairs={{0,1},{1,2},{2,3},{3,0},{4,5},{5,6},{6,7},{7,4},{8,9},{9,10},{10,1... | collective-permute-start | bytes 393224 | tf_op jit(solution)/shard_map/ppermute | solution.py:42
  90.5 6.7 %collective-permute-start.35 = (bf16[2,8,4096]{2,1,0:T(8,128)(2,1)S(1)}, bf16[2,8,4096]{2,1,0:T(8,128)(2,1)S(1)}, u32[]{:S(2)}, u32[]{:S(2)}) collective-permute-start(bf16[2,8,4096]{2,1,0:T(8,128)(2,1)S(1)} %pad_maximum_fusion.8), channel_id=1, source_target_pairs={{0,3},{1,0},{2,1},{3,2},{4,7},{5,4},{6,5},{7,6},{8,11},{9,8},{10,9... | collective-permute-start | bytes 393224 | tf_op jit(solution)/shard_map/ppermute | solution.py:42
  92.1 6.8 %collective-permute-start.34 = (bf16[2,8,4096]{2,1,0:T(8,128)(2,1)S(1)}, bf16[2,8,4096]{2,1,0:T(8,128)(2,1)S(1)}, u32[]{:S(2)}, u32[]{:S(2)}) collective-permute-start(bf16[2,8,4096]{2,1,0:T(8,128)(2,1)S(1)} %pad_maximum_fusion.8), channel_id=1, source_target_pairs={{0,2},{1,3},{2,0},{3,1},{4,6},{5,7},{6,4},{7,5},{8,10},{9,11},{10,... | collective-permute-start | bytes 393224 | tf_op jit(solution)/shard_map/ppermute | solution.py:42
  92.9 7.6 %collective-permute-start.33 = (bf16[2,8,4096]{2,1,0:T(8,128)(2,1)S(1)}, bf16[2,8,4096]{2,1,0:T(8,128)(2,1)S(1)}, u32[]{:S(2)}, u32[]{:S(2)}) collective-permute-start(bf16[2,8,4096]{2,1,0:T(8,128)(2,1)S(1)} %pad_maximum_fusion.8), channel_id=1, source_target_pairs={{0,1},{1,2},{2,3},{3,0},{4,5},{5,6},{6,7},{7,4},{8,9},{9,10},{10,1... | collective-permute-start | bytes 393224 | tf_op jit(solution)/shard_map/ppermute | solution.py:42
  95.1 14.4 %collective-permute-start.29 = (bf16[4,2,8,4096]{3,2,1,0:T(8,128)(2,1)S(1)}, bf16[4,2,8,4096]{3,2,1,0:T(8,128)(2,1)S(1)}, u32[]{:S(2)}, u32[]{:S(2)}) collective-permute-start(bf16[4,2,8,4096]{3,2,1,0:T(8,128)(2,1)S(1)} %pad_maximum_fusion.1), channel_id=1, source_target_pairs={{0,12},{1,13},{2,14},{3,15},{4,0},{5,1},{6,2},{7,3},{8,4},{9,5},{1... | collective-permute-start | bytes 1572872 | tf_op jit(solution)/shard_map/ppermute | solution.py:42
  97.1 16.0 %collective-permute-start.27 = (bf16[4,2,8,4096]{3,2,1,0:T(8,128)(2,1)S(1)}, bf16[4,2,8,4096]{3,2,1,0:T(8,128)(2,1)S(1)}, u32[]{:S(2)}, u32[]{:S(2)}) collective-permute-start(bf16[4,2,8,4096]{3,2,1,0:T(8,128)(2,1)S(1)} %pad_maximum_fusion.1), channel_id=1, source_target_pairs={{0,4},{1,5},{2,6},{3,7},{4,8},{5,9},{6,10},{7,11},{8,12},{9,13},{1... | collective-permute-start | bytes 1572872 | tf_op jit(solution)/shard_map/ppermute | solution.py:42
  97.2 15.9 %collective-permute-start.28 = (bf16[4,2,8,4096]{3,2,1,0:T(8,128)(2,1)S(1)}, bf16[4,2,8,4096]{3,2,1,0:T(8,128)(2,1)S(1)}, u32[]{:S(2)}, u32[]{:S(2)}) collective-permute-start(bf16[4,2,8,4096]{3,2,1,0:T(8,128)(2,1)S(1)} %pad_maximum_fusion.1), channel_id=1, source_target_pairs={{0,8},{1,9},{2,10},{3,11},{4,12},{5,13},{6,14},{7,15},{8,0},{9,1},... | collective-permute-start | bytes 1572872 | tf_op jit(solution)/shard_map/ppermute | solution.py:42
  109.5 13.9 %collective-permute-start.37 = (bf16[4,2,8,4096]{3,2,1,0:T(8,128)(2,1)S(1)}, bf16[4,2,8,4096]{3,2,1,0:T(8,128)(2,1)S(1)}, u32[]{:S(2)}, u32[]{:S(2)}) collective-permute-start(bf16[4,2,8,4096]{3,2,1,0:T(8,128)(2,1)S(1)} %pad_maximum_fusion.2), channel_id=1, source_target_pairs={{0,12},{1,13},{2,14},{3,15},{4,0},{5,1},{6,2},{7,3},{8,4},{9,5},{1... | collective-permute-start | bytes 1572872 | tf_op jit(solution)/shard_map/ppermute | solution.py:42
  113.1 10.4 %collective-permute-start.36 = (bf16[4,2,8,4096]{3,2,1,0:T(8,128)(2,1)S(1)}, bf16[4,2,8,4096]{3,2,1,0:T(8,128)(2,1)S(1)}, u32[]{:S(2)}, u32[]{:S(2)}) collective-permute-start(bf16[4,2,8,4096]{3,2,1,0:T(8,128)(2,1)S(1)} %pad_maximum_fusion.2), channel_id=1, source_target_pairs={{0,4},{1,5},{2,6},{3,7},{4,8},{5,9},{6,10},{7,11},{8,12},{9,13},{1... | collective-permute-start | bytes 1572872 | tf_op jit(solution)/shard_map/ppermute | solution.py:42
  115.6 7.7 %collective-permute-start.30 = (bf16[4,4,8,1024]{3,2,1,0:T(8,128)(2,1)S(1)}, bf16[4,4,8,1024]{3,2,1,0:T(8,128)(2,1)S(1)}, u32[]{:S(2)}, u32[]{:S(2)}) collective-permute-start(bf16[4,4,8,1024]{3,2,1,0:T(8,128)(2,1)S(1)} %get-tuple-element.76), channel_id=1, source_target_pairs={{0,96},{1,97},{2,98},{3,99},{4,100},{5,101},{6,102},{7,103},{8,104... | collective-permute-start | bytes 786440 | tf_op jit(solution)/shard_map/ppermute | solution.py:42
  115.7 7.6 %collective-permute-start.31 = (bf16[4,4,8,1024]{3,2,1,0:T(8,128)(2,1)S(1)}, bf16[4,4,8,1024]{3,2,1,0:T(8,128)(2,1)S(1)}, u32[]{:S(2)}, u32[]{:S(2)}) collective-permute-start(bf16[4,4,8,1024]{3,2,1,0:T(8,128)(2,1)S(1)} %get-tuple-element.75), channel_id=1, source_target_pairs={{0,32},{1,33},{2,34},{3,35},{4,36},{5,37},{6,38},{7,39},{8,40},{9,... | collective-permute-start | bytes 786440 | tf_op jit(solution)/shard_map/ppermute | solution.py:42
  118.9 14.8 %collective-permute-start.39 = (bf16[4,2,8,4096]{3,2,1,0:T(8,128)(2,1)S(1)}, bf16[4,2,8,4096]{3,2,1,0:T(8,128)(2,1)S(1)}, u32[]{:S(2)}, u32[]{:S(2)}) collective-permute-start(bf16[4,2,8,4096]{3,2,1,0:T(8,128)(2,1)S(1)} %pad_maximum_fusion.2), channel_id=1, source_target_pairs={{0,8},{1,9},{2,10},{3,11},{4,12},{5,13},{6,14},{7,15},{8,0},{9,1},... | collective-permute-start | bytes 1572872 | tf_op jit(solution)/shard_map/ppermute | solution.py:42
  125.4 15.8 %collective-permute-start.38 = (bf16[3,4,8,1024]{3,2,1,0:T(8,128)(2,1)S(1)}, bf16[3,4,8,1024]{3,2,1,0:T(8,128)(2,1)S(1)}, u32[]{:S(2)}, u32[]{:S(2)}) collective-permute-start(bf16[3,4,8,1024]{3,2,1,0:T(8,128)(2,1)S(1)} %fusion.44), channel_id=1, source_target_pairs={{0,64},{1,65},{2,66},{3,67},{4,68},{5,69},{6,70},{7,71},{8,72},{9,... | collective-permute-start | bytes 589832 | tf_op jit(solution)/shard_map/ppermute | solution.py:42
  133.7 7.5 %copy-start = (s32[3]{0:T(128)S(1)}, s32[3]{0:T(128)}, u32[]{:S(2)}) copy-start(s32[3]{0:T(128)} %pad_add_fusion.place) | copy-start | bytes 40
  135.4 5.8 %collective-permute-start.40 = (bf16[1,4,8,1024]{3,2,1,0:T(8,128)(2,1)S(1)}, bf16[1,4,8,1024]{3,2,1,0:T(8,128)(2,1)S(1)}, u32[]{:S(2)}, u32[]{:S(2)}) collective-permute-start(bf16[1,4,8,1024]{3,2,1,0:T(8,128)(2,1)S(1)} %fusion.51), channel_id=1, source_target_pairs={{0,64},{1,65},{2,66},{3,67},{4,68},{5,69},{6,70},{7,71},{8,72},{9,... | collective-permute-start | bytes 196616 | tf_op jit(solution)/shard_map/ppermute | solution.py:42
  (3 other events, 5.7 us)
